TPU v7x, 32 devices: a whole 2x2x4 slice. The times are simulated.
32 devices in a mesh: section: 2 (over x), head: 4 (over y, core), dp: 4 (over z).
Axes of the slice: x: 2, y: 2, z: 4, core: 2. Of those that a mesh axis runs over, the one named last changes fastest.
Arguments:
- inputs: bfloat16 [8, 1024, 1024], P('dp', 'head'), may hold values from -6 to 6
- memory: bfloat16 [2, 8, 256, 1024], P('section', 'dp', 'head'), may hold values from -6 to 6
- value_routes: int32 [2, 8, 1280, 4, 2], P('section', 'dp', None, 'head'), may hold values from 0 to 4, all different within a row
- out_routes: int32 [2, 8, 1024, 4, 2], P('section', 'dp', None, 'head'), may hold values from 0 to 4, all different within a row
- ln1_gain: float32 [2, 1024], P('section'), may hold values from 0.5 to 1.5
- ln1_bias: float32 [2, 1024], P('section'), may hold values from -1 to 1
- query_weight: bfloat16 [2, 4, 1024, 112], P('section', 'head'), may hold values from -0.1875 to 0.1875
- key_weight: bfloat16 [2, 4, 1024, 112], P('section', 'head'), may hold values from -0.1875 to 0.1875
- value_weight: bfloat16 [2, 4, 1024, 560], P('section', 'head'), may hold values from -0.1875 to 0.1875
- value_router: bfloat16 [2, 4, 1024, 5], P('section', 'head'), may hold values from -0.125 to 0.125
- out_router: bfloat16 [2, 4, 1024, 5], P('section', 'head'), may hold values from -0.125 to 0.125
- output_weight: bfloat16 [2, 4, 560, 1024], P('section', 'head'), may hold values from -6 to 6
- ln2_gain: float32 [2, 1024], P('section'), may hold values from 0.5 to 1.5
- ln2_bias: float32 [2, 1024], P('section'), may hold values from -1 to 1
- up_weight: bfloat16 [2, 1024, 4096], P('section', None, 'head'), may hold values from -0.1875 to 0.1875
- up_bias: float32 [2, 4096], P('section', 'head'), may hold values from -1.5 to 1.5
- down_weight: bfloat16 [2, 4096, 1024], P('section', 'head'), may hold values from -0.09375 to 0.09375
- down_bias: float32 [2, 1024], P('section'), may hold values from -1 to 1
- out_cot: bfloat16 [8, 1024, 1024], P('dp', 'head'), may hold values from -6 to 6
Outputs:
- layer_out: bfloat16 [2, 8, 1024, 1024], P('section', 'dp', 'head')
- input_grad: bfloat16 [2, 8, 1024, 1024], P('section', 'dp', 'head')
- ln1_gain_grad: float32 [2, 1024], P('section')
- ln1_bias_grad: float32 [2, 1024], P('section')
- query_grad: float32 [2, 4, 1024, 112], P('section', 'head')
- key_grad: float32 [2, 4, 1024, 112], P('section', 'head')
- value_grad: float32 [2, 4, 1024, 560], P('section', 'head')
- value_router_grad: float32 [2, 4, 1024, 5], P('section', 'head')
- out_router_grad: float32 [2, 4, 1024, 5], P('section', 'head')
- output_grad: float32 [2, 4, 560, 1024], P('section', 'head')
- ln2_gain_grad: float32 [2, 1024], P('section')
- ln2_bias_grad: float32 [2, 1024], P('section')
- up_grad: float32 [2, 1024, 4096], P('section', None, 'head')
- up_bias_grad: float32 [2, 4096], P('section', 'head')
- down_grad: float32 [2, 4096, 1024], P('section', 'head')
- down_bias_grad: float32 [2, 1024], P('section')
Inputs may be any that keep to these rules, and one draw needn't show every extreme that they name: `value_routes`: the 2 experts of a token and head are distinct, and every expert is named somewhere. `out_routes`: the 2 experts of a token and head are distinct, and every expert is named somewhere.
All inputs are finite; a program needn't handle non-finite values.
Results may differ from a plain program's by a relative error of at most 0.03.
Values may be sent and summed in bfloat16 or wider, within the bound.
No kernel may reach another device: no remote copies, remote signals or barrier semaphores. Data moves between devices by JAX's collectives and lax.ppermute only.
A program may use at most 320 MiB of HBM per device.

v0:
```python
import jax
import jax.numpy as jnp
from jax import lax
from jax.sharding import PartitionSpec as P

norm_eps = 1e-05
block_limit = 512
masked_score = -1e30


def as_sent(array):
    return jax.tree.map(lambda a: a.astype(jnp.bfloat16) if a.dtype == jnp.float32 else a, array)


def from_behind(array, axis, by):
    size = lax.axis_size(axis)
    pairs = [(i, i + by) for i in range(size) if 0 <= i + by < size]
    return lax.ppermute(array, axis, pairs)


def normalize(row_data, gain_vec, shift_vec):
    average = jnp.mean(row_data, axis=-1, keepdims=True)
    centred = row_data - average
    variance = jnp.mean(centred * centred, axis=-1, keepdims=True)
    return centred * lax.rsqrt(variance + norm_eps) * gain_vec + shift_vec


def round_trip(array_in):
    return lax.optimization_barrier(array_in.astype(jnp.bfloat16)).astype(jnp.float32)


def choose(route_ids, experts):
    expert_ids = jnp.arange(experts, dtype=jnp.int32)
    picked = jnp.sum((route_ids[..., None] == expert_ids).astype(jnp.float32), axis=2)
    return jnp.transpose(picked, (1, 0, 2))


def select_micro(array_in, micro_index):
    return lax.dynamic_index_in_dim(array_in, micro_index, 0, keepdims=False)


def block_scores(query_block, key_low, offset, memory_len):
    score_scale = query_block.shape[-1] ** (-0.5)
    scores = (
        jnp.einsum("hqe,hke->hqk", query_block, key_low, preferred_element_type=jnp.float32)
        * score_scale
    )
    query_pos = offset + memory_len + jnp.arange(query_block.shape[1], dtype=jnp.int32)[:, None]
    key_pos = jnp.arange(key_low.shape[1], dtype=jnp.int32)[None, :]
    return jnp.where(key_pos <= query_pos, scores, masked_score)


def attend_blocks(query_low, key_low, value_low, memory_len):
    seq_len = query_low.shape[1]
    block_rows = min(block_limit, seq_len)
    outputs = []
    log_totals = []
    for offset in range(0, seq_len, block_rows):
        scores = block_scores(
            query_low[:, offset : offset + block_rows], key_low, offset, memory_len
        )
        row_top = jnp.max(scores, axis=-1, keepdims=True)
        exponent = jnp.exp(scores - row_top)
        row_total = jnp.sum(exponent, axis=-1, keepdims=True)
        chance = (exponent / row_total).astype(jnp.bfloat16)
        outputs.append(
            jnp.einsum("hqk,hke->hqe", chance, value_low, preferred_element_type=jnp.float32)
        )
        log_totals.append(row_top + jnp.log(row_total))
    return (jnp.concatenate(outputs, axis=1), jnp.concatenate(log_totals, axis=1))


def attend_back(query_low, key_low, value_low, log_totals, attended_grad, memory_len):
    seq_len = query_low.shape[1]
    block_rows = min(block_limit, seq_len)
    score_scale = query_low.shape[-1] ** (-0.5)
    key_total = jnp.zeros(key_low.shape, jnp.float32)
    value_total = jnp.zeros(value_low.shape, jnp.float32)
    query_parts = []
    for offset in range(0, seq_len, block_rows):
        query_block = query_low[:, offset : offset + block_rows]
        scores = block_scores(query_block, key_low, offset, memory_len)
        chance = jnp.exp(scores - log_totals[:, offset : offset + block_rows])
        grad_block = attended_grad[:, offset : offset + block_rows]
        value_total = value_total + jnp.einsum(
            "hqk,hqe->hke",
            chance.astype(jnp.bfloat16),
            grad_block,
            preferred_element_type=jnp.float32,
        )
        chance_grad = round_trip(
            jnp.einsum("hqe,hke->hqk", grad_block, value_low, preferred_element_type=jnp.float32)
        )
        inner_sum = jnp.sum(chance_grad * chance, axis=-1, keepdims=True)
        score_grad = (chance * (chance_grad - inner_sum)).astype(jnp.bfloat16)
        query_parts.append(
            jnp.einsum("hqk,hke->hqe", score_grad, key_low, preferred_element_type=jnp.float32)
            * score_scale
        )
        key_total = (
            key_total
            + jnp.einsum(
                "hqk,hqe->hke", score_grad, query_block, preferred_element_type=jnp.float32
            )
            * score_scale
        )
    query_total = jnp.concatenate(query_parts, axis=1)
    return (
        query_total.astype(jnp.bfloat16),
        key_total.astype(jnp.bfloat16),
        value_total.astype(jnp.bfloat16),
    )


def gather_normed(weights, own_rows, mem_rows):
    norm1_gain, norm1_shift = (weights[0], weights[1])
    mem_part = normalize(mem_rows, norm1_gain, norm1_shift).astype(jnp.bfloat16)
    own_part = normalize(own_rows, norm1_gain, norm1_shift).astype(jnp.bfloat16)
    mem_norm, query_norm = (
        lax.all_gather(mem_part, "head", axis=0, tiled=True),
        lax.all_gather(own_part, "head", axis=0, tiled=True),
    )
    return jnp.concatenate([mem_norm, query_norm], axis=0)


def attention_local(weights, normed, memory_len, value_ids, out_ids):
    query_w, key_w, value_w, vroute_w, oroute_w = (
        weights[2],
        weights[3],
        weights[4],
        weights[5],
        weights[6],
    )
    query_norm = normed[memory_len:]
    heads_here = query_w.shape[0]
    head_width = query_w.shape[2]
    experts = vroute_w.shape[2]
    seq_len = query_norm.shape[0]
    width_all = normed.shape[0]
    query_low = jnp.einsum(
        "td,hde->hte", query_norm, query_w, preferred_element_type=jnp.float32
    ).astype(jnp.bfloat16)
    key_low = jnp.einsum("td,hde->hte", normed, key_w, preferred_element_type=jnp.float32).astype(
        jnp.bfloat16
    )
    expert_vals = jnp.einsum("td,hdf->htf", normed, value_w, preferred_element_type=jnp.float32)
    expert_vals = expert_vals.reshape(heads_here, width_all, experts, head_width)
    value_sig = jax.nn.sigmoid(
        jnp.einsum("td,hde->hte", normed, vroute_w, preferred_element_type=jnp.float32)
    )
    value_mask = choose(value_ids, experts)
    value_low = jnp.sum(expert_vals * (value_sig * value_mask)[..., None], axis=2).astype(
        jnp.bfloat16
    )
    out_sig = jax.nn.sigmoid(
        jnp.einsum("td,hde->hte", query_norm, oroute_w, preferred_element_type=jnp.float32)
    )
    out_mask = choose(out_ids, experts)
    attended, log_totals = attend_blocks(query_low, key_low, value_low, memory_len)
    mixed = (attended[:, :, None, :] * (out_sig * out_mask)[..., None]).reshape(
        heads_here, seq_len, experts * head_width
    )
    mixed = mixed.astype(jnp.bfloat16)
    return (
        query_norm,
        query_low,
        key_low,
        value_low,
        expert_vals,
        value_sig,
        value_mask,
        out_sig,
        out_mask,
        attended,
        log_totals,
        mixed,
    )


def ffn_local(weights, normed2):
    upper = jnp.dot(normed2, weights[10], preferred_element_type=jnp.float32) + weights[11]
    return (upper, jax.nn.gelu(upper).astype(jnp.bfloat16))


def front_pass(weights, own_rows, mem_rows, value_ids, out_ids):
    output_w, norm2_gain, norm2_shift = (weights[7], weights[8], weights[9])
    normed = gather_normed(weights, own_rows, mem_rows)
    memory_len = mem_rows.shape[0] * lax.axis_size("head")
    attn = attention_local(weights, normed, memory_len, value_ids, out_ids)
    mixed = attn[11]
    hidden = own_rows + lax.psum_scatter(
        jnp.einsum("htf,hfd->td", mixed, output_w, preferred_element_type=jnp.float32).astype(
            jnp.bfloat16
        ),
        "head",
        scatter_dimension=0,
        tiled=True,
    ).astype(jnp.float32)
    own_norm2 = normalize(hidden, norm2_gain, norm2_shift).astype(jnp.bfloat16)
    normed2 = lax.all_gather(own_norm2, "head", axis=0, tiled=True)
    return (hidden, normed, normed2, attn)


def layer_forward(weights, own_rows, mem_rows, value_ids, out_ids):
    hidden, normed, normed2, attn = front_pass(weights, own_rows, mem_rows, value_ids, out_ids)
    upper, active = ffn_local(weights, normed2)
    down_w = weights[12]
    result = (
        hidden
        + lax.psum_scatter(
            jnp.dot(active, down_w, preferred_element_type=jnp.float32).astype(jnp.bfloat16),
            "head",
            scatter_dimension=0,
            tiled=True,
        ).astype(jnp.float32)
        + weights[13]
    )
    return (result, (normed, hidden, normed2))


def layer_backward(weights, own_rows, mem_rows, value_ids, out_ids, grad_rows):
    (
        norm1_gain,
        norm1_shift,
        query_w,
        key_w,
        value_w,
        vroute_w,
        oroute_w,
        output_w,
        norm2_gain,
        norm2_shift,
        up_w,
        up_shift,
        down_w,
        down_shift,
    ) = weights
    memory_len = mem_rows.shape[0] * lax.axis_size("head")
    hidden, normed, normed2, attn = front_pass(weights, own_rows, mem_rows, value_ids, out_ids)
    upper, active = ffn_local(weights, normed2)
    (
        query_norm,
        query_low,
        key_low,
        value_low,
        expert_vals,
        value_sig,
        value_mask,
        out_sig,
        out_mask,
        attended,
        log_totals,
        mixed,
    ) = attn
    heads_here = query_low.shape[0]
    seq_len = query_low.shape[1]
    head_width = query_low.shape[2]
    experts = value_mask.shape[2]
    width_all = normed.shape[0]
    grad_all = lax.all_gather(grad_rows.astype(jnp.bfloat16), "head", axis=0, tiled=True)
    down_grad = jnp.einsum("tf,td->fd", active, grad_all, preferred_element_type=jnp.float32)
    active_grad = round_trip(
        jnp.einsum("td,fd->tf", grad_all, down_w, preferred_element_type=jnp.float32)
    )
    upper_grad = jax.vjp(jax.nn.gelu, upper)[1](active_grad)[0].astype(jnp.bfloat16)
    up_bias_grad = jnp.sum(upper_grad.astype(jnp.float32), axis=0)
    up_grad = jnp.einsum("td,tf->df", normed2, upper_grad, preferred_element_type=jnp.float32)
    normed2_grad = lax.psum_scatter(
        jnp.einsum("tf,df->td", upper_grad, up_w, preferred_element_type=jnp.float32).astype(
            jnp.bfloat16
        ),
        "head",
        scatter_dimension=0,
        tiled=True,
    ).astype(jnp.float32)
    hidden_back = jax.vjp(normalize, hidden, norm2_gain, norm2_shift)[1](normed2_grad)
    hidden_grad = grad_rows + hidden_back[0]
    down_bias_grad = jnp.sum(grad_rows, axis=0)
    attn_all = lax.all_gather(hidden_grad.astype(jnp.bfloat16), "head", axis=0, tiled=True)
    output_grad = jnp.einsum("htf,td->hfd", mixed, attn_all, preferred_element_type=jnp.float32)
    mixed_grad = round_trip(
        jnp.einsum("td,hfd->htf", attn_all, output_w, preferred_element_type=jnp.float32)
    )
    mixed_grad = mixed_grad.reshape(heads_here, seq_len, experts, head_width)
    out_gate = out_sig * out_mask
    attended_grad = jnp.sum(mixed_grad * out_gate[..., None], axis=2).astype(jnp.bfloat16)
    out_gate_grad = jnp.sum(mixed_grad * attended[:, :, None, :], axis=3)
    out_logit_grad = (out_gate_grad * out_mask * out_sig * (1.0 - out_sig)).astype(jnp.bfloat16)
    out_router_grad = jnp.einsum(
        "td,hte->hde", query_norm, out_logit_grad, preferred_element_type=jnp.float32
    )
    query_rows_grad, key_rows_grad, value_rows_grad = attend_back(
        query_low, key_low, value_low, log_totals, attended_grad, memory_len
    )
    value_wide = value_rows_grad.astype(jnp.float32)[:, :, None, :]
    value_gate = value_sig * value_mask
    expert_grad = (value_wide * value_gate[..., None]).reshape(
        heads_here, width_all, experts * head_width
    )
    expert_grad = expert_grad.astype(jnp.bfloat16)
    value_gate_grad = jnp.sum(value_wide * expert_vals, axis=3)
    value_logit_grad = (value_gate_grad * value_mask * value_sig * (1.0 - value_sig)).astype(
        jnp.bfloat16
    )
    query_grad = jnp.einsum(
        "td,hte->hde", query_norm, query_rows_grad, preferred_element_type=jnp.float32
    )
    key_grad = jnp.einsum("td,hte->hde", normed, key_rows_grad, preferred_element_type=jnp.float32)
    value_grad = jnp.einsum("td,htf->hdf", normed, expert_grad, preferred_element_type=jnp.float32)
    value_router_grad = jnp.einsum(
        "td,hte->hde", normed, value_logit_grad, preferred_element_type=jnp.float32
    )
    normed_grad = jnp.einsum(
        "hte,hde->td", key_rows_grad, key_w, preferred_element_type=jnp.float32
    )
    normed_grad = normed_grad + jnp.einsum(
        "htf,hdf->td", expert_grad, value_w, preferred_element_type=jnp.float32
    )
    normed_grad = normed_grad + jnp.einsum(
        "hte,hde->td", value_logit_grad, vroute_w, preferred_element_type=jnp.float32
    )
    query_part = jnp.einsum(
        "hte,hde->td", query_rows_grad, query_w, preferred_element_type=jnp.float32
    )
    query_part = query_part + jnp.einsum(
        "hte,hde->td", out_logit_grad, oroute_w, preferred_element_type=jnp.float32
    )
    mem_grad, own_grad = (
        lax.psum_scatter(
            normed_grad[:memory_len].astype(jnp.bfloat16), "head", scatter_dimension=0, tiled=True
        ).astype(jnp.float32),
        lax.psum_scatter(
            (normed_grad[memory_len:] + query_part).astype(jnp.bfloat16),
            "head",
            scatter_dimension=0,
            tiled=True,
        ).astype(jnp.float32),
    )
    norm_back = jax.vjp(
        lambda mem_in, own_data, gain_in, shift_in: (
            normalize(mem_in, gain_in, shift_in),
            normalize(own_data, gain_in, shift_in),
        ),
        mem_rows,
        own_rows,
        norm1_gain,
        norm1_shift,
    )[1]((mem_grad, own_grad))
    input_grad = hidden_grad + norm_back[1]
    weight_parts = (
        query_grad,
        key_grad,
        value_grad,
        value_router_grad,
        out_router_grad,
        output_grad,
        up_grad,
        up_bias_grad,
        down_grad,
    )
    norm_parts = (norm_back[2], norm_back[3], hidden_back[1], hidden_back[2], down_bias_grad)
    return (input_grad, weight_parts, norm_parts)


def reduce_grads(weight_parts, norm_parts):
    weight_sums = jax.tree.map(
        lambda part: part.astype(jnp.float32), lax.psum(as_sent(weight_parts), "dp")
    )
    norm_sums = lax.psum(norm_parts, ("head", "dp"))
    return (weight_sums, norm_sums)


def on_device(
    inputs,
    memory,
    value_routes,
    out_routes,
    ln1_gain,
    ln1_bias,
    query_weight,
    key_weight,
    value_weight,
    value_router,
    out_router,
    output_weight,
    ln2_gain,
    ln2_bias,
    up_weight,
    up_bias,
    down_weight,
    down_bias,
    out_cot,
):
    weights = tuple(
        (
            member[0]
            for member in (
                ln1_gain,
                ln1_bias,
                query_weight,
                key_weight,
                value_weight,
                value_router,
                out_router,
                output_weight,
                ln2_gain,
                ln2_bias,
                up_weight,
                up_bias,
                down_weight,
                down_bias,
            )
        )
    )
    seq_local = inputs.shape[0]
    section_index = lax.axis_index("section")
    is_first = section_index == 0
    received = jnp.zeros(inputs.shape[1:], jnp.bfloat16)
    layer_out = jnp.zeros_like(inputs)
    layer_in = jnp.zeros_like(inputs)
    for tick_index in range(seq_local + 1):
        micro_raw = tick_index - section_index
        micro_index = jnp.clip(micro_raw, 0, seq_local - 1)
        tick_valid = (micro_raw >= 0) & (micro_raw < seq_local)
        own_in = jnp.where(is_first, inputs[min(tick_index, seq_local - 1)], received)
        result, keep_rows = layer_forward(
            weights,
            own_in.astype(jnp.float32),
            select_micro(memory[0], micro_index).astype(jnp.float32),
            select_micro(value_routes[0], micro_index),
            select_micro(out_routes[0], micro_index),
        )
        result_low = result.astype(jnp.bfloat16)
        layer_out = jnp.where(
            tick_valid,
            lax.dynamic_update_index_in_dim(layer_out, result_low, micro_index, 0),
            layer_out,
        )
        layer_in = jnp.where(
            tick_valid, lax.dynamic_update_index_in_dim(layer_in, own_in, micro_index, 0), layer_in
        )
        received = from_behind(result_low, "section", 1)
    back_received = jnp.zeros(inputs.shape[1:], jnp.bfloat16)
    input_grads = jnp.zeros_like(inputs)
    weight_total = None
    norm_total = None
    for tick_index in range(seq_local + 1):
        micro_raw = tick_index - 1 + section_index
        micro_index = jnp.clip(micro_raw, 0, seq_local - 1)
        tick_valid = (micro_raw >= 0) & (micro_raw < seq_local)
        grad_in = jnp.where(
            is_first, back_received, out_cot[min(tick_index, seq_local - 1)]
        ).astype(jnp.float32)
        own_in = select_micro(layer_in, micro_index).astype(jnp.float32)
        input_grad, weight_parts, norm_parts = layer_backward(
            weights,
            own_in,
            select_micro(memory[0], micro_index).astype(jnp.float32),
            select_micro(value_routes[0], micro_index),
            select_micro(out_routes[0], micro_index),
            grad_in,
        )
        grad_low = input_grad.astype(jnp.bfloat16)
        input_grads = jnp.where(
            tick_valid,
            lax.dynamic_update_index_in_dim(input_grads, grad_low, micro_index, 0),
            input_grads,
        )
        valid_scale = tick_valid.astype(jnp.float32)
        weight_parts = jax.tree.map(lambda member: member * valid_scale, weight_parts)
        norm_parts = jax.tree.map(lambda member: member * valid_scale, norm_parts)
        if tick_index == 0:
            weight_total, norm_total = (weight_parts, norm_parts)
        else:
            weight_total = jax.tree.map(jnp.add, weight_total, weight_parts)
            norm_total = jax.tree.map(jnp.add, norm_total, norm_parts)
        back_received = from_behind(grad_low, "section", -1)
    weight_total, norm_total = reduce_grads(weight_total, norm_total)
    return (
        layer_out[None],
        input_grads[None],
        norm_total[0][None],
        norm_total[1][None],
        weight_total[0][None],
        weight_total[1][None],
        weight_total[2][None],
        weight_total[3][None],
        weight_total[4][None],
        weight_total[5][None],
        norm_total[2][None],
        norm_total[3][None],
        weight_total[6][None],
        weight_total[7][None],
        weight_total[8][None],
        norm_total[4][None],
    )


def solution(mesh):
    placed = (
        P("dp", "head", None),
        P("section", "dp", "head", None),
        P("section", "dp", None, "head", None),
        P("section", "dp", None, "head", None),
        P("section", None),
        P("section", None),
        P("section", "head", None, None),
        P("section", "head", None, None),
        P("section", "head", None, None),
        P("section", "head", None, None),
        P("section", "head", None, None),
        P("section", "head", None, None),
        P("section", None),
        P("section", None),
        P("section", None, "head"),
        P("section", "head"),
        P("section", "head", None),
        P("section", None),
        P("dp", "head", None),
    )
    return jax.shard_map(
        on_device,
        mesh=mesh,
        in_specs=placed,
        out_specs=(
            P("section", "dp", "head", None),
            P("section", "dp", "head", None),
            P("section", None),
            P("section", None),
            P("section", "head", None, None),
            P("section", "head", None, None),
            P("section", "head", None, None),
            P("section", "head", None, None),
            P("section", "head", None, None),
            P("section", "head", None, None),
            P("section", None),
            P("section", None),
            P("section", None, "head"),
            P("section", "head"),
            P("section", "head", None),
            P("section", None),
        ),
        check_vma=False,
    )
```

profile of v0, /device:TPU:0, one launch (start us, length us, event | category | flops | bytes accessed | tf_op | source)
XLA Modules:
  0.0 1589.2 jit_solution(2003795027381632541)
XLA Ops:
  70.3 31.3 %reduce-scatter.19.cloned.1.call-done = bf16[256,1024]{1,0:T(8,128)(2,1)} async-done(((bf16[1024,1024]{1,0:T(8,128)(2,1)}), bf16[256,1024]{1,0:T(8,128)(2,1)}) %reduce-scatter.19.cloned.1.call-update) | async-done | bytes 524304 | tf_op jit(solution)/shard_map/reduce_scatter | solution.py:191
  106.4 22.7 %all-gather.22.cloned.1.call-done = bf16[1024,1024]{1,0:T(8,128)(2,1)} async-done(((bf16[256,1024]{1,0:T(8,128)(2,1)}), bf16[1024,1024]{1,0:T(8,128)(2,1)}) %all-gather.22.cloned.1.call-update) | async-done | bytes 2097168 | tf_op jit(solution)/shard_map/all_gather | solution.py:200
  137.5 31.5 %reduce-scatter.21.cloned.1.call-done = bf16[256,1024]{1,0:T(8,128)(2,1)} async-done(((bf16[1024,1024]{1,0:T(8,128)(2,1)}), bf16[256,1024]{1,0:T(8,128)(2,1)}) %reduce-scatter.21.cloned.1.call-update) | async-done | bytes 524304 | tf_op jit(solution)/shard_map/reduce_scatter | solution.py:210
  249.0 31.5 %reduce-scatter.23.cloned.1.call-done = bf16[256,1024]{1,0:T(8,128)(2,1)} async-done(((bf16[1024,1024]{1,0:T(8,128)(2,1)}), bf16[256,1024]{1,0:T(8,128)(2,1)}) %reduce-scatter.23.cloned.1.call-update) | async-done | bytes 524304 | tf_op jit(solution)/shard_map/reduce_scatter | solution.py:191
  286.0 22.5 %all-gather.26.cloned.1.call-done = bf16[1024,1024]{1,0:T(8,128)(2,1)} async-done(((bf16[256,1024]{1,0:T(8,128)(2,1)}), bf16[1024,1024]{1,0:T(8,128)(2,1)}) %all-gather.26.cloned.1.call-update) | async-done | bytes 2097168 | tf_op jit(solution)/shard_map/all_gather | solution.py:200
  316.8 31.5 %reduce-scatter.25.cloned.1.call-done = bf16[256,1024]{1,0:T(8,128)(2,1)} async-done(((bf16[1024,1024]{1,0:T(8,128)(2,1)}), bf16[256,1024]{1,0:T(8,128)(2,1)}) %reduce-scatter.25.cloned.1.call-update) | async-done | bytes 524304 | tf_op jit(solution)/shard_map/reduce_scatter | solution.py:210
  436.2 28.9 %reduce-scatter.31.cloned.1.call-done = bf16[256,1024]{1,0:T(8,128)(2,1)} async-done(((bf16[1024,1024]{1,0:T(8,128)(2,1)}), bf16[256,1024]{1,0:T(8,128)(2,1)}) %reduce-scatter.31.cloned.1.call-update) | async-done | bytes 524304 | tf_op jit(solution)/shard_map/reduce_scatter | solution.py:191
  612.0 24.6 %reduce-scatter.43.cloned.1.call-done = bf16[256,1024]{1,0:T(8,128)(2,1)} async-done(((bf16[1024,1024]{1,0:T(8,128)(2,1)}), bf16[256,1024]{1,0:T(8,128)(2,1)}) %reduce-scatter.43.cloned.1.call-update) | async-done | bytes 524304 | tf_op jit(solution)/shard_map/reduce_scatter | solution.py:191
  636.6 34.6 %reduce-scatter.33.cloned.1.call-done = bf16[256,1024]{1,0:T(8,128)(2,1)} async-done(((bf16[1024,1024]{1,0:T(8,128)(2,1)}), bf16[256,1024]{1,0:T(8,128)(2,1)}) %reduce-scatter.33.cloned.1.call-update) | async-done | bytes 524304 | tf_op jit(solution)/shard_map/reduce_scatter | solution.py:268
  680.2 19.2 %all-gather.36.cloned.1.call-done = bf16[1024,1024]{1,0:T(8,128)(2,1)} async-done(((bf16[256,1024]{1,0:T(8,128)(2,1)}), bf16[1024,1024]{1,0:T(8,128)(2,1)}) %all-gather.36.cloned.1.call-update) | async-done | bytes 2097168 | tf_op jit(solution)/shard_map/all_gather | solution.py:279
  723.4 31.5 %reduce-scatter.35.cloned.1.call-done = bf16[256,1024]{1,0:T(8,128)(2,1)} async-done(((bf16[1024,1024]{1,0:T(8,128)(2,1)}), bf16[256,1024]{1,0:T(8,128)(2,1)}) %reduce-scatter.35.cloned.1.call-update) | async-done | bytes 524304 | tf_op jit(solution)/shard_map/reduce_scatter | solution.py:332
  790.1 18.9 %all-gather.38.cloned.1.call-done = bf16[1024,1024]{1,0:T(8,128)(2,1)} async-done(((bf16[256,1024]{1,0:T(8,128)(2,1)}), bf16[1024,1024]{1,0:T(8,128)(2,1)}) %all-gather.38.cloned.1.call-update) | async-done | bytes 2097168 | tf_op jit(solution)/shard_map/all_gather | solution.py:260
  822.9 31.5 %reduce-scatter.39.cloned.1.call-done = bf16[256,1024]{1,0:T(8,128)(2,1)} async-done(((bf16[1024,1024]{1,0:T(8,128)(2,1)}), bf16[256,1024]{1,0:T(8,128)(2,1)}) %reduce-scatter.39.cloned.1.call-update) | async-done | bytes 524304 | tf_op jit(solution)/shard_map/reduce_scatter | solution.py:268
  864.3 19.2 %all-gather.44.cloned.1.call-done = bf16[1024,1024]{1,0:T(8,128)(2,1)} async-done(((bf16[256,1024]{1,0:T(8,128)(2,1)}), bf16[1024,1024]{1,0:T(8,128)(2,1)}) %all-gather.44.cloned.1.call-update) | async-done | bytes 2097168 | tf_op jit(solution)/shard_map/all_gather | solution.py:279
  908.2 30.8 %reduce-scatter.41.cloned.1.call-done = bf16[256,1024]{1,0:T(8,128)(2,1)} async-done(((bf16[1024,1024]{1,0:T(8,128)(2,1)}), bf16[256,1024]{1,0:T(8,128)(2,1)}) %reduce-scatter.41.cloned.1.call-update) | async-done | bytes 524304 | tf_op jit(solution)/shard_map/reduce_scatter | solution.py:332
  969.7 18.3 %all-gather.46.cloned.1.call-done = bf16[1024,1024]{1,0:T(8,128)(2,1)} async-done(((bf16[256,1024]{1,0:T(8,128)(2,1)}), bf16[1024,1024]{1,0:T(8,128)(2,1)}) %all-gather.46.cloned.1.call-update) | async-done | bytes 2097168 | tf_op jit(solution)/shard_map/all_gather | solution.py:260
  1001.8 31.5 %reduce-scatter.45.cloned.1.call-done = bf16[256,1024]{1,0:T(8,128)(2,1)} async-done(((bf16[1024,1024]{1,0:T(8,128)(2,1)}), bf16[256,1024]{1,0:T(8,128)(2,1)}) %reduce-scatter.45.cloned.1.call-update) | async-done | bytes 524304 | tf_op jit(solution)/shard_map/reduce_scatter | solution.py:268
  1094.0 17.0 %reduce-scatter.49.cloned.1.call-done = bf16[64,1024]{1,0:T(8,128)(2,1)} async-done(((bf16[256,1024]{1,0:T(8,128)(2,1)}), bf16[64,1024]{1,0:T(8,128)(2,1)}) %reduce-scatter.49.cloned.1.call-update) | async-done | bytes 131088 | tf_op jit(solution)/shard_map/reduce_scatter | solution.py:329
  1111.0 24.9 %reduce-scatter.51.cloned.1.call-done = bf16[64,1024]{1,0:T(8,128)(2,1)} async-done(((bf16[256,1024]{1,0:T(8,128)(2,1)}), bf16[64,1024]{1,0:T(8,128)(2,1)}) %reduce-scatter.51.cloned.1.call-update) | async-done | bytes 131088 | tf_op jit(solution)/shard_map/reduce_scatter | solution.py:329
  1135.9 24.8 %reduce-scatter.53.cloned.1.call-done = bf16[64,1024]{1,0:T(8,128)(2,1)} async-done(((bf16[256,1024]{1,0:T(8,128)(2,1)}), bf16[64,1024]{1,0:T(8,128)(2,1)}) %reduce-scatter.53.cloned.1.call-update) | async-done | bytes 131088 | tf_op jit(solution)/shard_map/reduce_scatter | solution.py:329
  1304.8 24.7 %all-reduce.1 = (bf16[1,1,1024,5]{2,3,1,0:T(8,128)(2,1)S(1)}, bf16[1,1,1024,5]{2,3,1,0:T(8,128)(2,1)S(1)}, bf16[1,1024]{1,0:T(2,128)(2,1)S(1)}) all-reduce(bf16[1,1,1024,5]{2,3,1,0:T(8,128)(2,1)S(1)} %fusion.392, bf16[1,1,1024,5]{2,3,1,0:T(8,128)(2,1)S(1)} %fusion.391, ...), channel_id=1, replica_groups=mesh['section'=2,'head'=4,'dp'=4] {'dp'}, use_global_device_ids=true, to_apply=%region_140.141 | all-reduce | flops 11264 | bytes 45056 | tf_op jit(solution)/shard_map/psum | solution.py:367
  1334.6 77.8 %all-reduce = (f32[1,1024]{1,0:T(1,128)}, f32[1,1024]{1,0:T(1,128)}, f32[1,1024]{1,0:T(1,128)}, f32[1,1024]{1,0:T(1,128)}, f32[1,1024]{1,0:T(1,128)}) all-reduce(f32[1,1024]{1,0:T(1,128)S(1)} %bitcast.1364, f32[1,1024]{1,0:T(1,128)S(1)} %bitcast.1363, ...), channel_id=1, replica_groups=mesh['section'=2,'head'=4,'dp'=4] {'head','dp'}, use_global_device_ids=true, to_apply=%region_129.130 | all-reduce | flops 5120 | bytes 40960 | tf_op jit(solution)/shard_map/psum | solution.py:369
  1415.4 131.6 %all-reduce.5.cloned.1.call-done = (bf16[1,1,1024,112]{2,3,1,0:T(8,128)(2,1)}, bf16[1,1,1024,112]{2,3,1,0:T(8,128)(2,1)}, bf16[1,1,1024,560]{2,3,1,0:T(8,128)(2,...) async-done(((bf16[1,1,1024,112]{2,3,1,0:T(8,128)(2,1)}, bf16[1,1,1024,112]{2,3,1,0:T(8,128)(2,1)}, ...) | async-done | bytes 6946832 | tf_op jit(solution)/shard_map/psum | solution.py:367
  1560.4 19.4 %reduce-scatter.29.cloned.1.call-done = bf16[256,1024]{1,0:T(8,128)(2,1)} async-done(((bf16[1024,1024]{1,0:T(8,128)(2,1)}), bf16[256,1024]{1,0:T(8,128)(2,1)}) %reduce-scatter.29.cloned.1.call-update) | async-done | bytes 524304 | tf_op jit(solution)/shard_map/reduce_scatter | solution.py:210
  (1103 shorter events, 790.3 us)
Async XLA Ops:
  12.2 89.4 %reduce-scatter.19.cloned.1.call-start = ((), (), s32[]{:S(2)}) async-start(), calls=%async_computation.19 | async-start | bytes 2621440 | tf_op jit(solution)/shard_map/reduce_scatter | solution.py:191
  137.5 77.1 %all-gather.24.cloned.1.call-start = ((), (), s32[]{:S(2)}) async-start(), calls=%async_computation.22 | async-start | bytes 2621440 | tf_op jit(solution)/shard_map/all_gather | solution.py:121
  190.7 89.8 %reduce-scatter.23.cloned.1.call-start = ((), (), s32[]{:S(2)}) async-start(), calls=%async_computation.23 | async-start | bytes 2621440 | tf_op jit(solution)/shard_map/reduce_scatter | solution.py:191
  316.8 77.1 %all-gather.32.cloned.1.call-start = ((), (), s32[]{:S(2)}) async-start(), calls=%async_computation.30 | async-start | bytes 2621440 | tf_op jit(solution)/shard_map/all_gather | solution.py:121
  370.0 95.1 %reduce-scatter.31.cloned.1.call-start = ((), (), s32[]{:S(2)}) async-start(), calls=%async_computation.31 | async-start | bytes 2621440 | tf_op jit(solution)/shard_map/reduce_scatter | solution.py:191
  471.2 75.7 %all-gather.48.cloned.1.call-start = ((), (), s32[]{:S(2)}) async-start(), calls=%async_computation.44 | async-start | bytes 2621440 | tf_op jit(solution)/shard_map/all_gather | solution.py:121
  471.8 120.1 %all-gather.54.cloned.1.call-start = ((), (), s32[]{:S(2)}) async-start(), calls=%async_computation.53 | async-start | bytes 2621440 | tf_op jit(solution)/shard_map/all_gather | solution.py:260
  474.5 123.4 %all-gather.34.cloned.1.call-start = ((), (), s32[]{:S(2)}) async-start(), calls=%async_computation.32 | async-start | bytes 2621440 | tf_op jit(solution)/shard_map/all_gather | solution.py:200
  485.3 126.8 %reduce-scatter.37.cloned.1.call-start = ((), (), s32[]{:S(2)}) async-start(), calls=%async_computation.38 | async-start | bytes 2621440 | tf_op jit(solution)/shard_map/reduce_scatter | solution.py:191
  538.4 98.2 %reduce-scatter.43.cloned.1.call-start = ((), (), s32[]{:S(2)}) async-start(), calls=%async_computation.45 | async-start | bytes 2621440 | tf_op jit(solution)/shard_map/reduce_scatter | solution.py:191
  591.6 79.5 %reduce-scatter.33.cloned.1.call-start = ((), (), s32[]{:S(2)}) async-start(), calls=%async_computation.33 | async-start | bytes 2621440 | tf_op jit(solution)/shard_map/reduce_scatter | solution.py:268
  611.9 87.5 %all-gather.36.cloned.1.call-start = ((), (), s32[]{:S(2)}) async-start(), calls=%async_computation.34 | async-start | bytes 2621440 | tf_op jit(solution)/shard_map/all_gather | solution.py:279
  676.7 78.2 %reduce-scatter.35.cloned.1.call-start = ((), (), s32[]{:S(2)}) async-start(), calls=%async_computation.35 | async-start | bytes 2621440 | tf_op jit(solution)/shard_map/reduce_scatter | solution.py:332
  783.4 71.0 %reduce-scatter.39.cloned.1.call-start = ((), (), s32[]{:S(2)}) async-start(), calls=%async_computation.40 | async-start | bytes 2621440 | tf_op jit(solution)/shard_map/reduce_scatter | solution.py:268
  860.8 78.2 %reduce-scatter.41.cloned.1.call-start = ((), (), s32[]{:S(2)}) async-start(), calls=%async_computation.42 | async-start | bytes 2621440 | tf_op jit(solution)/shard_map/reduce_scatter | solution.py:332
  908.2 79.8 %all-gather.46.cloned.1.call-start = ((), (), s32[]{:S(2)}) async-start(), calls=%async_computation.43 | async-start | bytes 2621440 | tf_op jit(solution)/shard_map/all_gather | solution.py:260
  1040.2 70.8 %reduce-scatter.49.cloned.1.call-start = ((), (), s32[]{:S(2)}) async-start(), calls=%async_computation.50 | async-start | bytes 655360 | tf_op jit(solution)/shard_map/reduce_scatter | solution.py:329
  1042.4 93.5 %reduce-scatter.51.cloned.1.call-start = ((), (), s32[]{:S(2)}) async-start(), calls=%async_computation.51 | async-start | bytes 655360 | tf_op jit(solution)/shard_map/reduce_scatter | solution.py:329
  1047.9 112.8 %reduce-scatter.53.cloned.1.call-start = ((), (), s32[]{:S(2)}) async-start(), calls=%async_computation.52 | async-start | bytes 655360 | tf_op jit(solution)/shard_map/reduce_scatter | solution.py:329
  1083.6 147.4 %reduce-scatter.27.cloned.1.call-start = ((), (), s32[]{:S(2)}) async-start(), calls=%async_computation.27 | async-start | bytes 2621440 | tf_op jit(solution)/shard_map/reduce_scatter | solution.py:191
  1199.0 86.4 %all-gather.30.cloned.1.call-start = ((), (), s32[]{:S(2)}) async-start(), calls=%async_computation.28 | async-start | bytes 2621440 | tf_op jit(solution)/shard_map/all_gather | solution.py:200
  1236.2 95.1 %reduce-scatter.47.cloned.1.call-start = ((), (), s32[]{:S(2)}) async-start(), calls=%async_computation.49 | async-start | bytes 2621440 | tf_op jit(solution)/shard_map/reduce_scatter | solution.py:332
  1257.3 289.7 %all-reduce.5.cloned.1.call-start = ((), (), s32[]{:S(2)}) async-start(), calls=%async_computation.54 | async-start | bytes 13893632 | tf_op jit(solution)/shard_map/psum | solution.py:367
  1284.9 295.0 %reduce-scatter.29.cloned.1.call-start = ((), (), s32[]{:S(2)}) async-start(), calls=%async_computation.29 | async-start | bytes 2621440 | tf_op jit(solution)/shard_map/reduce_scatter | solution.py:210
  (332 other events, 4704.7 us)
Sparse Core Ops, SparseCore 0:
  12.3 25.2 all-gather.19
  70.1 31.4 reduce-scatter.18
  137.6 31.4 reduce-scatter.20
  190.8 23.7 all-gather.23
  249.0 31.4 reduce-scatter.22
  316.9 31.4 reduce-scatter.24
  370.1 23.7 all-gather.31
  433.7 31.4 reduce-scatter.30
  471.3 22.7 all-gather.39
  496.2 22.9 all-gather.47
  520.8 22.6 all-gather.53
  571.3 31.4 reduce-scatter.36
  605.1 31.4 reduce-scatter.42
  639.7 31.3 reduce-scatter.32
  676.8 22.6 all-gather.35
  723.5 31.3 reduce-scatter.34
  822.9 31.4 reduce-scatter.38
  907.6 31.4 reduce-scatter.40
  1001.9 31.4 reduce-scatter.44
  1199.1 31.8 reduce-scatter.26
  1236.4 22.5 all-gather.29
  1261.5 31.4 reduce-scatter.46
  1297.1 249.8 all-reduce.4
  1549.5 30.2 reduce-scatter.28
  (13 shorter events, 290.1 us)
where the time goes:
time: 1600 us; the launch traced here: 1590 us
  waiting for transfers between devices  808 us (50%)
  matrix products  291 us (18%)
  other arithmetic  164 us (10%)
  blocking collectives  146 us (9%)
  local copies, waits for them, and re-layouts  103 us (6%)
  Pallas kernels  42.9 us (3%)
  between operations  18.6 us (1%)
  starting transfers between devices  16 us (1%)
    psum x1, waiting for transfers between devices, reduce_grads(): lax.psum(as_sent(weight_parts), 'dp')  132 us
    reduce_scatter x6, waiting for transfers between devices, front_pass(): lax.psum_scatter(jnp.einsum('htf,hfd->td', mixed, output_w, preferred_ele...  127 us
    reduce_scatter x3, waiting for transfers between devices, layer_backward(): lax.psum_scatter(jnp.einsum('tf,df->td', upper_grad, up_w, preferred_elem...  97.6 us
    reduce_scatter x3, waiting for transfers between devices, layer_forward(): lax.psum_scatter(jnp.dot(active, down_w, preferred_element_type=jnp.float...  82.5 us
    psum x1, blocking collectives, reduce_grads(): norm_sums = lax.psum(norm_parts, ('head', 'dp'))  77.8 us
    reduce_scatter x3, waiting for transfers between devices, layer_backward(): lax.psum_scatter(normed_grad[:memory_len].astype(jnp.bfloat16), 'head', s...  66.7 us
    reduce_scatter x3, waiting for transfers between devices, layer_backward(): lax.psum_scatter((normed_grad[memory_len:] + query_part).astype(jnp.bfloa...  62.3 us
    unnamed x640, local copies, waits for them, and re-layouts  55.9 us
  transfers between devices with their start and end apart: 41, of which 34 were waited for; matrix products, arithmetic and copies ran while one was open for 17% of the time, Pallas kernels for 1%

commit v1 on v0

v1 whole, which is shorter than its diff:
```python
import functools

import jax
import jax.numpy as jnp
from jax import lax
from jax.experimental import pallas as pl
from jax.experimental.pallas import tpu as pltpu
from jax.sharding import PartitionSpec as P

norm_eps = 1e-05
masked_score = -1e30
lanes = 128
bf16 = jnp.bfloat16
f32 = jnp.float32
gelu_c = 0.7978845608028654
gelu_a = 0.044715

core_pairs = [(0, 1), (1, 0), (2, 3), (3, 2)]
chip_pairs = [(0, 2), (2, 0), (1, 3), (3, 1)]
vmem_bytes = 50 * 1024 * 1024


def dot(a, b):
    return lax.dot_general(a, b, (((1,), (0,)), ((), ())), preferred_element_type=f32)


def dot_t(a, b):
    return lax.dot_general(a, b, (((1,), (1,)), ((), ())), preferred_element_type=f32)


def t_dot(a, b):
    return lax.dot_general(a, b, (((0,), (0,)), ((), ())), preferred_element_type=f32)


def params(**more):
    return pltpu.CompilerParams(vmem_limit_bytes=vmem_bytes, **more)


def whole_spec(shape):
    return pl.BlockSpec(shape, lambda *_: (0,) * len(shape))


def cost(flops, nbytes, trans=0):
    return pl.CostEstimate(flops=int(flops), bytes_accessed=int(nbytes), transcendentals=int(trans))


def to_core(a):
    return lax.ppermute(a, "head", core_pairs)


def to_chip(a):
    return lax.ppermute(a, "head", chip_pairs)


def swap_section(a):
    return lax.ppermute(a, "section", [(0, 1), (1, 0)])


def gather_slots(own):
    from_chip = to_chip(own)
    from_core = to_core(own)
    from_both = to_core(from_chip)
    return [own, from_core, from_chip, from_both]


def scatter_slots(parts):
    from_core_far = to_core(parts[3])
    from_core = to_core(parts[1])
    far = (parts[2].astype(f32) + from_core_far.astype(f32)).astype(bf16)
    return parts[0], from_core, to_chip(far)


def norm_rows(x, gain, shift):
    average = jnp.mean(x, axis=-1, keepdims=True)
    centred = x - average
    variance = jnp.mean(centred * centred, axis=-1, keepdims=True)
    return centred * lax.rsqrt(variance + norm_eps) * gain + shift


def norm_kernel(x_ref, gain_ref, shift_ref, out_ref):
    out_ref[...] = norm_rows(x_ref[...].astype(f32), gain_ref[...], shift_ref[...]).astype(bf16)


def norm_only(x, gain, shift):
    return pl.pallas_call(
        norm_kernel,
        out_shape=jax.ShapeDtypeStruct(x.shape, bf16),
        compiler_params=params(),
        cost_estimate=cost(x.size * 8, x.size * 4),
        name="norm_only",
    )(x, gain, shift)


def add_norm_kernel(x_ref, a_ref, b_ref, c_ref, add_ref, gain_ref, shift_ref, sum_ref, out_ref):
    total = x_ref[...].astype(f32) + (a_ref[...].astype(f32) + b_ref[...].astype(f32) + c_ref[...].astype(f32))
    total = total + add_ref[...]
    sum_ref[...] = total.astype(sum_ref.dtype)
    total = sum_ref[...].astype(f32)
    out_ref[...] = norm_rows(total, gain_ref[...], shift_ref[...]).astype(bf16)


def add_norm(x, terms, add, gain, shift, sum_type):
    return pl.pallas_call(
        add_norm_kernel,
        out_shape=(jax.ShapeDtypeStruct(x.shape, sum_type), jax.ShapeDtypeStruct(x.shape, bf16)),
        compiler_params=params(),
        cost_estimate=cost(x.size * 12, x.size * 14),
        name="add_norm",
    )(x, *terms, add, gain, shift)


def norm_back_kernel(x_ref, a_ref, b_ref, c_ref, gain_ref, more_ref, dx_ref, low_ref, small_ref):
    x = x_ref[...].astype(f32)
    grad = a_ref[...].astype(f32) + b_ref[...].astype(f32) + c_ref[...].astype(f32)
    average = jnp.mean(x, axis=-1, keepdims=True)
    centred = x - average
    variance = jnp.mean(centred * centred, axis=-1, keepdims=True)
    scale = lax.rsqrt(variance + norm_eps)
    unit = centred * scale
    wide = grad * gain_ref[...]
    mean_wide = jnp.mean(wide, axis=-1, keepdims=True)
    mean_unit = jnp.mean(wide * unit, axis=-1, keepdims=True)
    more = more_ref[...].astype(f32)
    dx = more + scale * (wide - mean_wide - unit * mean_unit)
    dx_ref[...] = dx
    low_ref[...] = dx.astype(bf16)
    small_ref[0:1, :] = jnp.sum(grad * unit, axis=0, keepdims=True)
    small_ref[1:2, :] = jnp.sum(grad, axis=0, keepdims=True)
    small_ref[2:3, :] = jnp.sum(more, axis=0, keepdims=True)
    small_ref[3:8, :] = jnp.zeros((5, x.shape[1]), f32)


def norm_back(x, terms, gain, more):
    return pl.pallas_call(
        norm_back_kernel,
        out_shape=(
            jax.ShapeDtypeStruct(x.shape, f32),
            jax.ShapeDtypeStruct(x.shape, bf16),
            jax.ShapeDtypeStruct((8, x.shape[1]), f32),
        ),
        compiler_params=params(),
        cost_estimate=cost(x.size * 20, x.size * 20),
        name="norm_back",
    )(x, *terms, gain, more)


def norm_back_small_kernel(x_ref, a_ref, b_ref, c_ref, small_ref):
    x = x_ref[...].astype(f32)
    grad = a_ref[...].astype(f32) + b_ref[...].astype(f32) + c_ref[...].astype(f32)
    average = jnp.mean(x, axis=-1, keepdims=True)
    centred = x - average
    variance = jnp.mean(centred * centred, axis=-1, keepdims=True)
    unit = centred * lax.rsqrt(variance + norm_eps)
    small_ref[0:1, :] = jnp.sum(grad * unit, axis=0, keepdims=True)
    small_ref[1:2, :] = jnp.sum(grad, axis=0, keepdims=True)
    small_ref[2:8, :] = jnp.zeros((6, x.shape[1]), f32)


def norm_back_small(x, terms):
    return pl.pallas_call(
        norm_back_small_kernel,
        out_shape=jax.ShapeDtypeStruct((8, x.shape[1]), f32),
        compiler_params=params(),
        cost_estimate=cost(x.size * 10, x.size * 8),
        name="norm_back_small",
    )(x, *terms)


def pick_slot(slot, refs, target):
    for number, ref in enumerate(refs):

        @pl.when(slot == number)
        def _(ref=ref):
            target[...] = ref[...]


def attn_fwd_kernel(
    experts,
    head_width,
    me_ref,
    mem_ref,
    p0_ref,
    p1_ref,
    p2_ref,
    p3_ref,
    w_ref,
    wo_ref,
    mask_ref,
    out_ref,
    normed_ref,
    q_ref,
    k_ref,
    v_ref,
    ev_ref,
    gate_ref,
    att_ref,
    mixed_ref,
    rows_s,
    k_s,
    v_s,
    mask_s,
):
    step = pl.program_id(0)
    me = me_ref[0]
    block = rows_s.shape[0]
    wide = experts * lanes
    quarter = block // 4

    @pl.when(step == 0)
    def _():
        rows_s[...] = mem_ref[...]
        for slot in range(4):
            start = pl.multiple_of((me ^ slot) * quarter, quarter)
            mask_s[slot * quarter : (slot + 1) * quarter, :] = mask_ref[pl.ds(start, quarter), :]

    @pl.when(step > 0)
    def _():
        pick_slot((step - 1) ^ me, (p0_ref, p1_ref, p2_ref, p3_ref), rows_s)
        mask_s[...] = mask_ref[pl.ds(pl.multiple_of(step * block, block), block), :]

    x = rows_s[...]
    normed_ref[...] = x
    proj = dot(x, w_ref[...])
    gate = jax.nn.sigmoid(proj[:, wide : wide + lanes]) * mask_s[...]
    value = jnp.zeros((block, lanes), f32)
    for j in range(experts):
        value = value + gate[:, j : j + 1] * proj[:, j * lanes : (j + 1) * lanes]
    start = pl.multiple_of(step * block, block)
    keys = proj[:, wide + lanes : wide + 2 * lanes].astype(bf16)
    value = value.astype(bf16)
    k_s[pl.ds(start, block), :] = keys
    v_s[pl.ds(start, block), :] = value
    k_ref[...] = keys
    v_ref[...] = value
    ev_ref[...] = proj[:, :wide].astype(bf16)
    queries = proj[:, wide + 2 * lanes :].astype(bf16)
    q_ref[...] = queries

    @pl.when(step == 0)
    def _():
        gate_ref[...] = gate

    scale = head_width ** (-0.5)
    for count in range(1, 5):

        @pl.when(step == count)
        def _(count=count):
            span = (count + 1) * block
            scores = dot_t(queries, k_s[0:span, :]) * scale
            row = lax.broadcasted_iota(jnp.int32, (block, block), 0)
            col = lax.broadcasted_iota(jnp.int32, (block, block), 1)
            last = jnp.where(col <= row, scores[:, span - block :], masked_score)
            scores = jnp.concatenate([scores[:, : span - block], last], axis=1)
            top = jnp.max(scores, axis=-1, keepdims=True)
            exponent = jnp.exp(scores - top)
            total = jnp.sum(exponent, axis=-1, keepdims=True)
            probs = (exponent * (1.0 / total)).astype(bf16)
            attended = dot(probs, v_s[0:span, :])
            att_ref[...] = attended
            lane = lax.broadcasted_iota(jnp.int32, (block, lanes), 1)
            gate_ref[...] = jnp.where(lane == 2 * experts, top + jnp.log(total), gate)
            mixed = jnp.concatenate(
                [(gate[:, experts + j : experts + j + 1] * attended).astype(bf16) for j in range(experts)], axis=1
            )
            mixed_ref[...] = mixed
            out_ref[0] = dot(mixed, wo_ref[...]).astype(bf16)


def attn_fwd(me, mem, slots, w, wo, mask, experts, head_width):
    block, width = slots[0].shape
    total = 5 * block
    wide = experts * lanes
    later = lambda i, me_ref: (jnp.maximum(i - 1, 0), 0)
    every = lambda i, me_ref: (i, 0)
    shapes = lambda rows, cols, kind: jax.ShapeDtypeStruct((rows, cols), kind)
    grid_spec = pltpu.PrefetchScalarGridSpec(
        num_scalar_prefetch=1,
        grid=(5,),
        in_specs=[whole_spec((block, width))] * 5
        + [whole_spec(w.shape), whole_spec(wo.shape), whole_spec(mask.shape)],
        out_specs=[
            pl.BlockSpec((1, block, width), lambda i, me_ref: (jnp.maximum(i - 1, 0) ^ me_ref[0], 0, 0)),
            pl.BlockSpec((block, width), every),
            pl.BlockSpec((block, lanes), every),
            pl.BlockSpec((block, lanes), every),
            pl.BlockSpec((block, lanes), every),
            pl.BlockSpec((block, wide), every),
            pl.BlockSpec((block, lanes), every),
            pl.BlockSpec((block, lanes), later),
            pl.BlockSpec((block, wide), later),
        ],
        scratch_shapes=[
            pltpu.VMEM((block, width), bf16),
            pltpu.VMEM((total, lanes), bf16),
            pltpu.VMEM((total, lanes), bf16),
            pltpu.VMEM((block, lanes), f32),
        ],
    )
    return pl.pallas_call(
        functools.partial(attn_fwd_kernel, experts, head_width),
        grid_spec=grid_spec,
        out_shape=(
            jax.ShapeDtypeStruct((4, block, width), bf16),
            shapes(total, width, bf16),
            shapes(total, lanes, bf16),
            shapes(total, lanes, bf16),
            shapes(total, lanes, bf16),
            shapes(total, wide, bf16),
            shapes(total, lanes, f32),
            shapes(4 * block, lanes, f32),
            shapes(4 * block, wide, bf16),
        ),
        compiler_params=params(dimension_semantics=("arbitrary",)),
        cost_estimate=cost(2 * total * width * w.shape[1] + 2 * 4 * block * wide * width, 20 * 1024 * 1024, total * total),
        name="attn_fwd",
    )(me, mem, *slots, w, wo, mask)


def attn_bwd_kernel(
    experts,
    head_width,
    me_ref,
    d0_ref,
    d1_ref,
    d2_ref,
    d3_ref,
    w_ref,
    wo_ref,
    q_ref,
    k_ref,
    v_ref,
    ev_ref,
    gate_ref,
    att_ref,
    ngs_ref,
    ngm_ref,
    dproj_ref,
    da_ref,
    rows_s,
    dk_s,
    dv_s,
    dq_s,
    dlog_s,
):
    step = pl.program_id(0)
    me = me_ref[0]
    here = 4 - step
    block = rows_s.shape[0]
    wide = experts * lanes
    scale = head_width ** (-0.5)
    gate = gate_ref[...]
    lane = lax.broadcasted_iota(jnp.int32, (block, lanes), 1)

    @pl.when(step == 0)
    def _():
        dk_s[...] = jnp.zeros_like(dk_s)
        dv_s[...] = jnp.zeros_like(dv_s)

    @pl.when(here == 0)
    def _():
        dq_s[...] = jnp.zeros_like(dq_s)
        dlog_s[...] = jnp.zeros_like(dlog_s)

    for count in range(1, 5):

        @pl.when(here == count)
        def _(count=count):
            pick_slot((count - 1) ^ me, (d0_ref, d1_ref, d2_ref, d3_ref), rows_s)
            rows = rows_s[...]
            da_ref[...] = rows
            mixed_grad = dot_t(rows, wo_ref[...])
            attended = att_ref[...]
            att_grad = jnp.zeros((block, lanes), f32)
            logit_grad = jnp.zeros((block, lanes), f32)
            for j in range(experts):
                part = mixed_grad[:, j * lanes : (j + 1) * lanes]
                att_grad = att_grad + gate[:, experts + j : experts + j + 1] * part
                inner = jnp.sum(part * attended, axis=-1, keepdims=True)
                logit_grad = jnp.where(lane == experts + j, inner, logit_grad)
            dlog_s[...] = logit_grad
            grad_low = att_grad.astype(bf16)
            row_sum = jnp.sum(att_grad * attended, axis=-1, keepdims=True)
            log_total = gate[:, 2 * experts : 2 * experts + 1]
            span = (count + 1) * block
            queries = q_ref[...]
            keys = k_ref[0:span, :]
            scores = dot_t(queries, keys) * scale
            row = lax.broadcasted_iota(jnp.int32, (block, block), 0)
            col = lax.broadcasted_iota(jnp.int32, (block, block), 1)
            last = jnp.where(col <= row, scores[:, span - block :], masked_score)
            scores = jnp.concatenate([scores[:, : span - block], last], axis=1)
            probs = jnp.exp(scores - log_total)
            probs_grad = dot_t(grad_low, v_ref[0:span, :])
            score_grad = (probs * (probs_grad - row_sum)).astype(bf16)
            dq_s[...] = dot(score_grad, keys) * scale
            dk_s[0:span, :] += t_dot(score_grad, queries)
            dv_s[0:span, :] += t_dot(probs.astype(bf16), grad_low)

    start = pl.multiple_of(here * block, block)
    value_grad = dv_s[pl.ds(start, block), :].astype(bf16).astype(f32)
    parts = []
    logit_grad = dlog_s[...]
    for j in range(experts):
        parts.append((gate[:, j : j + 1] * value_grad).astype(bf16))
        inner = jnp.sum(value_grad * ev_ref[:, j * lanes : (j + 1) * lanes].astype(f32), axis=-1, keepdims=True)
        logit_grad = jnp.where(lane == j, inner, logit_grad)
    slope = jnp.where(lane < 2 * experts, gate * (1.0 - gate), 0.0)
    parts.append((logit_grad * slope).astype(bf16))
    parts.append((dk_s[pl.ds(start, block), :] * scale).astype(bf16))
    parts.append(dq_s[...].astype(bf16))
    dproj = jnp.concatenate(parts, axis=1)
    dproj_ref[...] = dproj
    normed_grad = dot_t(dproj, w_ref[...]).astype(bf16)

    @pl.when(here > 0)
    def _():
        ngs_ref[0] = normed_grad

    @pl.when(here == 0)
    def _():
        ngm_ref[...] = normed_grad


def attn_bwd(me, slots, w, wo, saved, experts, head_width):
    q, k, v, ev, gate, att = saved
    block, width = slots[0].shape
    total = 5 * block
    wide = experts * lanes
    back = lambda i, me_ref: (4 - i, 0)
    later = lambda i, me_ref: (jnp.maximum(3 - i, 0), 0)
    grid_spec = pltpu.PrefetchScalarGridSpec(
        num_scalar_prefetch=1,
        grid=(5,),
        in_specs=[whole_spec((block, width))] * 4
        + [
            whole_spec(w.shape),
            whole_spec(wo.shape),
            pl.BlockSpec((block, lanes), back),
            whole_spec(k.shape),
            whole_spec(v.shape),
            pl.BlockSpec((block, wide), back),
            pl.BlockSpec((block, lanes), back),
            pl.BlockSpec((block, lanes), later),
        ],
        out_specs=[
            pl.BlockSpec((1, block, width), lambda i, me_ref: (jnp.maximum(3 - i, 0) ^ me_ref[0], 0, 0)),
            whole_spec((block, width)),
            pl.BlockSpec((block, w.shape[1]), back),
            pl.BlockSpec((block, width), later),
        ],
        scratch_shapes=[
            pltpu.VMEM((block, width), bf16),
            pltpu.VMEM((total, lanes), f32),
            pltpu.VMEM((total, lanes), f32),
            pltpu.VMEM((block, lanes), f32),
            pltpu.VMEM((block, lanes), f32),
        ],
    )
    return pl.pallas_call(
        functools.partial(attn_bwd_kernel, experts, head_width),
        grid_spec=grid_spec,
        out_shape=(
            jax.ShapeDtypeStruct((4, block, width), bf16),
            jax.ShapeDtypeStruct((block, width), bf16),
            jax.ShapeDtypeStruct((total, w.shape[1]), bf16),
            jax.ShapeDtypeStruct((4 * block, width), bf16),
        ),
        compiler_params=params(dimension_semantics=("arbitrary",)),
        cost_estimate=cost(2 * total * width * w.shape[1] + 2 * 4 * block * wide * width, 20 * 1024 * 1024, total * total),
        name="attn_bwd",
    )(me, *slots, w, wo, q, k, v, ev, gate, att)


def ffn_fwd_kernel(p0_ref, p1_ref, p2_ref, p3_ref, wu_ref, bu_ref, wd_ref, out_ref, rows_ref, upper_ref, active_ref, rows_s):
    pick_slot(pl.program_id(0), (p0_ref, p1_ref, p2_ref, p3_ref), rows_s)
    x = rows_s[...]
    rows_ref[...] = x
    upper = dot(x, wu_ref[...]) + bu_ref[...]
    upper_ref[...] = upper.astype(bf16)
    active = jax.nn.gelu(upper).astype(bf16)
    active_ref[...] = active
    out_ref[0] = dot(active, wd_ref[...]).astype(bf16)


def ffn_fwd(slots, wu, bu, wd):
    block, width = slots[0].shape
    hidden = wu.shape[1]
    rows = lambda i: (i, 0)
    return pl.pallas_call(
        ffn_fwd_kernel,
        grid=(4,),
        in_specs=[whole_spec((block, width))] * 4 + [whole_spec(wu.shape), whole_spec(bu.shape), whole_spec(wd.shape)],
        out_specs=[
            pl.BlockSpec((1, block, width), lambda i: (i, 0, 0)),
            pl.BlockSpec((block, width), rows),
            pl.BlockSpec((block, hidden), rows),
            pl.BlockSpec((block, hidden), rows),
        ],
        out_shape=(
            jax.ShapeDtypeStruct((4, block, width), bf16),
            jax.ShapeDtypeStruct((4 * block, width), bf16),
            jax.ShapeDtypeStruct((4 * block, hidden), bf16),
            jax.ShapeDtypeStruct((4 * block, hidden), bf16),
        ),
        scratch_shapes=[pltpu.VMEM((block, width), bf16)],
        compiler_params=params(dimension_semantics=("arbitrary",)),
        cost_estimate=cost(16 * block * width * hidden, 14 * 1024 * 1024, 4 * block * hidden),
        name="ffn_fwd",
    )(*slots, wu, bu, wd)


def ffn_bwd_kernel(
    g0_ref, g1_ref, g2_ref, g3_ref, upper_ref, wd_ref, wu_ref, out_ref, rows_ref, ug_ref, bias_ref, rows_s
):
    step = pl.program_id(0)
    pick_slot(step, (g0_ref, g1_ref, g2_ref, g3_ref), rows_s)
    g = rows_s[...]
    rows_ref[...] = g
    active_grad = dot_t(g, wd_ref[...])
    u = upper_ref[...].astype(f32)
    square = u * u
    t = jnp.tanh(gelu_c * u * (1.0 + gelu_a * square))
    slope = 0.5 * (1.0 + t) + 0.5 * gelu_c * u * (1.0 - t * t) * (1.0 + 3.0 * gelu_a * square)
    upper_grad = (active_grad * slope).astype(bf16)
    ug_ref[...] = upper_grad
    sums = jnp.sum(upper_grad.astype(f32), axis=0, keepdims=True)

    @pl.when(step == 0)
    def _():
        bias_ref[...] = sums

    @pl.when(step > 0)
    def _():
        bias_ref[...] += sums

    out_ref[0] = dot_t(upper_grad, wu_ref[...]).astype(bf16)


def ffn_bwd(slots, upper, wd, wu):
    block, width = slots[0].shape
    hidden = wu.shape[1]
    rows = lambda i: (i, 0)
    return pl.pallas_call(
        ffn_bwd_kernel,
        grid=(4,),
        in_specs=[whole_spec((block, width))] * 4
        + [pl.BlockSpec((block, hidden), rows), whole_spec(wd.shape), whole_spec(wu.shape)],
        out_specs=[
            pl.BlockSpec((1, block, width), lambda i: (i, 0, 0)),
            pl.BlockSpec((block, width), rows),
            pl.BlockSpec((block, hidden), rows),
            whole_spec((1, hidden)),
        ],
        out_shape=(
            jax.ShapeDtypeStruct((4, block, width), bf16),
            jax.ShapeDtypeStruct((4 * block, width), bf16),
            jax.ShapeDtypeStruct((4 * block, hidden), bf16),
            jax.ShapeDtypeStruct((1, hidden), f32),
        ),
        scratch_shapes=[pltpu.VMEM((block, width), bf16)],
        compiler_params=params(dimension_semantics=("arbitrary",)),
        cost_estimate=cost(16 * block * width * hidden, 14 * 1024 * 1024, 4 * block * hidden),
        name="ffn_bwd",
    )(*slots, upper, wd, wu)


def sum_dp(part):
    if lax.axis_size("dp") != 4:
        return lax.psum(part, "dp").astype(f32)
    kind = part.dtype
    place = lax.axis_index("dp")
    inward = lax.ppermute(part, "dp", [(0, 1), (3, 2)])
    half = (part.astype(f32) + inward.astype(f32)).astype(kind)
    other = lax.ppermute(half, "dp", [(1, 2), (2, 1)])
    full = (half.astype(f32) + other.astype(f32)).astype(kind)
    outward = lax.ppermute(full, "dp", [(1, 0), (2, 3)])
    return jnp.where((place == 1) | (place == 2), full, outward).astype(f32)


def cut(a, pieces):
    rows = a.shape[0] // pieces
    return [a[i * rows : (i + 1) * rows] for i in range(pieces)]


def pad_lanes(a, axis, count, width):
    shape = a.shape[:axis] + (count, width) + a.shape[axis + 1 :]
    pads = [(0, 0)] * len(shape)
    pads[axis + 1] = (0, lanes - width)
    padded = jnp.pad(a.reshape(shape), pads)
    return padded.reshape(a.shape[:axis] + (count * lanes,) + a.shape[axis + 1 :])


def spread(pack, experts, width):
    ev = experts * width
    routers = jnp.pad(pack[:, ev + 2 * width :], ((0, 0), (0, lanes - 2 * experts)))
    key = jnp.pad(pack[:, ev : ev + width], ((0, 0), (0, lanes - width)))
    query = jnp.pad(pack[:, ev + width : ev + 2 * width], ((0, 0), (0, lanes - width)))
    return jnp.concatenate([pad_lanes(pack[:, :ev], 1, experts, width), routers, key, query], axis=1)


def squeeze(wide, experts, width):
    base = experts * lanes
    parts = [wide[:, j * lanes : j * lanes + width] for j in range(experts)]
    parts.append(wide[:, base + lanes : base + lanes + width])
    parts.append(wide[:, base + 2 * lanes : base + 2 * lanes + width])
    parts.append(wide[:, base : base + 2 * experts])
    return jnp.concatenate(parts, axis=1)


def route_mask(value_ids, out_ids, experts, memory_len):
    lane = jnp.arange(lanes, dtype=jnp.int32)[None, :]
    out_full = jnp.pad(out_ids, ((0, 0), (memory_len, 0)), constant_values=-1)
    hit = jnp.zeros((value_ids.shape[1], lanes), jnp.bool_)
    for k in range(value_ids.shape[0]):
        hit = hit | (lane == value_ids[k][:, None])
        hit = hit | ((lane == out_full[k][:, None] + experts) & (out_full[k][:, None] >= 0))
    return hit.astype(f32)


def on_device(
    inputs,
    memory,
    value_routes,
    out_routes,
    ln1_gain,
    ln1_bias,
    query_weight,
    key_weight,
    value_weight,
    value_router,
    out_router,
    output_weight,
    ln2_gain,
    ln2_bias,
    up_weight,
    up_bias,
    down_weight,
    down_bias,
    out_cot,
):
    experts = value_router.shape[-1]
    head_width = query_weight.shape[-1]
    sec = lax.axis_index("section")
    head = lax.axis_index("head")
    me = head.astype(jnp.int32).reshape(1)
    first = sec == 0
    pick = lambda a, index: lax.dynamic_index_in_dim(a, index, 0, keepdims=False)
    memory_len = memory.shape[2] * lax.axis_size("head")

    pack = jnp.concatenate([value_weight[0, 0], key_weight[0, 0], query_weight[0, 0], value_router[0, 0], out_router[0, 0]], axis=1)
    small = jnp.concatenate([ln1_gain, ln1_bias, ln2_gain, ln2_bias, up_bias, down_bias, jnp.zeros_like(jnp.tile(ln1_gain, (2, 1)))], axis=0)
    route_rows = jnp.concatenate(
        [
            jnp.transpose(value_routes[0, :, :, 0, :], (0, 2, 1)),
            jnp.pad(jnp.transpose(out_routes[0, :, :, 0, :], (0, 2, 1)), ((0, 0), (0, 0), (memory_len, 0)), constant_values=-1),
        ],
        axis=1,
    )

    def both_layers(own, sent):
        got = swap_section(sent)
        return jnp.where(first, own, got), jnp.where(first, got, own)

    smalls = both_layers(small, small)
    route_sets = both_layers(pick(route_rows, sec), pick(route_rows, 1 - sec))
    memories = both_layers(pick(memory[0], sec), pick(memory[0], 1 - sec))
    packs = both_layers(pack, pack)
    outs_w = both_layers(output_weight[0, 0], output_weight[0, 0])
    ups = both_layers(up_weight[0], up_weight[0])
    downs = both_layers(down_weight[0], down_weight[0])

    x = pick(inputs, sec)
    cot = pick(out_cot, sec)
    topk = value_routes.shape[-1]

    layers = []
    for number in range(2):
        vec = smalls[number]
        routes = route_sets[number]
        layers.append(
            dict(
                gain1=vec[0:1],
                shift1=vec[1:2],
                gain2=vec[2:3],
                shift2=vec[3:4],
                up_b=vec[4:5],
                down_b=vec[5:6],
                w=spread(packs[number], experts, head_width),
                wo=pad_lanes(outs_w[number], 0, experts, head_width),
                wu=ups[number],
                wd=downs[number],
                mask=route_mask(routes[:topk], routes[topk:, memory_len:], experts, memory_len),
                mem=memories[number],
            )
        )
    no_add = jnp.zeros_like(layers[0]["gain1"])

    own_norm = norm_only(x, layers[0]["gain1"], layers[0]["shift1"])
    slots = gather_slots(own_norm)
    for layer in layers:
        layer["mem_all"] = jnp.concatenate(gather_slots(norm_only(layer["mem"], layer["gain1"], layer["shift1"])), axis=0)
    cot_slots = gather_slots(cot)

    saves = []
    rows_in = x
    layer_outs = []
    for number, layer in enumerate(layers):
        out, normed, q, k, v, ev, gate, att, mixed = attn_fwd(
            me, layer["mem_all"], slots, layer["w"], layer["wo"], layer["mask"], experts, head_width
        )
        terms = scatter_slots([out[s] for s in range(4)])
        hidden, own_norm2 = add_norm(rows_in, terms, no_add, layer["gain2"], layer["shift2"], f32)
        n2_slots = gather_slots(own_norm2)
        ffn, n2, upper, active = ffn_fwd(n2_slots, layer["wu"], layer["up_b"], layer["wd"])
        terms = scatter_slots([ffn[s] for s in range(4)])
        next_layer = layers[min(number + 1, 1)]
        result, own_norm = add_norm(hidden, terms, layer["down_b"], next_layer["gain1"], next_layer["shift1"], bf16)
        layer_outs.append(result)
        saves.append(
            dict(rows=rows_in, normed=normed, attn=(q, k, v, ev, gate, att), mixed=mixed, hidden=hidden, n2=n2, upper=upper, active=active)
        )
        if number == 0:
            rows_in = result
            slots = gather_slots(own_norm)

    input_grads = [None, None]
    grads = [None, None]
    g_rows = cot
    g_slots = cot_slots
    for number in (1, 0):
        layer, saved = layers[number], saves[number]
        ffn, g_all, upper_grad, up_bias_grad = ffn_bwd(g_slots, saved["upper"], layer["wd"], layer["wu"])
        terms = scatter_slots([ffn[s] for s in range(4)])
        down_grad = t_dot(saved["active"], g_all).astype(bf16)
        up_grad = t_dot(saved["n2"], upper_grad).astype(bf16)
        hidden_grad, hidden_low, small2 = norm_back(saved["hidden"], terms, layer["gain2"], g_rows)
        a_slots = gather_slots(hidden_low)
        ngs, ngm, dproj, a_all = attn_bwd(me, a_slots, layer["w"], layer["wo"], saved["attn"], experts, head_width)
        seq_terms = scatter_slots([ngs[s] for s in range(4)])
        mem_terms = scatter_slots(cut(ngm, 4))
        out_grad = t_dot(saved["mixed"], a_all).astype(bf16)
        out_grad = out_grad.reshape(experts, lanes, -1)[:, :head_width].reshape(experts * head_width, -1)
        pack_grad = squeeze(t_dot(saved["normed"], dproj).astype(bf16), experts, head_width)
        _, input_low, small1 = norm_back(saved["rows"], seq_terms, layer["gain1"], hidden_grad)
        small_mem = norm_back_small(layer["mem"], mem_terms)
        input_grads[number] = input_low
        over_head = jnp.concatenate([(small1 + small_mem)[0:2], small2[0:3], jnp.zeros_like(small2[0:3])], axis=0)
        grads[number] = dict(
            arrays=cut(down_grad, 2) + cut(up_grad, 2) + cut(out_grad, 1) + cut(pack_grad, 2),
            over_head=over_head,
            up_bias=up_bias_grad,
        )
        if number == 1:
            g_rows = input_low
            g_slots = gather_slots(input_low)

    def combine(one, two):
        kind = one.dtype
        from_first = lax.ppermute(two, "section", [(0, 1)])
        from_second = lax.ppermute(one, "section", [(1, 0)])
        at_second = (two.astype(f32) + from_first.astype(f32)).astype(kind)
        at_first = (one.astype(f32) + from_second.astype(f32)).astype(kind)
        return jnp.where(first, at_first, at_second)

    sums = [sum_dp(combine(one, two)) for one, two in zip(grads[0]["arrays"], grads[1]["arrays"])]
    vecs = []
    for grad in grads:
        vec = grad["over_head"]
        vec = vec + to_core(vec)
        vec = vec + to_chip(vec)
        vecs.append(jnp.concatenate([vec[0:5], grad["up_bias"], vec[6:8]], axis=0))
    vec = sum_dp(combine(*vecs))

    down_sum = jnp.concatenate(sums[0:2], axis=0)
    up_sum = jnp.concatenate(sums[2:4], axis=0)
    out_sum = sums[4]
    pack_sum = jnp.concatenate(sums[5:7], axis=0)
    ev = experts * head_width
    value_sum, key_sum = pack_sum[:, :ev], pack_sum[:, ev : ev + head_width]
    query_sum = pack_sum[:, ev + head_width : ev + 2 * head_width]
    vroute_sum = pack_sum[:, ev + 2 * head_width : ev + 2 * head_width + experts]
    oroute_sum = pack_sum[:, ev + 2 * head_width + experts :]

    def by_layer(one, two):
        kept = jnp.where(first, one, two)
        got = swap_section(jnp.where(first, two, one))
        return jnp.stack([jnp.where(first, kept, got), jnp.where(first, got, kept)])[None]

    return (
        by_layer(*layer_outs),
        by_layer(*input_grads),
        vec[0:1],
        vec[1:2],
        query_sum[None, None],
        key_sum[None, None],
        value_sum[None, None],
        vroute_sum[None, None],
        oroute_sum[None, None],
        out_sum[None, None],
        vec[2:3],
        vec[3:4],
        up_sum[None],
        vec[5:6],
        down_sum[None],
        vec[4:5],
    )


def solution(mesh):
    placed = (
        P("dp", "head", None),
        P("section", "dp", "head", None),
        P("section", "dp", None, "head", None),
        P("section", "dp", None, "head", None),
        P("section", None),
        P("section", None),
        P("section", "head", None, None),
        P("section", "head", None, None),
        P("section", "head", None, None),
        P("section", "head", None, None),
        P("section", "head", None, None),
        P("section", "head", None, None),
        P("section", None),
        P("section", None),
        P("section", None, "head"),
        P("section", "head"),
        P("section", "head", None),
        P("section", None),
        P("dp", "head", None),
    )
    return jax.shard_map(
        on_device,
        mesh=mesh,
        in_specs=placed,
        out_specs=(
            P("section", "dp", "head", None),
            P("section", "dp", "head", None),
            P("section", None),
            P("section", None),
            P("section", "head", None, None),
            P("section", "head", None, None),
            P("section", "head", None, None),
            P("section", "head", None, None),
            P("section", "head", None, None),
            P("section", "head", None, None),
            P("section", None),
            P("section", None),
            P("section", None, "head"),
            P("section", "head"),
            P("section", "head", None),
            P("section", None),
        ),
        check_vma=False,
    )
```

time: 1600 us -> 962 us (0.60)
  waiting for transfers between devices: 808 us -> 459 us
  matrix products: 291 us -> 31.2 us
  starting transfers between devices: 16 us -> 181 us
  blocking collectives: 146 us -> 0 us
  other arithmetic: 164 us -> 74.5 us
  Pallas kernels: 42.9 us -> 129 us
  local copies, waits for them, and re-layouts: 103 us -> 78.3 us
  between operations: 18.6 us -> 2.48 us
    reduce_scatter x18 -> x0, waiting for transfers between devices: 436 us -> none  [the longest x6 127 us: front_pass(): lax.psum_scatter(jnp.einsum('htf,hfd->td', mixed, output_w, preferred_ele...]
    ppermute x4 -> x113, waiting for transfers between devices: 48.6 us -> 459 us  [the longest x22 133 us: to_chip(): return lax.ppermute(a, 'head', chip_pairs)]
    dot_general x126 -> x8, matrix products: 291 us -> 31.2 us  [t_dot(): lax.dot_general(a, b, (((0,), (0,)), ((), ())), preferred_element_type=f32)]
    all_gather x18 -> x0, waiting for transfers between devices: 189 us -> none  [the longest x6 52.8 us: gather_normed(): lax.all_gather(own_part, 'head', axis=0, tiled=True)]
    ppermute x4 -> x113, starting transfers between devices: 10.9 us -> 181 us  [the longest x8 68.5 us: sum_dp(): inward = lax.ppermute(part, 'dp', [(0, 1), (3, 2)])]
    psum x1 -> x0, waiting for transfers between devices: 132 us -> none  [reduce_grads(): lax.psum(as_sent(weight_parts), 'dp')]
    pallas_call x0 -> x21, Pallas kernels: none -> 129 us  [the longest x2 38.3 us: attn_fwd(): pl.pallas_call(functools.partial(attn_fwd_kernel, experts, head_width), g...]
    psum x2 -> x0, blocking collectives: 102 us -> none  [the longest x1 77.8 us: reduce_grads(): norm_sums = lax.psum(norm_parts, ('head', 'dp'))]
  transfers between devices with their start and end apart: 41 -> 113, of which waited for: 34 -> 36; matrix products, arithmetic and copies ran while one was open for 17% -> 18% of each run, Pallas kernels for 1% -> 10%
where the time goes in v1:
time: 962 us; the launch traced here: 956 us
  waiting for transfers between devices  459 us (48%)
  starting transfers between devices  181 us (19%)
  Pallas kernels  129 us (13%)
  local copies, waits for them, and re-layouts  78.3 us (8%)
  other arithmetic  74.5 us (8%)
  matrix products  31.2 us (3%)
    ppermute x22, waiting for transfers between devices, to_chip(): return lax.ppermute(a, 'head', chip_pairs)  133 us
    ppermute x8, waiting for transfers between devices, sum_dp(): outward = lax.ppermute(full, 'dp', [(1, 0), (2, 3)])  124 us
    ppermute x9, waiting for transfers between devices, swap_section(): return lax.ppermute(a, 'section', [(0, 1), (1, 0)])  89.1 us
    ppermute x8, starting transfers between devices, sum_dp(): inward = lax.ppermute(part, 'dp', [(0, 1), (3, 2)])  68.5 us
    ppermute x8, waiting for transfers between devices, sum_dp(): inward = lax.ppermute(part, 'dp', [(0, 1), (3, 2)])  56.2 us
    ppermute x8, waiting for transfers between devices, combine(): from_second = lax.ppermute(one, 'section', [(1, 0)])  54.3 us
    pallas_call x2, Pallas kernels, attn_fwd(): pl.pallas_call(functools.partial(attn_fwd_kernel, experts, head_width), g...  38.3 us
    pallas_call x2, Pallas kernels, attn_bwd(): pl.pallas_call(functools.partial(attn_bwd_kernel, experts, head_width), g...  31.6 us
  transfers between devices with their start and end apart: 113, of which 36 were waited for; matrix products, arithmetic and copies ran while one was open for 18% of the time, Pallas kernels for 10%

profile of v1, /device:TPU:0, one launch (start us, length us, event | category | flops | bytes accessed | tf_op | source)
XLA Modules:
  0.0 955.9 jit_solution(8604428873850016947)
XLA Ops:
  23.5 55.0 %collective-permute-done.10 = s32[4,1280]{1,0:T(4,128)} collective-permute-done((s32[4,1280]{1,0:T(4,128)}, s32[4,1280]{1,0:T(4,128)}, u32[]{:S(2)}, u32[]{:S(2)}) %collective-permute-start.10) | collective-permute-done | bytes 20512 | tf_op jit(solution)/shard_map/ppermute | solution.py:56
  116.3 14.4 %attn_fwd.2 = (bf16[4,256,1024]{2,1,0:T(8,128)(2,1)}, bf16[1280,1024]{1,0:T(8,128)(2,1)}, bf16[1280,128]{1,0:T(8,128)(2,1)S(1)}, bf16[1280,128]{1,0:T(8,128)(2,1...) custom-call(s32[1]{0:T(128)} %bitcast.1.me_ref, ...), custom_call_target="tpu_custom_call" | custom-call | flops 4026531840 | bytes 20971520 | tf_op jit(solution)/shard_map/attn_fwd/pallas_call | solution.py:299
  138.5 12.6 %collective-permute-done.13.c_ref = bf16[256,1024]{1,0:T(8,128)(2,1)S(1)} collective-permute-done((bf16[256,1024]{1,0:T(8,128)(2,1)S(1)}, bf16[256,1024]{1,0:T(8,128)(2,1)S(1)}, u32[]{:S(2)}, u32[]{:S(2)}) %collective-permute-start.13) | collective-permute-done | bytes 524320 | tf_op jit(solution)/shard_map/ppermute | solution.py:52
  200.6 12.4 %collective-permute-done.21.c_ref = bf16[256,1024]{1,0:T(8,128)(2,1)S(1)} collective-permute-done((bf16[256,1024]{1,0:T(8,128)(2,1)S(1)}, bf16[256,1024]{1,0:T(8,128)(2,1)S(1)}, u32[]{:S(2)}, u32[]{:S(2)}) %collective-permute-start.21) | collective-permute-done | bytes 524320 | tf_op jit(solution)/shard_map/ppermute | solution.py:52
  239.6 23.8 %attn_fwd.3 = (bf16[4,256,1024]{2,1,0:T(8,128)(2,1)}, bf16[1280,1024]{1,0:T(8,128)(2,1)}, bf16[1280,128]{1,0:T(8,128)(2,1)S(1)}, bf16[1280,128]{1,0:T(8,128)(2,1...) custom-call(s32[1]{0:T(128)} %bitcast.1.me_ref, ...), custom_call_target="tpu_custom_call" | custom-call | flops 4026531840 | bytes 20971520 | tf_op jit(solution)/shard_map/attn_fwd/pallas_call | solution.py:299
  270.4 12.7 %collective-permute-done.30.c_ref = bf16[256,1024]{1,0:T(8,128)(2,1)S(1)} collective-permute-done((bf16[256,1024]{1,0:T(8,128)(2,1)S(1)}, bf16[256,1024]{1,0:T(8,128)(2,1)S(1)}, u32[]{:S(2)}, u32[]{:S(2)}) %collective-permute-start.30) | collective-permute-done | bytes 524320 | tf_op jit(solution)/shard_map/ppermute | solution.py:52
  286.6 12.9 %collective-permute-done.32.p2_ref = bf16[256,1024]{1,0:T(8,128)(2,1)S(1)} collective-permute-done((bf16[256,1024]{1,0:T(8,128)(2,1)}, bf16[256,1024]{1,0:T(8,128)(2,1)S(1)}, u32[]{:S(2)}, u32[]{:S(2)}) %collective-permute-start.32) | collective-permute-done | bytes 524320 | tf_op jit(solution)/shard_map/ppermute | solution.py:52
  383.3 21.8 %collective-permute-done.37 = bf16[256,1024]{1,0:T(8,128)(2,1)S(1)} collective-permute-done((bf16[256,1024]{1,0:T(8,128)(2,1)S(1)}, bf16[256,1024]{1,0:T(8,128)(2,1)S(1)}, u32[]{:S(2)}, u32[]{:S(2)}) %collective-permute-start.37) | collective-permute-done | bytes 524320 | tf_op jit(solution)/shard_map/ppermute | solution.py:56
  406.3 16.0 %attn_bwd.2 = (bf16[4,256,1024]{2,1,0:T(8,128)(2,1)}, bf16[256,1024]{1,0:T(8,128)(2,1)S(1)}, bf16[1280,1024]{1,0:T(8,128)(2,1)}, bf16[1024,1024]{1,0:T(8,128)(2,1)}) custom-call(s32[1]{0:T(128)} %bitcast.1.me_ref, bf16[256,1024]{1,0:T(8,128)(2,1)S(1)} %get-tuple-element.88.d0_ref, bf16[256,1024]{1,0:T(8,128)(2,1)S(1)} %collective-permute-done.44.d1_ref, ...), custom_call_target="tpu_custom_call" | custom-call | flops 4026531840 | bytes 20971520 | tf_op jit(solution)/shard_map/attn_bwd/pallas_call | solution.py:459
  549.4 14.1 %collective-permute-done.103 = bf16[512,1024]{1,0:T(8,128)(2,1)} collective-permute-done((bf16[512,1024]{1,0:T(8,128)(2,1)}, bf16[512,1024]{1,0:T(8,128)(2,1)}, u32[]{:S(2)}, u32[]{:S(2)}) %collective-permute-start.103) | collective-permute-done | bytes 1048608 | tf_op jit(solution)/shard_map/ppermute | solution.py:760
  565.8 19.4 %collective-permute-done.108 = bf16[512,1024]{1,0:T(8,128)(2,1)} collective-permute-done((bf16[512,1024]{1,0:T(8,128)(2,1)}, bf16[512,1024]{1,0:T(8,128)(2,1)}, u32[]{:S(2)}, u32[]{:S(2)}) %collective-permute-start.108) | collective-permute-done | bytes 1048608 | tf_op jit(solution)/shard_map/ppermute | solution.py:760
  598.1 15.6 %attn_bwd.3 = (bf16[4,256,1024]{2,1,0:T(8,128)(2,1)}, bf16[256,1024]{1,0:T(8,128)(2,1)S(1)}, bf16[1280,1024]{1,0:T(8,128)(2,1)}, bf16[1024,1024]{1,0:T(8,128)(2,1)}) custom-call(s32[1]{0:T(128)} %bitcast.1.me_ref, bf16[256,1024]{1,0:T(8,128)(2,1)S(1)} %get-tuple-element.100.d0_ref, bf16[256,1024]{1,0:T(8,128)(2,1)S(1)} %collective-permute-done.56.d1_ref, ...), custom_call_target="tpu_custom_call" | custom-call | flops 4026531840 | bytes 20971520 | tf_op jit(solution)/shard_map/attn_bwd/pallas_call | solution.py:459
  642.5 15.1 %collective-permute-done.110 = bf16[512,1024]{1,0:T(8,128)(2,1)} collective-permute-done((bf16[512,1024]{1,0:T(8,128)(2,1)S(1)}, bf16[512,1024]{1,0:T(8,128)(2,1)}, u32[]{:S(2)}, u32[]{:S(2)}) %collective-permute-start.110) | collective-permute-done | bytes 1048608 | tf_op jit(solution)/shard_map/ppermute | solution.py:572
  664.5 13.9 %collective-permute-done.105 = bf16[512,1024]{1,0:T(8,128)(2,1)S(1)} collective-permute-done((bf16[512,1024]{1,0:T(8,128)(2,1)S(1)}, bf16[512,1024]{1,0:T(8,128)(2,1)S(1)}, u32[]{:S(2)}, u32[]{:S(2)}) %collective-permute-start.105) | collective-permute-done | bytes 1048608 | tf_op jit(solution)/shard_map/ppermute | solution.py:572
  724.0 34.7 %collective-permute-start.85 = (bf16[512,794]{0,1:T(8,128)(2,1)S(1)}, bf16[512,794]{0,1:T(8,128)(2,1)S(1)}, u32[]{:S(2)}, u32[]{:S(2)}) collective-permute-start(bf16[512,794]{0,1:T(8,128)(2,1)S(1)} %get-tuple-element.205), channel_id=1, source_target_pairs={{0,1},{3,2},{4,5},{7,6},{8,9},{11,10},{12,13},{15,14},{16,17},{19,... | collective-permute-start | bytes 2439176 | tf_op jit(solution)/shard_map/ppermute | solution.py:572
  761.6 16.1 %collective-permute-start.75 = (f32[8,1024]{1,0:T(8,128)S(1)}, f32[8,1024]{1,0:T(8,128)S(1)}, u32[]{:S(2)}, u32[]{:S(2)}) collective-permute-start(f32[8,1024]{1,0:T(8,128)S(1)} %add_select_fusion), channel_id=1, source_target_pairs={{0,1},{3,2},{4,5},{7,6},{8,9},{11,10},{12,13},{15,14},{16,17},{19,... | collective-permute-start | bytes 98312 | tf_op jit(solution)/shard_map/ppermute | solution.py:572
  778.1 15.8 %collective-permute-done.75 = f32[8,1024]{1,0:T(8,128)S(1)} collective-permute-done((f32[8,1024]{1,0:T(8,128)S(1)}, f32[8,1024]{1,0:T(8,128)S(1)}, u32[]{:S(2)}, u32[]{:S(2)}) %collective-permute-start.75) | collective-permute-done | bytes 32800 | tf_op jit(solution)/shard_map/ppermute | solution.py:572
  801.9 24.6 %collective-permute-done.77 = f32[8,1024]{1,0:T(8,128)S(1)} collective-permute-done((f32[8,1024]{1,0:T(8,128)S(1)}, f32[8,1024]{1,0:T(8,128)S(1)}, u32[]{:S(2)}, u32[]{:S(2)}) %collective-permute-start.77) | collective-permute-done | bytes 32800 | tf_op jit(solution)/shard_map/ppermute | solution.py:576
  838.6 15.9 %collective-permute-done.97 = bf16[512,1024]{1,0:T(8,128)(2,1)S(1)} collective-permute-done((bf16[512,1024]{1,0:T(8,128)(2,1)S(1)}, bf16[512,1024]{1,0:T(8,128)(2,1)S(1)}, u32[]{:S(2)}, u32[]{:S(2)}) %collective-permute-start.97) | collective-permute-done | bytes 1048608 | tf_op jit(solution)/shard_map/ppermute | solution.py:576
  855.3 21.6 %collective-permute-done.112 = bf16[512,1024]{1,0:T(8,128)(2,1)S(1)} collective-permute-done((bf16[512,1024]{1,0:T(8,128)(2,1)S(1)}, bf16[512,1024]{1,0:T(8,128)(2,1)S(1)}, u32[]{:S(2)}, u32[]{:S(2)}) %collective-permute-start.112) | collective-permute-done | bytes 1048608 | tf_op jit(solution)/shard_map/ppermute | solution.py:576
  880.7 13.7 %collective-permute-done.107 = bf16[512,1024]{1,0:T(8,128)(2,1)S(1)} collective-permute-done((bf16[512,1024]{1,0:T(8,128)(2,1)S(1)}, bf16[512,1024]{1,0:T(8,128)(2,1)S(1)}, u32[]{:S(2)}, u32[]{:S(2)}) %collective-permute-start.107) | collective-permute-done | bytes 1048608 | tf_op jit(solution)/shard_map/ppermute | solution.py:576
  901.9 16.0 %collective-permute-done.87 = bf16[512,794]{0,1:T(8,128)(2,1)S(1)} collective-permute-done((bf16[512,794]{0,1:T(8,128)(2,1)S(1)}, bf16[512,794]{0,1:T(8,128)(2,1)S(1)}, u32[]{:S(2)}, u32[]{:S(2)}) %collective-permute-start.87) | collective-permute-done | bytes 813088 | tf_op jit(solution)/shard_map/ppermute | solution.py:576
  918.0 17.5 %collective-permute-done.82 = bf16[512,794]{0,1:T(8,128)(2,1)S(1)} collective-permute-done((bf16[512,794]{0,1:T(8,128)(2,1)S(1)}, bf16[512,794]{0,1:T(8,128)(2,1)S(1)}, u32[]{:S(2)}, u32[]{:S(2)}) %collective-permute-start.82) | collective-permute-done | bytes 813088 | tf_op jit(solution)/shard_map/ppermute | solution.py:576
  939.8 14.3 %collective-permute-done.92 = bf16[560,1024]{1,0:T(8,128)(2,1)S(1)} collective-permute-done((bf16[560,1024]{1,0:T(8,128)(2,1)S(1)}, bf16[560,1024]{1,0:T(8,128)(2,1)S(1)}, u32[]{:S(2)}, u32[]{:S(2)}) %collective-permute-start.92) | collective-permute-done | bytes 1146912 | tf_op jit(solution)/shard_map/ppermute | solution.py:576
  (478 shorter events, 503.5 us)
Async XLA Ops:
  15.9 80.4 %collective-permute-start.8 = (bf16[1024,794]{0,1:T(8,128)(2,1)}, bf16[1024,794]{0,1:T(8,128)(2,1)}, u32[]{:S(2)}, u32[]{:S(2)}) collective-permute-start(bf16[1024,794]{0,1:T(8,128)(2,1)} %copy.58), channel_id=1, source_target_pairs={{0,16},{16,0},{1,17},{17,1},{2,18},{18,2},{3,19},{19,3},{4,20},{20... | collective-permute-start | bytes 4878344 | tf_op jit(solution)/shard_map/ppermute | solution.py:56
  17.9 74.4 %collective-permute-start.9 = (bf16[560,1024]{1,0:T(8,128)(2,1)}, bf16[560,1024]{1,0:T(8,128)(2,1)}, u32[]{:S(2)}, u32[]{:S(2)}) collective-permute-start(bf16[560,1024]{1,0:T(8,128)(2,1)} %bitcast.188), channel_id=1, source_target_pairs={{0,16},{16,0},{1,17},{17,1},{2,18},{18,2},{3,19},{19,3},{4,20},{20... | collective-permute-start | bytes 3440648 | tf_op jit(solution)/shard_map/ppermute | solution.py:56
  18.6 59.9 %collective-permute-start.10 = (s32[4,1280]{1,0:T(4,128)}, s32[4,1280]{1,0:T(4,128)}, u32[]{:S(2)}, u32[]{:S(2)}) collective-permute-start(s32[4,1280]{1,0:T(4,128)} %dynamic-slice_bitcast_fusion.3), channel_id=1, source_target_pairs={{0,16},{16,0},{1,17},{17,1},{2,18},{18,2},{3,19},{19,3},{4,20},{20... | collective-permute-start | bytes 61448 | tf_op jit(solution)/shard_map/ppermute | solution.py:56
  21.9 59.7 %collective-permute-start.3 = (bf16[64,1024]{1,0:T(8,128)(2,1)S(1)}, bf16[64,1024]{1,0:T(8,128)(2,1)S(1)}, u32[]{:S(2)}, u32[]{:S(2)}) collective-permute-start(bf16[64,1024]{1,0:T(8,128)(2,1)S(1)} %norm_only.3), channel_id=1, source_target_pairs={{0,8},{8,0},{4,12},{12,4},{1,9},{9,1},{5,13},{13,5},{2,10},{10,2},... | collective-permute-start | bytes 393224 | tf_op jit(solution)/shard_map/ppermute | solution.py:52
  85.0 80.1 %collective-permute-start.17 = (bf16[1024,1024]{1,0:T(8,128)(2,1)}, bf16[1024,1024]{1,0:T(8,128)(2,1)}, u32[]{:S(2)}, u32[]{:S(2)}) collective-permute-start(bf16[1024,1024]{1,0:T(8,128)(2,1)} %bitcast.24), channel_id=1, source_target_pairs={{0,16},{16,0},{1,17},{17,1},{2,18},{18,2},{3,19},{19,3},{4,20},{20... | collective-permute-start | bytes 6291464 | tf_op jit(solution)/shard_map/ppermute | solution.py:56
  345.4 147.6 %collective-permute-start.94 = (bf16[512,1024]{1,0:T(8,128)(2,1)}, bf16[512,1024]{1,0:T(8,128)(2,1)}, u32[]{:S(2)}, u32[]{:S(2)}) collective-permute-start(bf16[512,1024]{1,0:T(8,128)(2,1)} %get-tuple-element.212), channel_id=1, source_target_pairs={{0,16},{1,17},{2,18},{3,19},{4,20},{5,21},{6,22},{7,23},{8,24},{9,... | collective-permute-start | bytes 3145736 | tf_op jit(solution)/shard_map/ppermute | solution.py:759
  349.7 144.6 %collective-permute-start.99 = (bf16[512,1024]{1,0:T(8,128)(2,1)}, bf16[512,1024]{1,0:T(8,128)(2,1)}, u32[]{:S(2)}, u32[]{:S(2)}) collective-permute-start(bf16[512,1024]{1,0:T(8,128)(2,1)} %get-tuple-element.213), channel_id=1, source_target_pairs={{0,16},{1,17},{2,18},{3,19},{4,20},{5,21},{6,22},{7,23},{8,24},{9,... | collective-permute-start | bytes 3145736 | tf_op jit(solution)/shard_map/ppermute | solution.py:759
  356.7 48.4 %collective-permute-start.37 = (bf16[256,1024]{1,0:T(8,128)(2,1)S(1)}, bf16[256,1024]{1,0:T(8,128)(2,1)S(1)}, u32[]{:S(2)}, u32[]{:S(2)}) collective-permute-start(bf16[256,1024]{1,0:T(8,128)(2,1)S(1)} %broadcast_select_fusion.16), channel_id=1, source_target_pairs={{0,16},{16,0},{1,17},{17,1},{2,18},{18,2},{3,19},{19,3},{4,20},{20... | collective-permute-start | bytes 1572872 | tf_op jit(solution)/shard_map/ppermute | solution.py:56
  522.2 63.0 %collective-permute-start.108 = (bf16[512,1024]{1,0:T(8,128)(2,1)}, bf16[512,1024]{1,0:T(8,128)(2,1)}, u32[]{:S(2)}, u32[]{:S(2)}) collective-permute-start(bf16[512,1024]{1,0:T(8,128)(2,1)} %get-tuple-element.211), channel_id=1, source_target_pairs={{16,0},{17,1},{18,2},{19,3},{20,4},{21,5},{22,6},{23,7},{24,8},{25... | collective-permute-start | bytes 3145736 | tf_op jit(solution)/shard_map/ppermute | solution.py:760
  541.0 52.5 %collective-permute-start.56 = (bf16[256,1024]{1,0:T(8,128)(2,1)S(1)}, bf16[256,1024]{1,0:T(8,128)(2,1)S(1)}, u32[]{:S(2)}, u32[]{:S(2)}) collective-permute-start(bf16[256,1024]{1,0:T(8,128)(2,1)S(1)} %get-tuple-element.100.d0_ref), channel_id=1, source_target_pairs={{0,4},{4,0},{8,12},{12,8},{1,5},{5,1},{9,13},{13,9},{2,6},{6,2},{1... | collective-permute-start | bytes 1572872 | tf_op jit(solution)/shard_map/ppermute | solution.py:48
  541.0 54.8 %collective-permute-start.58 = (bf16[256,1024]{1,0:T(8,128)(2,1)S(1)}, bf16[256,1024]{1,0:T(8,128)(2,1)S(1)}, u32[]{:S(2)}, u32[]{:S(2)}) collective-permute-start(bf16[256,1024]{1,0:T(8,128)(2,1)S(1)} %collective-permute-done.57.d2_ref), channel_id=1, source_target_pairs={{0,4},{4,0},{8,12},{12,8},{1,5},{5,1},{9,13},{13,9},{2,6},{6,2},{1... | collective-permute-start | bytes 1572872 | tf_op jit(solution)/shard_map/ppermute | solution.py:48
  547.0 94.9 %collective-permute-start.79 = (bf16[512,794]{0,1:T(8,128)(2,1)}, bf16[512,794]{0,1:T(8,128)(2,1)}, u32[]{:S(2)}, u32[]{:S(2)}) collective-permute-start(bf16[512,794]{0,1:T(8,128)(2,1)} %get-tuple-element.248), channel_id=1, source_target_pairs={{0,16},{1,17},{2,18},{3,19},{4,20},{5,21},{6,22},{7,23},{8,24},{9,... | collective-permute-start | bytes 2439176 | tf_op jit(solution)/shard_map/ppermute | solution.py:759
  563.4 98.4 %collective-permute-start.84 = (bf16[512,794]{0,1:T(8,128)(2,1)}, bf16[512,794]{0,1:T(8,128)(2,1)}, u32[]{:S(2)}, u32[]{:S(2)}) collective-permute-start(bf16[512,794]{0,1:T(8,128)(2,1)} %get-tuple-element.249), channel_id=1, source_target_pairs={{0,16},{1,17},{2,18},{3,19},{4,20},{5,21},{6,22},{7,23},{8,24},{9,... | collective-permute-start | bytes 2439176 | tf_op jit(solution)/shard_map/ppermute | solution.py:759
  595.8 61.8 %collective-permute-start.110 = (bf16[512,1024]{1,0:T(8,128)(2,1)S(1)}, bf16[512,1024]{1,0:T(8,128)(2,1)}, u32[]{:S(2)}, u32[]{:S(2)}) collective-permute-start(bf16[512,1024]{1,0:T(8,128)(2,1)S(1)} %get-tuple-element.195), channel_id=1, source_target_pairs={{0,1},{3,2},{4,5},{7,6},{8,9},{11,10},{12,13},{15,14},{16,17},{19,... | collective-permute-start | bytes 3145736 | tf_op jit(solution)/shard_map/ppermute | solution.py:572
  620.3 58.1 %collective-permute-start.105 = (bf16[512,1024]{1,0:T(8,128)(2,1)S(1)}, bf16[512,1024]{1,0:T(8,128)(2,1)S(1)}, u32[]{:S(2)}, u32[]{:S(2)}) collective-permute-start(bf16[512,1024]{1,0:T(8,128)(2,1)S(1)} %get-tuple-element.194), channel_id=1, source_target_pairs={{0,1},{3,2},{4,5},{7,6},{8,9},{11,10},{12,13},{15,14},{16,17},{19,... | collective-permute-start | bytes 3145736 | tf_op jit(solution)/shard_map/ppermute | solution.py:572
  682.3 114.7 %collective-permute-start.89 = (bf16[560,1024]{1,0:T(8,128)(2,1)S(1)}, bf16[560,1024]{1,0:T(8,128)(2,1)}, u32[]{:S(2)}, u32[]{:S(2)}) collective-permute-start(bf16[560,1024]{1,0:T(8,128)(2,1)S(1)} %bitcast.181), channel_id=1, source_target_pairs={{0,16},{1,17},{2,18},{3,19},{4,20},{5,21},{6,22},{7,23},{8,24},{9,... | collective-permute-start | bytes 3440648 | tf_op jit(solution)/shard_map/ppermute | solution.py:759
  706.4 92.0 %collective-permute-start.88 = (bf16[560,1024]{1,0:T(8,128)(2,1)S(1)}, bf16[560,1024]{1,0:T(8,128)(2,1)S(1)}, u32[]{:S(2)}, u32[]{:S(2)}) collective-permute-start(bf16[560,1024]{1,0:T(8,128)(2,1)S(1)} %bitcast.182), channel_id=1, source_target_pairs={{16,0},{17,1},{18,2},{19,3},{20,4},{21,5},{22,6},{23,7},{24,8},{25... | collective-permute-start | bytes 3440648 | tf_op jit(solution)/shard_map/ppermute | solution.py:760
  707.7 53.9 %collective-permute-start.106 = (bf16[512,1024]{1,0:T(8,128)(2,1)S(1)}, bf16[512,1024]{1,0:T(8,128)(2,1)S(1)}, u32[]{:S(2)}, u32[]{:S(2)}) collective-permute-start(bf16[512,1024]{1,0:T(8,128)(2,1)S(1)} %add_convert_fusion.9), channel_id=1, source_target_pairs={{1,2},{2,1},{5,6},{6,5},{9,10},{10,9},{13,14},{14,13},{17,18},{18,... | collective-permute-start | bytes 3145736 | tf_op jit(solution)/shard_map/ppermute | solution.py:574
  724.0 106.9 %collective-permute-start.85 = (bf16[512,794]{0,1:T(8,128)(2,1)S(1)}, bf16[512,794]{0,1:T(8,128)(2,1)S(1)}, u32[]{:S(2)}, u32[]{:S(2)}) collective-permute-start(bf16[512,794]{0,1:T(8,128)(2,1)S(1)} %get-tuple-element.205), channel_id=1, source_target_pairs={{0,1},{3,2},{4,5},{7,6},{8,9},{11,10},{12,13},{15,14},{16,17},{19,... | collective-permute-start | bytes 2439176 | tf_op jit(solution)/shard_map/ppermute | solution.py:572
  758.7 74.0 %collective-permute-start.80 = (bf16[512,794]{0,1:T(8,128)(2,1)S(1)}, bf16[512,794]{0,1:T(8,128)(2,1)S(1)}, u32[]{:S(2)}, u32[]{:S(2)}) collective-permute-start(bf16[512,794]{0,1:T(8,128)(2,1)S(1)} %get-tuple-element.204), channel_id=1, source_target_pairs={{0,1},{3,2},{4,5},{7,6},{8,9},{11,10},{12,13},{15,14},{16,17},{19,... | collective-permute-start | bytes 2439176 | tf_op jit(solution)/shard_map/ppermute | solution.py:572
  828.5 48.5 %collective-permute-start.112 = (bf16[512,1024]{1,0:T(8,128)(2,1)S(1)}, bf16[512,1024]{1,0:T(8,128)(2,1)S(1)}, u32[]{:S(2)}, u32[]{:S(2)}) collective-permute-start(bf16[512,1024]{1,0:T(8,128)(2,1)S(1)} %add_convert_fusion.4), channel_id=1, source_target_pairs={{1,0},{2,3},{5,4},{6,7},{9,8},{10,11},{13,12},{14,15},{17,16},{18,... | collective-permute-start | bytes 3145736 | tf_op jit(solution)/shard_map/ppermute | solution.py:576
  830.9 63.5 %collective-permute-start.107 = (bf16[512,1024]{1,0:T(8,128)(2,1)S(1)}, bf16[512,1024]{1,0:T(8,128)(2,1)S(1)}, u32[]{:S(2)}, u32[]{:S(2)}) collective-permute-start(bf16[512,1024]{1,0:T(8,128)(2,1)S(1)} %add_convert_fusion.8), channel_id=1, source_target_pairs={{1,0},{2,3},{5,4},{6,7},{9,8},{10,11},{13,12},{14,15},{17,16},{18,... | collective-permute-start | bytes 3145736 | tf_op jit(solution)/shard_map/ppermute | solution.py:576
  837.8 56.8 %collective-permute-start.86 = (bf16[512,794]{0,1:T(8,128)(2,1)S(1)}, bf16[512,794]{0,1:T(8,128)(2,1)S(1)}, u32[]{:S(2)}, u32[]{:S(2)}) collective-permute-start(bf16[512,794]{0,1:T(8,128)(2,1)S(1)} %add_convert_fusion.21), channel_id=1, source_target_pairs={{1,2},{2,1},{5,6},{6,5},{9,10},{10,9},{13,14},{14,13},{17,18},{18,... | collective-permute-start | bytes 2439176 | tf_op jit(solution)/shard_map/ppermute | solution.py:574
  900.6 53.6 %collective-permute-start.92 = (bf16[560,1024]{1,0:T(8,128)(2,1)S(1)}, bf16[560,1024]{1,0:T(8,128)(2,1)S(1)}, u32[]{:S(2)}, u32[]{:S(2)}) collective-permute-start(bf16[560,1024]{1,0:T(8,128)(2,1)S(1)} %add_convert_fusion), channel_id=1, source_target_pairs={{1,0},{2,3},{5,4},{6,7},{9,8},{10,11},{13,12},{14,15},{17,16},{18,... | collective-permute-start | bytes 3440648 | tf_op jit(solution)/shard_map/ppermute | solution.py:576
  (136 other events, 2349.1 us)

commit v2 on v1

--- a/solution.py
+++ b/solution.py
@@ -10,6 +10,8 @@
 norm_eps = 1e-05
 masked_score = -1e30
 lanes = 128
+out_lane = 8
+log_lane = 16
 bf16 = jnp.bfloat16
 f32 = jnp.float32
 gelu_c = 0.7978845608028654
@@ -63,11 +65,15 @@
     return [own, from_core, from_chip, from_both]
 
 
-def scatter_slots(parts):
+def scatter_slots(parts, beside=None):
     from_core_far = to_core(parts[3])
     from_core = to_core(parts[1])
     far = (parts[2].astype(f32) + from_core_far.astype(f32)).astype(bf16)
-    return parts[0], from_core, to_chip(far)
+    from_chip = to_chip(far)
+    if beside is None:
+        return parts[0], from_core, from_chip
+    from_chip, beside = lax.optimization_barrier((from_chip, beside))
+    return (parts[0], from_core, from_chip), beside
 
 
 def norm_rows(x, gain, shift):
@@ -174,19 +180,50 @@
             target[...] = ref[...]
 
 
+def store_slot(slot, refs, block):
+    for number, ref in enumerate(refs):
+
+        @pl.when(slot == number)
+        def _(ref=ref):
+            ref[...] = block
+
+
+def fill_experts(target, source, experts, width):
+    for j in range(experts):
+        target[j * lanes : j * lanes + width, :] = source[j * width : (j + 1) * width, :]
+        target[j * lanes + width : (j + 1) * lanes, :] = jnp.zeros((lanes - width, target.shape[1]), bf16)
+
+
+def fill_weights(w_s, wo_s, wv_ref, wk_ref, wo_ref, experts, width):
+    fill_experts(w_s, wv_ref, experts, width)
+    fill_experts(wo_s, wo_ref, experts, width)
+    start = 0
+    for place, rows in ((experts + 1, width), (experts + 2, width), (experts, 2 * out_lane)):
+        w_s[place * lanes : place * lanes + rows, :] = wk_ref[start : start + rows, :]
+        w_s[place * lanes + rows : (place + 1) * lanes, :] = jnp.zeros((lanes - rows, w_s.shape[1]), bf16)
+        start += rows
+
+
 def attn_fwd_kernel(
     experts,
     head_width,
     me_ref,
-    mem_ref,
+    m0_ref,
+    m1_ref,
+    m2_ref,
+    m3_ref,
     p0_ref,
     p1_ref,
     p2_ref,
     p3_ref,
-    w_ref,
+    wv_ref,
+    wk_ref,
     wo_ref,
     mask_ref,
-    out_ref,
+    o0_ref,
+    o1_ref,
+    o2_ref,
+    o3_ref,
     normed_ref,
     q_ref,
     k_ref,
@@ -199,6 +236,8 @@
     k_s,
     v_s,
     mask_s,
+    w_s,
+    wo_s,
 ):
     step = pl.program_id(0)
     me = me_ref[0]
@@ -208,8 +247,9 @@
 
     @pl.when(step == 0)
     def _():
-        rows_s[...] = mem_ref[...]
-        for slot in range(4):
+        fill_weights(w_s, wo_s, wv_ref, wk_ref, wo_ref, experts, head_width)
+        for slot, mem_ref in enumerate((m0_ref, m1_ref, m2_ref, m3_ref)):
+            rows_s[slot * quarter : (slot + 1) * quarter, :] = mem_ref[...]
             start = pl.multiple_of((me ^ slot) * quarter, quarter)
             mask_s[slot * quarter : (slot + 1) * quarter, :] = mask_ref[pl.ds(start, quarter), :]
 
@@ -220,7 +260,7 @@
 
     x = rows_s[...]
     normed_ref[...] = x
-    proj = dot(x, w_ref[...])
+    proj = dot_t(x, w_s[...])
     gate = jax.nn.sigmoid(proj[:, wide : wide + lanes]) * mask_s[...]
     value = jnp.zeros((block, lanes), f32)
     for j in range(experts):
@@ -258,15 +298,15 @@
             attended = dot(probs, v_s[0:span, :])
             att_ref[...] = attended
             lane = lax.broadcasted_iota(jnp.int32, (block, lanes), 1)
-            gate_ref[...] = jnp.where(lane == 2 * experts, top + jnp.log(total), gate)
+            gate_ref[...] = jnp.where(lane == log_lane, top + jnp.log(total), gate)
             mixed = jnp.concatenate(
-                [(gate[:, experts + j : experts + j + 1] * attended).astype(bf16) for j in range(experts)], axis=1
+                [(gate[:, out_lane + j : out_lane + j + 1] * attended).astype(bf16) for j in range(experts)], axis=1
             )
             mixed_ref[...] = mixed
-            out_ref[0] = dot(mixed, wo_ref[...]).astype(bf16)
-
-
-def attn_fwd(me, mem, slots, w, wo, mask, experts, head_width):
+            store_slot((count - 1) ^ me, (o0_ref, o1_ref, o2_ref, o3_ref), dot(mixed, wo_s[...]).astype(bf16))
+
+
+def attn_fwd(me, mems, slots, w, mask, experts, head_width):
     block, width = slots[0].shape
     total = 5 * block
     wide = experts * lanes
@@ -276,10 +316,12 @@
     grid_spec = pltpu.PrefetchScalarGridSpec(
         num_scalar_prefetch=1,
         grid=(5,),
-        in_specs=[whole_spec((block, width))] * 5
-        + [whole_spec(w.shape), whole_spec(wo.shape), whole_spec(mask.shape)],
+        in_specs=[whole_spec((block // 4, width))] * 4
+        + [whole_spec((block, width))] * 4
+        + [whole_spec(a.shape) for a in w]
+        + [whole_spec(mask.shape)],
         out_specs=[
-            pl.BlockSpec((1, block, width), lambda i, me_ref: (jnp.maximum(i - 1, 0) ^ me_ref[0], 0, 0)),
+            *[whole_spec((block, width))] * 4,
             pl.BlockSpec((block, width), every),
             pl.BlockSpec((block, lanes), every),
             pl.BlockSpec((block, lanes), every),
@@ -294,13 +336,15 @@
             pltpu.VMEM((total, lanes), bf16),
             pltpu.VMEM((total, lanes), bf16),
             pltpu.VMEM((block, lanes), f32),
+            pltpu.VMEM((wide + 3 * lanes, width), bf16),
+            pltpu.VMEM((wide, width), bf16),
         ],
     )
     return pl.pallas_call(
         functools.partial(attn_fwd_kernel, experts, head_width),
         grid_spec=grid_spec,
         out_shape=(
-            jax.ShapeDtypeStruct((4, block, width), bf16),
+            *[shapes(block, width, bf16)] * 4,
             shapes(total, width, bf16),
             shapes(total, lanes, bf16),
             shapes(total, lanes, bf16),
@@ -311,9 +355,9 @@
             shapes(4 * block, wide, bf16),
         ),
         compiler_params=params(dimension_semantics=("arbitrary",)),
-        cost_estimate=cost(2 * total * width * w.shape[1] + 2 * 4 * block * wide * width, 20 * 1024 * 1024, total * total),
+        cost_estimate=cost(4 * total * width * wide, 16 * 1024 * 1024, total * total),
         name="attn_fwd",
-    )(me, mem, *slots, w, wo, mask)
+    )(me, *mems, *slots, *w, mask)
 
 
 def attn_bwd_kernel(
@@ -324,7 +368,8 @@
     d1_ref,
     d2_ref,
     d3_ref,
-    w_ref,
+    wv_ref,
+    wk_ref,
     wo_ref,
     q_ref,
     k_ref,
@@ -332,7 +377,10 @@
     ev_ref,
     gate_ref,
     att_ref,
-    ngs_ref,
+    n0_ref,
+    n1_ref,
+    n2_ref,
+    n3_ref,
     ngm_ref,
     dproj_ref,
     da_ref,
@@ -341,6 +389,8 @@
     dv_s,
     dq_s,
     dlog_s,
+    w_s,
+    wo_s,
 ):
     step = pl.program_id(0)
     me = me_ref[0]
@@ -353,6 +403,7 @@
 
     @pl.when(step == 0)
     def _():
+        fill_weights(w_s, wo_s, wv_ref, wk_ref, wo_ref, experts, head_width)
         dk_s[...] = jnp.zeros_like(dk_s)
         dv_s[...] = jnp.zeros_like(dv_s)
 
@@ -368,19 +419,19 @@
             pick_slot((count - 1) ^ me, (d0_ref, d1_ref, d2_ref, d3_ref), rows_s)
             rows = rows_s[...]
             da_ref[...] = rows
-            mixed_grad = dot_t(rows, wo_ref[...])
+            mixed_grad = dot_t(rows, wo_s[...])
             attended = att_ref[...]
             att_grad = jnp.zeros((block, lanes), f32)
             logit_grad = jnp.zeros((block, lanes), f32)
             for j in range(experts):
                 part = mixed_grad[:, j * lanes : (j + 1) * lanes]
-                att_grad = att_grad + gate[:, experts + j : experts + j + 1] * part
+                att_grad = att_grad + gate[:, out_lane + j : out_lane + j + 1] * part
                 inner = jnp.sum(part * attended, axis=-1, keepdims=True)
-                logit_grad = jnp.where(lane == experts + j, inner, logit_grad)
+                logit_grad = jnp.where(lane == out_lane + j, inner, logit_grad)
             dlog_s[...] = logit_grad
             grad_low = att_grad.astype(bf16)
             row_sum = jnp.sum(att_grad * attended, axis=-1, keepdims=True)
-            log_total = gate[:, 2 * experts : 2 * experts + 1]
+            log_total = gate[:, log_lane : log_lane + 1]
             span = (count + 1) * block
             queries = q_ref[...]
             keys = k_ref[0:span, :]
@@ -404,24 +455,24 @@
         parts.append((gate[:, j : j + 1] * value_grad).astype(bf16))
         inner = jnp.sum(value_grad * ev_ref[:, j * lanes : (j + 1) * lanes].astype(f32), axis=-1, keepdims=True)
         logit_grad = jnp.where(lane == j, inner, logit_grad)
-    slope = jnp.where(lane < 2 * experts, gate * (1.0 - gate), 0.0)
+    slope = jnp.where(lane < log_lane, gate * (1.0 - gate), 0.0)
     parts.append((logit_grad * slope).astype(bf16))
     parts.append((dk_s[pl.ds(start, block), :] * scale).astype(bf16))
     parts.append(dq_s[...].astype(bf16))
     dproj = jnp.concatenate(parts, axis=1)
     dproj_ref[...] = dproj
-    normed_grad = dot_t(dproj, w_ref[...]).astype(bf16)
+    normed_grad = dot(dproj, w_s[...]).astype(bf16)
 
     @pl.when(here > 0)
     def _():
-        ngs_ref[0] = normed_grad
+        store_slot((here - 1) ^ me, (n0_ref, n1_ref, n2_ref, n3_ref), normed_grad)
 
     @pl.when(here == 0)
     def _():
         ngm_ref[...] = normed_grad
 
 
-def attn_bwd(me, slots, w, wo, saved, experts, head_width):
+def attn_bwd(me, slots, w, saved, experts, head_width):
     q, k, v, ev, gate, att = saved
     block, width = slots[0].shape
     total = 5 * block
@@ -432,9 +483,8 @@
         num_scalar_prefetch=1,
         grid=(5,),
         in_specs=[whole_spec((block, width))] * 4
+        + [whole_spec(a.shape) for a in w]
         + [
-            whole_spec(w.shape),
-            whole_spec(wo.shape),
             pl.BlockSpec((block, lanes), back),
             whole_spec(k.shape),
             whole_spec(v.shape),
@@ -443,9 +493,8 @@
             pl.BlockSpec((block, lanes), later),
         ],
         out_specs=[
-            pl.BlockSpec((1, block, width), lambda i, me_ref: (jnp.maximum(3 - i, 0) ^ me_ref[0], 0, 0)),
-            whole_spec((block, width)),
-            pl.BlockSpec((block, w.shape[1]), back),
+            *[whole_spec((block, width))] * 5,
+            pl.BlockSpec((block, wide + 3 * lanes), back),
             pl.BlockSpec((block, width), later),
         ],
         scratch_shapes=[
@@ -454,127 +503,149 @@
             pltpu.VMEM((total, lanes), f32),
             pltpu.VMEM((block, lanes), f32),
             pltpu.VMEM((block, lanes), f32),
+            pltpu.VMEM((wide + 3 * lanes, width), bf16),
+            pltpu.VMEM((wide, width), bf16),
         ],
     )
     return pl.pallas_call(
         functools.partial(attn_bwd_kernel, experts, head_width),
         grid_spec=grid_spec,
         out_shape=(
-            jax.ShapeDtypeStruct((4, block, width), bf16),
-            jax.ShapeDtypeStruct((block, width), bf16),
-            jax.ShapeDtypeStruct((total, w.shape[1]), bf16),
+            *[jax.ShapeDtypeStruct((block, width), bf16)] * 5,
+            jax.ShapeDtypeStruct((total, wide + 3 * lanes), bf16),
             jax.ShapeDtypeStruct((4 * block, width), bf16),
         ),
         compiler_params=params(dimension_semantics=("arbitrary",)),
-        cost_estimate=cost(2 * total * width * w.shape[1] + 2 * 4 * block * wide * width, 20 * 1024 * 1024, total * total),
+        cost_estimate=cost(4 * total * width * wide, 16 * 1024 * 1024, total * total),
         name="attn_bwd",
-    )(me, *slots, w, wo, q, k, v, ev, gate, att)
-
-
-def ffn_fwd_kernel(p0_ref, p1_ref, p2_ref, p3_ref, wu_ref, bu_ref, wd_ref, out_ref, rows_ref, upper_ref, active_ref, rows_s):
-    pick_slot(pl.program_id(0), (p0_ref, p1_ref, p2_ref, p3_ref), rows_s)
-    x = rows_s[...]
-    rows_ref[...] = x
-    upper = dot(x, wu_ref[...]) + bu_ref[...]
+    )(me, *slots, *w, q, k, v, ev, gate, att)
+
+
+def ffn_fwd_kernel(a_ref, b_ref, wu_ref, bu_ref, wd_ref, *refs):
+    oa_ref, ob_ref, rows_ref, upper_ref, active_ref = refs[-5:]
+    half = a_ref.shape[0]
+    rows_ref[0:half, :] = a_ref[...]
+    rows_ref[half:, :] = b_ref[...]
+    upper = dot(rows_ref[...], wu_ref[...]) + bu_ref[...]
     upper_ref[...] = upper.astype(bf16)
-    active = jax.nn.gelu(upper).astype(bf16)
-    active_ref[...] = active
-    out_ref[0] = dot(active, wd_ref[...]).astype(bf16)
-
-
-def ffn_fwd(slots, wu, bu, wd):
-    block, width = slots[0].shape
+    active_ref[...] = jax.nn.gelu(upper).astype(bf16)
+    out = dot(active_ref[...], wd_ref[...]).astype(bf16)
+    oa_ref[...] = out[0:half]
+    ob_ref[...] = out[half:]
+
+
+def ffn_fwd(pair, number, wu, bu, wd, earlier):
+    block, width = pair[0].shape
     hidden = wu.shape[1]
-    rows = lambda i: (i, 0)
+    here = lambda i: (number, 0)
+    specs = [whole_spec((block, width))] * 2 + [whole_spec(wu.shape), whole_spec(bu.shape), whole_spec(wd.shape)]
     return pl.pallas_call(
         ffn_fwd_kernel,
-        grid=(4,),
-        in_specs=[whole_spec((block, width))] * 4 + [whole_spec(wu.shape), whole_spec(bu.shape), whole_spec(wd.shape)],
-        out_specs=[
-            pl.BlockSpec((1, block, width), lambda i: (i, 0, 0)),
-            pl.BlockSpec((block, width), rows),
-            pl.BlockSpec((block, hidden), rows),
-            pl.BlockSpec((block, hidden), rows),
-        ],
+        grid=(1,),
+        in_specs=specs + [pl.BlockSpec(memory_space=pl.ANY)] * len(earlier),
+        out_specs=[whole_spec((block, width))] * 2
+        + [pl.BlockSpec((2 * block, width), here)]
+        + [pl.BlockSpec((2 * block, hidden), here)] * 2,
         out_shape=(
-            jax.ShapeDtypeStruct((4, block, width), bf16),
+            jax.ShapeDtypeStruct((block, width), bf16),
+            jax.ShapeDtypeStruct((block, width), bf16),
             jax.ShapeDtypeStruct((4 * block, width), bf16),
             jax.ShapeDtypeStruct((4 * block, hidden), bf16),
             jax.ShapeDtypeStruct((4 * block, hidden), bf16),
         ),
-        scratch_shapes=[pltpu.VMEM((block, width), bf16)],
-        compiler_params=params(dimension_semantics=("arbitrary",)),
-        cost_estimate=cost(16 * block * width * hidden, 14 * 1024 * 1024, 4 * block * hidden),
+        input_output_aliases={5 + i: 2 + i for i in range(len(earlier))},
+        compiler_params=params(),
+        cost_estimate=cost(8 * block * width * hidden, 9 * 1024 * 1024, 2 * block * hidden),
         name="ffn_fwd",
-    )(*slots, wu, bu, wd)
-
-
-def ffn_bwd_kernel(
-    g0_ref, g1_ref, g2_ref, g3_ref, upper_ref, wd_ref, wu_ref, out_ref, rows_ref, ug_ref, bias_ref, rows_s
-):
-    step = pl.program_id(0)
-    pick_slot(step, (g0_ref, g1_ref, g2_ref, g3_ref), rows_s)
-    g = rows_s[...]
-    rows_ref[...] = g
-    active_grad = dot_t(g, wd_ref[...])
+    )(*pair, wu, bu, wd, *earlier)
+
+
+def ffn_bwd_kernel(a_ref, b_ref, upper_ref, wd_ref, wu_ref, *refs):
+    oa_ref, ob_ref, bias_ref, rows_ref, ug_ref = refs[-5:]
+    half = a_ref.shape[0]
+    rows_ref[0:half, :] = a_ref[...]
+    rows_ref[half:, :] = b_ref[...]
+    active_grad = dot_t(rows_ref[...], wd_ref[...])
     u = upper_ref[...].astype(f32)
     square = u * u
     t = jnp.tanh(gelu_c * u * (1.0 + gelu_a * square))
     slope = 0.5 * (1.0 + t) + 0.5 * gelu_c * u * (1.0 - t * t) * (1.0 + 3.0 * gelu_a * square)
     upper_grad = (active_grad * slope).astype(bf16)
     ug_ref[...] = upper_grad
-    sums = jnp.sum(upper_grad.astype(f32), axis=0, keepdims=True)
-
-    @pl.when(step == 0)
-    def _():
-        bias_ref[...] = sums
-
-    @pl.when(step > 0)
-    def _():
-        bias_ref[...] += sums
-
-    out_ref[0] = dot_t(upper_grad, wu_ref[...]).astype(bf16)
-
-
-def ffn_bwd(slots, upper, wd, wu):
-    block, width = slots[0].shape
+    bias_ref[...] = jnp.sum(upper_grad.astype(f32), axis=0, keepdims=True)
+    out = dot_t(ug_ref[...], wu_ref[...]).astype(bf16)
+    oa_ref[...] = out[0:half]
+    ob_ref[...] = out[half:]
+
+
+def ffn_bwd(pair, number, upper, wd, wu, earlier):
+    block, width = pair[0].shape
     hidden = wu.shape[1]
-    rows = lambda i: (i, 0)
+    here = lambda i: (number, 0)
+    specs = [whole_spec((block, width))] * 2
+    specs += [pl.BlockSpec((2 * block, hidden), here), whole_spec(wd.shape), whole_spec(wu.shape)]
     return pl.pallas_call(
         ffn_bwd_kernel,
-        grid=(4,),
-        in_specs=[whole_spec((block, width))] * 4
-        + [pl.BlockSpec((block, hidden), rows), whole_spec(wd.shape), whole_spec(wu.shape)],
-        out_specs=[
-            pl.BlockSpec((1, block, width), lambda i: (i, 0, 0)),
-            pl.BlockSpec((block, width), rows),
-            pl.BlockSpec((block, hidden), rows),
-            whole_spec((1, hidden)),
-        ],
+        grid=(1,),
+        in_specs=specs + [pl.BlockSpec(memory_space=pl.ANY)] * len(earlier),
+        out_specs=[whole_spec((block, width))] * 2
+        + [whole_spec((1, hidden)), pl.BlockSpec((2 * block, width), here), pl.BlockSpec((2 * block, hidden), here)],
         out_shape=(
-            jax.ShapeDtypeStruct((4, block, width), bf16),
+            jax.ShapeDtypeStruct((block, width), bf16),
+            jax.ShapeDtypeStruct((block, width), bf16),
+            jax.ShapeDtypeStruct((1, hidden), f32),
             jax.ShapeDtypeStruct((4 * block, width), bf16),
             jax.ShapeDtypeStruct((4 * block, hidden), bf16),
-            jax.ShapeDtypeStruct((1, hidden), f32),
         ),
-        scratch_shapes=[pltpu.VMEM((block, width), bf16)],
-        compiler_params=params(dimension_semantics=("arbitrary",)),
-        cost_estimate=cost(16 * block * width * hidden, 14 * 1024 * 1024, 4 * block * hidden),
+        input_output_aliases={5 + i: 3 + i for i in range(len(earlier))},
+        compiler_params=params(),
+        cost_estimate=cost(8 * block * width * hidden, 9 * 1024 * 1024, 2 * block * hidden),
         name="ffn_bwd",
-    )(*slots, upper, wd, wu)
-
-
-def sum_dp(part):
-    if lax.axis_size("dp") != 4:
-        return lax.psum(part, "dp").astype(f32)
-    kind = part.dtype
-    place = lax.axis_index("dp")
-    inward = lax.ppermute(part, "dp", [(0, 1), (3, 2)])
-    half = (part.astype(f32) + inward.astype(f32)).astype(kind)
-    other = lax.ppermute(half, "dp", [(1, 2), (2, 1)])
-    full = (half.astype(f32) + other.astype(f32)).astype(kind)
-    outward = lax.ppermute(full, "dp", [(1, 0), (2, 3)])
-    return jnp.where((place == 1) | (place == 2), full, outward).astype(f32)
+    )(*pair, upper, wd, wu, *earlier)
+
+
+def plus(a, b):
+    return jax.tree.map(lambda one, two: (one.astype(f32) + two.astype(f32)).astype(one.dtype), a, b)
+
+
+def move(a, axis, pairs):
+    return jax.tree.map(lambda one: lax.ppermute(one, axis, pairs), a)
+
+
+def after(a, token):
+    return lax.optimization_barrier((a, token))[0]
+
+
+class ChunkSums:
+    def __init__(self):
+        self.chunks = []
+        self.token = None
+        self.direct = lax.axis_size("dp") != 4
+        place = lax.axis_index("dp")
+        self.middle = (place == 1) | (place == 2)
+
+    def add(self, own, got):
+        self.chunks.append(dict(own=own, moving=got, step=0))
+
+    def turn(self, number):
+        chunk = self.chunks[number]
+        got = chunk["moving"] if self.token is None else after(chunk["moving"], self.token)
+        step = chunk["step"]
+        chunk["step"] += 1
+        if self.direct:
+            if step == 0:
+                chunk["end"] = lax.psum(plus(chunk["own"], got), "dp")
+            return
+        if step == 3:
+            chunk["end"] = jax.tree.map(lambda full, far: jnp.where(self.middle, full, far), chunk["own"], got)
+            return
+        total = plus(chunk["own"], got)
+        pairs = ([(0, 1), (3, 2)], [(1, 2), (2, 1)], [(1, 0), (2, 3)])[step]
+        chunk["own"], chunk["moving"] = total, move(total, "dp", pairs)
+        self.token = total
+
+    def before(self, a):
+        return a if self.token is None else after(a, self.token)
 
 
 def cut(a, pieces):
@@ -582,29 +653,38 @@
     return [a[i * rows : (i + 1) * rows] for i in range(pieces)]
 
 
-def pad_lanes(a, axis, count, width):
-    shape = a.shape[:axis] + (count, width) + a.shape[axis + 1 :]
-    pads = [(0, 0)] * len(shape)
-    pads[axis + 1] = (0, lanes - width)
-    padded = jnp.pad(a.reshape(shape), pads)
-    return padded.reshape(a.shape[:axis] + (count * lanes,) + a.shape[axis + 1 :])
-
-
-def spread(pack, experts, width):
-    ev = experts * width
-    routers = jnp.pad(pack[:, ev + 2 * width :], ((0, 0), (0, lanes - 2 * experts)))
-    key = jnp.pad(pack[:, ev : ev + width], ((0, 0), (0, lanes - width)))
-    query = jnp.pad(pack[:, ev + width : ev + 2 * width], ((0, 0), (0, lanes - width)))
-    return jnp.concatenate([pad_lanes(pack[:, :ev], 1, experts, width), routers, key, query], axis=1)
+def padded_rows(a, rows):
+    return jnp.pad(a, ((0, rows - a.shape[0]), (0, 0)))
+
+
+def squeeze_out(wide, experts, width):
+    return jnp.concatenate([wide[j * lanes : j * lanes + width] for j in range(experts)], axis=0)
 
 
 def squeeze(wide, experts, width):
     base = experts * lanes
-    parts = [wide[:, j * lanes : j * lanes + width] for j in range(experts)]
-    parts.append(wide[:, base + lanes : base + lanes + width])
-    parts.append(wide[:, base + 2 * lanes : base + 2 * lanes + width])
-    parts.append(wide[:, base : base + 2 * experts])
-    return jnp.concatenate(parts, axis=1)
+    parts = [wide[j * lanes : j * lanes + width] for j in range(experts)]
+    parts.append(wide[base + lanes : base + lanes + width])
+    parts.append(wide[base + 2 * lanes : base + 2 * lanes + width])
+    parts.append(wide[base : base + 2 * out_lane])
+    return jnp.concatenate(parts, axis=0)
+
+
+def swap_weights(weights):
+    size = lax.axis_size("dp")
+    if size % 2:
+        return [swap_section(a) for a in weights]
+    odd = lax.axis_index("dp") % 2
+    results = []
+    token = None
+    for a in weights:
+        rows = a.shape[0] // 2
+        half = lax.dynamic_slice_in_dim(a if token is None else after(a, token), odd * rows, rows, 0)
+        token = half
+        got = swap_section(half)
+        other = lax.ppermute(got, "dp", [(i, i ^ 1) for i in range(size)])
+        results.append(jnp.concatenate([jnp.where(odd == 0, got, other), jnp.where(odd == 0, other, got)], axis=0))
+    return results
 
 
 def route_mask(value_ids, out_ids, experts, memory_len):
@@ -613,7 +693,7 @@
     hit = jnp.zeros((value_ids.shape[1], lanes), jnp.bool_)
     for k in range(value_ids.shape[0]):
         hit = hit | (lane == value_ids[k][:, None])
-        hit = hit | ((lane == out_full[k][:, None] + experts) & (out_full[k][:, None] >= 0))
+        hit = hit | ((lane == out_full[k][:, None] + out_lane) & (out_full[k][:, None] >= 0))
     return hit.astype(f32)
 
 
@@ -647,8 +727,11 @@
     pick = lambda a, index: lax.dynamic_index_in_dim(a, index, 0, keepdims=False)
     memory_len = memory.shape[2] * lax.axis_size("head")
 
-    pack = jnp.concatenate([value_weight[0, 0], key_weight[0, 0], query_weight[0, 0], value_router[0, 0], out_router[0, 0]], axis=1)
-    small = jnp.concatenate([ln1_gain, ln1_bias, ln2_gain, ln2_bias, up_bias, down_bias, jnp.zeros_like(jnp.tile(ln1_gain, (2, 1)))], axis=0)
+    value_rows = experts * head_width
+    router_rows = [padded_rows(a[0, 0].T, out_lane) for a in (value_router, out_router)]
+    kqr = jnp.concatenate([key_weight[0, 0].T, query_weight[0, 0].T, *router_rows])
+    weights = [kqr, value_weight[0, 0].T, output_weight[0, 0], up_weight[0], down_weight[0]]
+    small = jnp.concatenate([ln1_gain, ln1_bias, ln2_gain, ln2_bias, up_bias, down_bias, ln1_gain, ln1_bias], axis=0)
     route_rows = jnp.concatenate(
         [
             jnp.transpose(value_routes[0, :, :, 0, :], (0, 2, 1)),
@@ -656,18 +739,19 @@
         ],
         axis=1,
     )
-
-    def both_layers(own, sent):
-        got = swap_section(sent)
+    sends = [small, pick(memory[0], 1 - sec), pick(route_rows, 1 - sec)]
+    sends, weights = lax.optimization_barrier((sends, weights))
+    gots = [swap_section(a) for a in sends]
+    weights, gots = lax.optimization_barrier((weights, gots))
+    small_got, memory_got, routes_got = gots
+
+    def both_layers(own, got):
         return jnp.where(first, own, got), jnp.where(first, got, own)
 
-    smalls = both_layers(small, small)
-    route_sets = both_layers(pick(route_rows, sec), pick(route_rows, 1 - sec))
-    memories = both_layers(pick(memory[0], sec), pick(memory[0], 1 - sec))
-    packs = both_layers(pack, pack)
-    outs_w = both_layers(output_weight[0, 0], output_weight[0, 0])
-    ups = both_layers(up_weight[0], up_weight[0])
-    downs = both_layers(down_weight[0], down_weight[0])
+    smalls = both_layers(small, small_got)
+    route_sets = both_layers(pick(route_rows, sec), routes_got)
+    memories = both_layers(pick(memory[0], sec), memory_got)
+    weight_sets = [both_layers(a, got) for a, got in zip(weights, swap_weights(weights))]
 
     x = pick(inputs, sec)
     cot = pick(out_cot, sec)
@@ -685,10 +769,9 @@
                 shift2=vec[3:4],
                 up_b=vec[4:5],
                 down_b=vec[5:6],
-                w=spread(packs[number], experts, head_width),
-                wo=pad_lanes(outs_w[number], 0, experts, head_width),
-                wu=ups[number],
-                wd=downs[number],
+                w=(weight_sets[1][number], weight_sets[0][number], weight_sets[2][number]),
+                wu=weight_sets[3][number],
+                wd=weight_sets[4][number],
                 mask=route_mask(routes[:topk], routes[topk:, memory_len:], experts, memory_len),
                 mem=memories[number],
             )
@@ -698,21 +781,22 @@
     own_norm = norm_only(x, layers[0]["gain1"], layers[0]["shift1"])
     slots = gather_slots(own_norm)
     for layer in layers:
-        layer["mem_all"] = jnp.concatenate(gather_slots(norm_only(layer["mem"], layer["gain1"], layer["shift1"])), axis=0)
+        layer["mem_slots"] = gather_slots(norm_only(layer["mem"], layer["gain1"], layer["shift1"]))
     cot_slots = gather_slots(cot)
 
     saves = []
     rows_in = x
     layer_outs = []
     for number, layer in enumerate(layers):
-        out, normed, q, k, v, ev, gate, att, mixed = attn_fwd(
-            me, layer["mem_all"], slots, layer["w"], layer["wo"], layer["mask"], experts, head_width
+        *out, normed, q, k, v, ev, gate, att, mixed = attn_fwd(
+            me, layer["mem_slots"], slots, layer["w"], layer["mask"], experts, head_width
         )
-        terms = scatter_slots([out[s] for s in range(4)])
+        terms = scatter_slots(out)
         hidden, own_norm2 = add_norm(rows_in, terms, no_add, layer["gain2"], layer["shift2"], f32)
         n2_slots = gather_slots(own_norm2)
-        ffn, n2, upper, active = ffn_fwd(n2_slots, layer["wu"], layer["up_b"], layer["wd"])
-        terms = scatter_slots([ffn[s] for s in range(4)])
+        near_a, near_b, *kept = ffn_fwd(n2_slots[0:2], 0, layer["wu"], layer["up_b"], layer["wd"], ())
+        far_a, far_b, n2, upper, active = ffn_fwd(n2_slots[2:4], 1, layer["wu"], layer["up_b"], layer["wd"], kept)
+        terms = scatter_slots([near_a, near_b, far_a, far_b])
         next_layer = layers[min(number + 1, 1)]
         result, own_norm = add_norm(hidden, terms, layer["down_b"], next_layer["gain1"], next_layer["shift1"], bf16)
         layer_outs.append(result)
@@ -723,79 +807,111 @@
             rows_in = result
             slots = gather_slots(own_norm)
 
+    def by_layer(one, two):
+        got = swap_section(jnp.where(first, two, one))
+        kept = jnp.where(first, one, two)
+        return jnp.stack([jnp.where(first, kept, got), jnp.where(first, got, kept)])[None]
+
+    def send_chunks(one, two, pieces):
+        gots, owns = [], []
+        for part_one, part_two in zip(cut(one, pieces), cut(two, pieces)):
+            gots.append(jnp.where(first, part_two, part_one))
+            owns.append(jnp.where(first, part_one, part_two))
+        return gots, owns
+
+    layer_out = by_layer(*layer_outs)
+    sums = ChunkSums()
+    grads = [{}, {}]
+    smalls_out = [None, None]
     input_grads = [None, None]
-    grads = [None, None]
     g_rows = cot
     g_slots = cot_slots
     for number in (1, 0):
-        layer, saved = layers[number], saves[number]
-        ffn, g_all, upper_grad, up_bias_grad = ffn_bwd(g_slots, saved["upper"], layer["wd"], layer["wu"])
-        terms = scatter_slots([ffn[s] for s in range(4)])
-        down_grad = t_dot(saved["active"], g_all).astype(bf16)
-        up_grad = t_dot(saved["n2"], upper_grad).astype(bf16)
+        layer, saved, grad = layers[number], saves[number], grads[number]
+        near_a, near_b, near_bias, *kept = ffn_bwd(g_slots[0:2], 0, saved["upper"], layer["wd"], layer["wu"], ())
+        far_a, far_b, far_bias, g_all, upper_grad = ffn_bwd(g_slots[2:4], 1, saved["upper"], layer["wd"], layer["wu"], kept)
+        grad["down"] = t_dot(saved["active"], g_all).astype(bf16)
+        grad["up"] = t_dot(saved["n2"], upper_grad).astype(bf16)
+        if number == 0:
+            down_sends, down_owns = send_chunks(grads[0]["down"], grads[1]["down"], 2)
+            up_sends, up_owns = send_chunks(grads[0]["up"], grads[1]["up"], 2)
+            up_sends = after(up_sends, down_sends)
+            beside = (down_sends, up_sends)
+        else:
+            beside = (grad["down"], grad["up"])
+        terms, beside = scatter_slots([near_a, near_b, far_a, far_b], beside)
+        if number == 0:
+            for own, send in zip((*down_owns, *up_owns), (*down_sends, *up_sends)):
+                sums.add(own, swap_section(send))
+        else:
+            grad["down"], grad["up"] = beside
         hidden_grad, hidden_low, small2 = norm_back(saved["hidden"], terms, layer["gain2"], g_rows)
         a_slots = gather_slots(hidden_low)
-        ngs, ngm, dproj, a_all = attn_bwd(me, a_slots, layer["w"], layer["wo"], saved["attn"], experts, head_width)
-        seq_terms = scatter_slots([ngs[s] for s in range(4)])
+        if number == 0:
+            sums.turn(0)
+            sums.turn(1)
+            a_slots[3] = sums.before(a_slots[3])
+        *ngs, ngm, dproj, a_all = attn_bwd(me, a_slots, layer["w"], saved["attn"], experts, head_width)
+        grad["out"] = squeeze_out(t_dot(saved["mixed"], a_all).astype(bf16), experts, head_width)
+        grad["pack"] = squeeze(t_dot(dproj, saved["normed"]).astype(bf16), experts, head_width)
+        if number == 0:
+            out_sends, out_owns = send_chunks(grads[0]["out"], grads[1]["out"], 1)
+            pack_sends, pack_owns = send_chunks(grads[0]["pack"], grads[1]["pack"], 2)
+            pack_sends = after(pack_sends, out_sends)
+            beside = (out_sends, pack_sends)
+        else:
+            beside = (grad["out"], grad["pack"], layer_out)
+        seq_terms, beside = scatter_slots(ngs, beside)
         mem_terms = scatter_slots(cut(ngm, 4))
-        out_grad = t_dot(saved["mixed"], a_all).astype(bf16)
-        out_grad = out_grad.reshape(experts, lanes, -1)[:, :head_width].reshape(experts * head_width, -1)
-        pack_grad = squeeze(t_dot(saved["normed"], dproj).astype(bf16), experts, head_width)
-        _, input_low, small1 = norm_back(saved["rows"], seq_terms, layer["gain1"], hidden_grad)
+        if number == 0:
+            for own, send in zip((*out_owns, *pack_owns), (*out_sends, *pack_sends)):
+                sums.add(own, swap_section(send))
+            sums.token = ngs[0]
+            sums.turn(0)
+            sums.turn(2)
+            sums.turn(1)
+            seq_terms = (*seq_terms[0:2], sums.before(seq_terms[2]))
+        else:
+            grad["out"], grad["pack"], layer_out = beside
+        input_grad, input_low, small1 = norm_back(saved["rows"], seq_terms, layer["gain1"], hidden_grad)
         small_mem = norm_back_small(layer["mem"], mem_terms)
         input_grads[number] = input_low
-        over_head = jnp.concatenate([(small1 + small_mem)[0:2], small2[0:3], jnp.zeros_like(small2[0:3])], axis=0)
-        grads[number] = dict(
-            arrays=cut(down_grad, 2) + cut(up_grad, 2) + cut(out_grad, 1) + cut(pack_grad, 2),
-            over_head=over_head,
-            up_bias=up_bias_grad,
-        )
+        vec = jnp.concatenate([(small1 + small_mem)[0:2], small2[0:3], jnp.zeros_like(small2[0:3])], axis=0)
+        vec = vec + to_core(vec)
+        vec = vec + to_chip(vec)
+        smalls_out[number] = jnp.concatenate([vec[0:5], near_bias + far_bias, vec[6:8]], axis=0)
         if number == 1:
             g_rows = input_low
             g_slots = gather_slots(input_low)
 
-    def combine(one, two):
-        kind = one.dtype
-        from_first = lax.ppermute(two, "section", [(0, 1)])
-        from_second = lax.ppermute(one, "section", [(1, 0)])
-        at_second = (two.astype(f32) + from_first.astype(f32)).astype(kind)
-        at_first = (one.astype(f32) + from_second.astype(f32)).astype(kind)
-        return jnp.where(first, at_first, at_second)
-
-    sums = [sum_dp(combine(one, two)) for one, two in zip(grads[0]["arrays"], grads[1]["arrays"])]
-    vecs = []
-    for grad in grads:
-        vec = grad["over_head"]
-        vec = vec + to_core(vec)
-        vec = vec + to_chip(vec)
-        vecs.append(jnp.concatenate([vec[0:5], grad["up_bias"], vec[6:8]], axis=0))
-    vec = sum_dp(combine(*vecs))
-
-    down_sum = jnp.concatenate(sums[0:2], axis=0)
-    up_sum = jnp.concatenate(sums[2:4], axis=0)
-    out_sum = sums[4]
-    pack_sum = jnp.concatenate(sums[5:7], axis=0)
-    ev = experts * head_width
-    value_sum, key_sum = pack_sum[:, :ev], pack_sum[:, ev : ev + head_width]
-    query_sum = pack_sum[:, ev + head_width : ev + 2 * head_width]
-    vroute_sum = pack_sum[:, ev + 2 * head_width : ev + 2 * head_width + experts]
-    oroute_sum = pack_sum[:, ev + 2 * head_width + experts :]
-
-    def by_layer(one, two):
-        kept = jnp.where(first, one, two)
-        got = swap_section(jnp.where(first, two, one))
-        return jnp.stack([jnp.where(first, kept, got), jnp.where(first, got, kept)])[None]
+    vec_own = jnp.where(first, smalls_out[0], smalls_out[1])
+    vec_got = swap_section(jnp.where(first, smalls_out[1], smalls_out[0]))
+    last_chunk = sums.chunks[-1]
+    last_chunk["own"], last_chunk["moving"] = (last_chunk["own"], vec_own), (last_chunk["moving"], vec_got)
+    for newest in range(3, len(sums.chunks) + 3):
+        for number in range(min(newest, len(sums.chunks) - 1), -1, -1):
+            if sums.chunks[number]["step"] < 4:
+                sums.turn(number)
+    *chunks, (last, vec) = [chunk["end"] for chunk in sums.chunks]
+    input_grad = by_layer(*input_grads)
+    down_sum = jnp.concatenate(chunks[0:2], axis=0).astype(f32)
+    up_sum = jnp.concatenate(chunks[2:4], axis=0).astype(f32)
+    out_sum = chunks[4].astype(f32)
+    pack_sum = jnp.concatenate([chunks[5], last], axis=0).astype(f32)
+    value_sum, key_sum, query_sum = pack_sum[:value_rows], pack_sum[value_rows : value_rows + head_width], pack_sum[value_rows + head_width : value_rows + 2 * head_width]
+    vroute_sum = pack_sum[value_rows + 2 * head_width : value_rows + 2 * head_width + experts]
+    oroute_sum = pack_sum[value_rows + 2 * head_width + out_lane : value_rows + 2 * head_width + out_lane + experts]
 
     return (
-        by_layer(*layer_outs),
-        by_layer(*input_grads),
+        layer_out,
+        input_grad,
         vec[0:1],
         vec[1:2],
-        query_sum[None, None],
-        key_sum[None, None],
-        value_sum[None, None],
-        vroute_sum[None, None],
-        oroute_sum[None, None],
+        query_sum.T[None, None],
+        key_sum.T[None, None],
+        value_sum.T[None, None],
+        vroute_sum.T[None, None],
+        oroute_sum.T[None, None],
         out_sum[None, None],
         vec[2:3],
         vec[3:4],

time: 962 us -> 721 us (0.75)
  waiting for transfers between devices: 459 us -> 333 us
  local copies, waits for them, and re-layouts: 78.3 us -> 19.6 us
  starting transfers between devices: 181 us -> 124 us
    ppermute x40 -> x29, waiting for transfers between devices: 234 us -> 116 us  [the longest x24 89.9 us: move(): return jax.tree.map(lambda one: lax.ppermute(one, axis, pairs), a)]
    ppermute x40 -> x29, starting transfers between devices: 129 us -> 70.6 us  [the longest x24 62.7 us: move(): return jax.tree.map(lambda one: lax.ppermute(one, axis, pairs), a)]
    ppermute x9 -> x18, waiting for transfers between devices: 89.1 us -> 66.2 us  [swap_section(): return lax.ppermute(a, 'section', [(0, 1), (1, 0)])]
    convert_element_type x14 -> x24, other arithmetic: 13.2 us -> 35.3 us  [the longest x21 30 us: plus(): (one.astype(f32) + two.astype(f32)).astype(one.dtype)]
    ppermute x22, waiting for transfers between devices: 133 us -> 148 us  [to_chip(): return lax.ppermute(a, 'head', chip_pairs)]
    squeeze x8 -> x0, local copies, waits for them, and re-layouts: 12.6 us -> none  [the longest x4 6.21 us: on_device(): terms = scatter_slots([ffn[s] for s in range(4)])]
    slice x11 -> x2, local copies, waits for them, and re-layouts: 10.1 us -> 0.01 us  [on_device(): vec[6:8]]
    ppermute x9 -> x18, starting transfers between devices: 13.9 us -> 22.4 us  [swap_section(): return lax.ppermute(a, 'section', [(0, 1), (1, 0)])]
  transfers between devices with their start and end apart: 113 -> 111, of which waited for: 36 -> 40; matrix products, arithmetic and copies ran while one was open for 18% -> 13% of each run, Pallas kernels for 10% -> 12%
where the time goes in v2:
time: 721 us; the launch traced here: 716 us
  waiting for transfers between devices  333 us (46%)
  Pallas kernels  135 us (19%)
  starting transfers between devices  124 us (17%)
  other arithmetic  74.2 us (10%)
  matrix products  27.6 us (4%)
  local copies, waits for them, and re-layouts  19.6 us (3%)
    ppermute x22, waiting for transfers between devices, to_chip(): return lax.ppermute(a, 'head', chip_pairs)  148 us
    ppermute x24, waiting for transfers between devices, move(): return jax.tree.map(lambda one: lax.ppermute(one, axis, pairs), a)  89.9 us
    ppermute x18, waiting for transfers between devices, swap_section(): return lax.ppermute(a, 'section', [(0, 1), (1, 0)])  66.2 us
    ppermute x24, starting transfers between devices, move(): return jax.tree.map(lambda one: lax.ppermute(one, axis, pairs), a)  62.7 us
    pallas_call x2, Pallas kernels, attn_fwd(): pl.pallas_call(functools.partial(attn_fwd_kernel, experts, head_width), g...  38.2 us
    pallas_call x2, Pallas kernels, attn_bwd(): pl.pallas_call(functools.partial(attn_bwd_kernel, experts, head_width), g...  32.5 us
    convert_element_type x21, other arithmetic, plus(): (one.astype(f32) + two.astype(f32)).astype(one.dtype)  30 us
    dot_general x8, matrix products, t_dot(): lax.dot_general(a, b, (((0,), (0,)), ((), ())), preferred_element_type=f32)  27.6 us
  transfers between devices with their start and end apart: 111, of which 40 were waited for; matrix products, arithmetic and copies ran while one was open for 13% of the time, Pallas kernels for 12%

profile of v2, /device:TPU:0, one launch (start us, length us, event | category | flops | bytes accessed | tf_op | source)
XLA Modules:
  0.0 716.3 jit_solution(9484020912240934844)
XLA Ops:
  27.2 22.5 %collective-permute-done.13 = bf16[280,1024]{1,0:T(8,128)(2,1)S(1)} collective-permute-done((bf16[280,1024]{1,0:T(8,128)(2,1)S(1)}, bf16[280,1024]{1,0:T(8,128)(2,1)S(1)}, u32[]{:S(2)}, u32[]{:S(2)}) %collective-permute-start.13) | collective-permute-done | bytes 573472 | tf_op jit(solution)/shard_map/ppermute | solution.py:58
  55.0 9.4 %collective-permute-done.14 = bf16[280,1024]{1,0:T(8,128)(2,1)S(1)} collective-permute-done((bf16[280,1024]{1,0:T(8,128)(2,1)S(1)}, bf16[280,1024]{1,0:T(8,128)(2,1)S(1)}, u32[]{:S(2)}, u32[]{:S(2)}) %collective-permute-start.14) | collective-permute-done | bytes 573472 | tf_op jit(solution)/shard_map/ppermute | solution.py:685
  70.1 8.8 %collective-permute-done.10 = bf16[280,1024]{1,0:T(8,128)(2,1)S(1)} collective-permute-done((bf16[280,1024]{1,0:T(8,128)(2,1)S(1)}, bf16[280,1024]{1,0:T(8,128)(2,1)S(1)}, u32[]{:S(2)}, u32[]{:S(2)}) %collective-permute-start.10) | collective-permute-done | bytes 573472 | tf_op jit(solution)/shard_map/ppermute | solution.py:685
  85.2 15.0 %attn_fwd.2 = (bf16[256,1024]{1,0:T(8,128)(2,1)S(1)}, bf16[256,1024]{1,0:T(8,128)(2,1)S(1)}, bf16[256,1024]{1,0:T(8,128)(2,1)S(1)}, bf16[256,1024]{1,0:T(8,128)(...) custom-call(s32[1]{0:T(128)} %bitcast.me_ref, ...), custom_call_target="tpu_custom_call" | custom-call | flops 3355443200 | bytes 16777216 | tf_op jit(solution)/shard_map/attn_fwd/pallas_call | solution.py:343
  110.3 10.5 %collective-permute-done.17.c_ref = bf16[256,1024]{1,0:T(8,128)(2,1)S(1)} collective-permute-done((bf16[256,1024]{1,0:T(8,128)(2,1)S(1)}, bf16[256,1024]{1,0:T(8,128)(2,1)S(1)}, u32[]{:S(2)}, u32[]{:S(2)}) %collective-permute-start.17) | collective-permute-done | bytes 524320 | tf_op jit(solution)/shard_map/ppermute | solution.py:54
  152.5 13.7 %collective-permute-done.27.c_ref = bf16[256,1024]{1,0:T(8,128)(2,1)S(1)} collective-permute-done((bf16[256,1024]{1,0:T(8,128)(2,1)S(1)}, bf16[256,1024]{1,0:T(8,128)(2,1)S(1)}, u32[]{:S(2)}, u32[]{:S(2)}) %collective-permute-start.27) | collective-permute-done | bytes 524320 | tf_op jit(solution)/shard_map/ppermute | solution.py:54
  169.2 12.5 %collective-permute-done.32.p2_ref = bf16[256,1024]{1,0:T(8,128)(2,1)S(1)} collective-permute-done((bf16[256,1024]{1,0:T(8,128)(2,1)S(1)}, bf16[256,1024]{1,0:T(8,128)(2,1)S(1)}, u32[]{:S(2)}, u32[]{:S(2)}) %collective-permute-start.32) | collective-permute-done | bytes 524320 | tf_op jit(solution)/shard_map/ppermute | solution.py:54
  187.0 23.2 %attn_fwd.3 = (bf16[256,1024]{1,0:T(8,128)(2,1)S(1)}, bf16[256,1024]{1,0:T(8,128)(2,1)S(1)}, bf16[256,1024]{1,0:T(8,128)(2,1)S(1)}, bf16[256,1024]{1,0:T(8,128)(...) custom-call(s32[1]{0:T(128)} %bitcast.me_ref, ...), custom_call_target="tpu_custom_call" | custom-call | flops 3355443200 | bytes 16777216 | tf_op jit(solution)/shard_map/attn_fwd/pallas_call | solution.py:343
  213.1 13.7 %collective-permute-done.36.c_ref = bf16[256,1024]{1,0:T(8,128)(2,1)S(1)} collective-permute-done((bf16[256,1024]{1,0:T(8,128)(2,1)S(1)}, bf16[256,1024]{1,0:T(8,128)(2,1)S(1)}, u32[]{:S(2)}, u32[]{:S(2)}) %collective-permute-start.36) | collective-permute-done | bytes 524320 | tf_op jit(solution)/shard_map/ppermute | solution.py:54
  229.6 12.7 %collective-permute-done.38.a_ref = bf16[256,1024]{1,0:T(8,128)(2,1)S(1)} collective-permute-done((bf16[256,1024]{1,0:T(8,128)(2,1)S(1)}, bf16[256,1024]{1,0:T(8,128)(2,1)S(1)}, u32[]{:S(2)}, u32[]{:S(2)}) %collective-permute-start.38) | collective-permute-done | bytes 524320 | tf_op jit(solution)/shard_map/ppermute | solution.py:54
  242.8 9.3 %collective-permute-done.42.a_ref = bf16[256,1024]{1,0:T(8,128)(2,1)S(1)} collective-permute-done((bf16[256,1024]{1,0:T(8,128)(2,1)S(1)}, bf16[256,1024]{1,0:T(8,128)(2,1)S(1)}, u32[]{:S(2)}, u32[]{:S(2)}) %collective-permute-start.42) | collective-permute-done | bytes 524320 | tf_op jit(solution)/shard_map/ppermute | solution.py:54
  289.0 20.8 %collective-permute-done.45.c_ref = bf16[256,1024]{1,0:T(8,128)(2,1)S(1)} collective-permute-done((bf16[256,1024]{1,0:T(8,128)(2,1)S(1)}, bf16[256,1024]{1,0:T(8,128)(2,1)S(1)}, u32[]{:S(2)}, u32[]{:S(2)}) %collective-permute-start.45) | collective-permute-done | bytes 524320 | tf_op jit(solution)/shard_map/ppermute | solution.py:54
  316.7 10.0 %collective-permute-done.47.d2_ref = bf16[256,1024]{1,0:T(8,128)(2,1)S(1)} collective-permute-done((bf16[256,1024]{1,0:T(8,128)(2,1)S(1)}, bf16[256,1024]{1,0:T(8,128)(2,1)S(1)}, u32[]{:S(2)}, u32[]{:S(2)}) %collective-permute-start.47) | collective-permute-done | bytes 524320 | tf_op jit(solution)/shard_map/ppermute | solution.py:54
  330.6 16.0 %attn_bwd.2 = (bf16[256,1024]{1,0:T(8,128)(2,1)S(1)}, bf16[256,1024]{1,0:T(8,128)(2,1)S(1)}, bf16[256,1024]{1,0:T(8,128)(2,1)S(1)}, bf16[256,1024]{1,0:T(8,128)(...) custom-call(s32[1]{0:T(128)} %bitcast.me_ref, ...), custom_call_target="tpu_custom_call" | custom-call | flops 3355443200 | bytes 16777216 | tf_op jit(solution)/shard_map/attn_bwd/pallas_call | solution.py:510
  357.4 12.7 %collective-permute-done.50.c_ref = bf16[256,1024]{1,0:T(8,128)(2,1)S(1)} collective-permute-done((bf16[256,1024]{1,0:T(8,128)(2,1)S(1)}, bf16[256,1024]{1,0:T(8,128)(2,1)S(1)}, u32[]{:S(2)}, u32[]{:S(2)}) %collective-permute-start.50) | collective-permute-done | bytes 524320 | tf_op jit(solution)/shard_map/ppermute | solution.py:54
  374.8 12.0 %collective-permute-done.58.a_ref = bf16[256,1024]{1,0:T(8,128)(2,1)S(1)} collective-permute-done((bf16[256,1024]{1,0:T(8,128)(2,1)S(1)}, bf16[256,1024]{1,0:T(8,128)(2,1)S(1)}, u32[]{:S(2)}, u32[]{:S(2)}) %collective-permute-start.58) | collective-permute-done | bytes 524320 | tf_op jit(solution)/shard_map/ppermute | solution.py:54
  447.6 9.4 %collective-permute-done.65 = bf16[512,1024]{1,0:T(8,128)(2,1)} collective-permute-done((bf16[512,1024]{1,0:T(8,128)(2,1)}, bf16[512,1024]{1,0:T(8,128)(2,1)}, u32[]{:S(2)}, u32[]{:S(2)}) %collective-permute-start.65) | collective-permute-done | bytes 1048608 | tf_op jit(solution)/shard_map/ppermute | solution.py:58
  466.2 16.5 %attn_bwd.3 = (bf16[256,1024]{1,0:T(8,128)(2,1)S(1)}, bf16[256,1024]{1,0:T(8,128)(2,1)S(1)}, bf16[256,1024]{1,0:T(8,128)(2,1)S(1)}, bf16[256,1024]{1,0:T(8,128)(...) custom-call(s32[1]{0:T(128)} %bitcast.me_ref, ...), custom_call_target="tpu_custom_call" | custom-call | flops 3355443200 | bytes 16777216 | tf_op jit(solution)/shard_map/attn_bwd/pallas_call | solution.py:510
  521.9 14.1 %collective-permute-start.87 = (bf16[512,1024]{1,0:T(8,128)(2,1)S(1)}, bf16[512,1024]{1,0:T(8,128)(2,1)}, u32[]{:S(2)}, u32[]{:S(2)}) collective-permute-start(bf16[512,1024]{1,0:T(8,128)(2,1)S(1)} %copy-done.26), channel_id=1, source_target_pairs={{0,1},{3,2},{4,5},{7,6},{8,9},{11,10},{12,13},{15,14},{16,17},{19,... | collective-permute-start | bytes 3145736 | tf_op jit(solution)/shard_map/ppermute | solution.py:612
  559.0 9.1 %collective-permute-done.73 = bf16[256,1024]{1,0:T(8,128)(2,1)S(1)} collective-permute-done((bf16[256,1024]{1,0:T(8,128)(2,1)S(1)}, bf16[256,1024]{1,0:T(8,128)(2,1)S(1)}, u32[]{:S(2)}, u32[]{:S(2)}) %collective-permute-start.73) | collective-permute-done | bytes 524320 | tf_op jit(solution)/shard_map/ppermute | solution.py:58
  576.5 21.2 %collective-permute-done.109 = bf16[512,1024]{1,0:T(8,128)(2,1)S(1)} collective-permute-done((bf16[512,1024]{1,0:T(8,128)(2,1)S(1)}, bf16[512,1024]{1,0:T(8,128)(2,1)S(1)}, u32[]{:S(2)}, u32[]{:S(2)}) %collective-permute-start.109) | collective-permute-done | bytes 1048608 | tf_op jit(solution)/shard_map/ppermute | solution.py:612
  642.9 16.5 %collective-permute-done.108 = bf16[512,1024]{1,0:T(8,128)(2,1)S(1)} collective-permute-done((bf16[512,1024]{1,0:T(8,128)(2,1)S(1)}, bf16[512,1024]{1,0:T(8,128)(2,1)S(1)}, u32[]{:S(2)}, u32[]{:S(2)}) %collective-permute-start.108) | collective-permute-done | bytes 1048608 | tf_op jit(solution)/shard_map/ppermute | solution.py:612
  664.9 36.6 %collective-permute-done.105 = bf16[400,1024]{1,0:T(8,128)(2,1)S(1)} collective-permute-done((bf16[400,1024]{1,0:T(8,128)(2,1)S(1)}, bf16[400,1024]{1,0:T(8,128)(2,1)S(1)}, u32[]{:S(2)}, u32[]{:S(2)}) %collective-permute-start.105) | collective-permute-done | bytes 819232 | tf_op jit(solution)/shard_map/ppermute | solution.py:612
  703.1 8.0 %collective-permute-done.104 = f32[8,1024]{1,0:T(8,128)S(1)} collective-permute-done((f32[8,1024]{1,0:T(8,128)S(1)}, f32[8,1024]{1,0:T(8,128)S(1)}, u32[]{:S(2)}, u32[]{:S(2)}) %collective-permute-start.104) | collective-permute-done | bytes 32800 | tf_op jit(solution)/shard_map/ppermute | solution.py:612
  (486 shorter events, 359.5 us)
Async XLA Ops:
  14.9 55.2 %collective-permute-start.7 = (bf16[256,1024]{1,0:T(8,128)(2,1)S(1)}, bf16[256,1024]{1,0:T(8,128)(2,1)}, u32[]{:S(2)}, u32[]{:S(2)}) collective-permute-start(bf16[256,1024]{1,0:T(8,128)(2,1)S(1)} %norm_only.4.p0_ref), channel_id=1, source_target_pairs={{0,8},{8,0},{4,12},{12,4},{1,9},{9,1},{5,13},{13,5},{2,10},{10,2},... | collective-permute-start | bytes 1572872 | tf_op jit(solution)/shard_map/ppermute | solution.py:54
  16.7 67.7 %collective-permute-start.6 = (bf16[256,1024]{1,0:T(8,128)(2,1)S(1)}, bf16[256,1024]{1,0:T(8,128)(2,1)}, u32[]{:S(2)}, u32[]{:S(2)}) collective-permute-start(bf16[256,1024]{1,0:T(8,128)(2,1)S(1)} %norm_only.4.p0_ref), channel_id=1, source_target_pairs={{0,4},{4,0},{8,12},{12,8},{1,5},{5,1},{9,13},{13,9},{2,6},{6,2},{1... | collective-permute-start | bytes 1572872 | tf_op jit(solution)/shard_map/ppermute | solution.py:50
  19.1 35.3 %collective-permute-start.9 = (bf16[280,1024]{1,0:T(8,128)(2,1)}, bf16[280,1024]{1,0:T(8,128)(2,1)S(1)}, u32[]{:S(2)}, u32[]{:S(2)}) collective-permute-start(bf16[280,1024]{1,0:T(8,128)(2,1)} %constant_dynamic-slice_fusion.3), channel_id=1, source_target_pairs={{0,16},{16,0},{1,17},{17,1},{2,18},{18,2},{3,19},{19,3},{4,20},{20... | collective-permute-start | bytes 1720328 | tf_op jit(solution)/shard_map/ppermute | solution.py:58
  257.5 56.1 %collective-permute-start.51 = (bf16[256,1024]{1,0:T(8,128)(2,1)S(1)}, bf16[256,1024]{1,0:T(8,128)(2,1)S(1)}, u32[]{:S(2)}, u32[]{:S(2)}) collective-permute-start(bf16[256,1024]{1,0:T(8,128)(2,1)S(1)} %get-tuple-element.247), channel_id=1, source_target_pairs={{0,4},{4,0},{8,12},{12,8},{1,5},{5,1},{9,13},{13,9},{2,6},{6,2},{1... | collective-permute-start | bytes 1572872 | tf_op jit(solution)/shard_map/ppermute | solution.py:50
  277.9 31.9 %collective-permute-start.41 = (bf16[256,1024]{1,0:T(8,128)(2,1)S(1)}, bf16[256,1024]{1,0:T(8,128)(2,1)S(1)}, u32[]{:S(2)}, u32[]{:S(2)}) collective-permute-start(bf16[256,1024]{1,0:T(8,128)(2,1)S(1)} %get-tuple-element.223), channel_id=1, source_target_pairs={{0,4},{4,0},{8,12},{12,8},{1,5},{5,1},{9,13},{13,9},{2,6},{6,2},{1... | collective-permute-start | bytes 1572872 | tf_op jit(solution)/shard_map/ppermute | solution.py:50
  387.5 51.8 %collective-permute-start.80 = (bf16[64,1024]{1,0:T(8,128)(2,1)S(1)}, bf16[64,1024]{1,0:T(8,128)(2,1)S(1)}, u32[]{:S(2)}, u32[]{:S(2)}) collective-permute-start(bf16[64,1024]{1,0:T(8,128)(2,1)S(1)} %get-tuple-element.406), channel_id=1, source_target_pairs={{0,4},{4,0},{8,12},{12,8},{1,5},{5,1},{9,13},{13,9},{2,6},{6,2},{1... | collective-permute-start | bytes 393224 | tf_op jit(solution)/shard_map/ppermute | solution.py:50
  409.7 47.3 %collective-permute-start.65 = (bf16[512,1024]{1,0:T(8,128)(2,1)}, bf16[512,1024]{1,0:T(8,128)(2,1)}, u32[]{:S(2)}, u32[]{:S(2)}) collective-permute-start(bf16[512,1024]{1,0:T(8,128)(2,1)} %get-tuple-element.368), channel_id=1, source_target_pairs={{0,16},{16,0},{1,17},{17,1},{2,18},{18,2},{3,19},{19,3},{4,20},{20... | collective-permute-start | bytes 3145736 | tf_op jit(solution)/shard_map/ppermute | solution.py:58
  436.1 46.5 %collective-permute-start.72 = (bf16[512,1024]{1,0:T(8,128)(2,1)}, bf16[512,1024]{1,0:T(8,128)(2,1)}, u32[]{:S(2)}, u32[]{:S(2)}) collective-permute-start(bf16[512,1024]{1,0:T(8,128)(2,1)} %add_convert_fusion.14), channel_id=1, source_target_pairs={{0,1},{3,2},{4,5},{7,6},{8,9},{11,10},{12,13},{15,14},{16,17},{19,... | collective-permute-start | bytes 3145736 | tf_op jit(solution)/shard_map/ppermute | solution.py:612
  445.4 42.1 %collective-permute-start.71 = (bf16[512,1024]{1,0:T(8,128)(2,1)}, bf16[512,1024]{1,0:T(8,128)(2,1)S(1)}, u32[]{:S(2)}, u32[]{:S(2)}) collective-permute-start(bf16[512,1024]{1,0:T(8,128)(2,1)} %get-tuple-element.270), channel_id=1, source_target_pairs={{0,16},{16,0},{1,17},{17,1},{2,18},{18,2},{3,19},{19,3},{4,20},{20... | collective-permute-start | bytes 3145736 | tf_op jit(solution)/shard_map/ppermute | solution.py:58
  457.0 50.0 %collective-permute-start.86 = (bf16[512,1024]{1,0:T(8,128)(2,1)}, bf16[512,1024]{1,0:T(8,128)(2,1)}, u32[]{:S(2)}, u32[]{:S(2)}) collective-permute-start(bf16[512,1024]{1,0:T(8,128)(2,1)} %get-tuple-element.271), channel_id=1, source_target_pairs={{0,16},{16,0},{1,17},{17,1},{2,18},{18,2},{3,19},{19,3},{4,20},{20... | collective-permute-start | bytes 3145736 | tf_op jit(solution)/shard_map/ppermute | solution.py:58
  462.0 37.7 %collective-permute-start.70 = (bf16[512,1024]{1,0:T(8,128)(2,1)}, bf16[512,1024]{1,0:T(8,128)(2,1)}, u32[]{:S(2)}, u32[]{:S(2)}) collective-permute-start(bf16[512,1024]{1,0:T(8,128)(2,1)} %add_convert_fusion.13), channel_id=1, source_target_pairs={{0,1},{3,2},{4,5},{7,6},{8,9},{11,10},{12,13},{15,14},{16,17},{19,... | collective-permute-start | bytes 3145736 | tf_op jit(solution)/shard_map/ppermute | solution.py:612
  485.7 57.1 %collective-permute-start.89 = (bf16[512,1024]{1,0:T(8,128)(2,1)}, bf16[512,1024]{1,0:T(8,128)(2,1)}, u32[]{:S(2)}, u32[]{:S(2)}) collective-permute-start(bf16[512,1024]{1,0:T(8,128)(2,1)} %add_convert_fusion.12), channel_id=1, source_target_pairs={{1,2},{2,1},{5,6},{6,5},{9,10},{10,9},{13,14},{14,13},{17,18},{18,... | collective-permute-start | bytes 3145736 | tf_op jit(solution)/shard_map/ppermute | solution.py:612
  519.3 33.0 %collective-permute-start.88 = (bf16[560,1024]{1,0:T(8,128)(2,1)}, bf16[560,1024]{1,0:T(8,128)(2,1)S(1)}, u32[]{:S(2)}, u32[]{:S(2)}) collective-permute-start(bf16[560,1024]{1,0:T(8,128)(2,1)} %broadcast_select_fusion.4), channel_id=1, source_target_pairs={{0,16},{16,0},{1,17},{17,1},{2,18},{18,2},{3,19},{19,3},{4,20},{20... | collective-permute-start | bytes 3440648 | tf_op jit(solution)/shard_map/ppermute | solution.py:58
  521.9 34.8 %collective-permute-start.87 = (bf16[512,1024]{1,0:T(8,128)(2,1)S(1)}, bf16[512,1024]{1,0:T(8,128)(2,1)}, u32[]{:S(2)}, u32[]{:S(2)}) collective-permute-start(bf16[512,1024]{1,0:T(8,128)(2,1)S(1)} %copy-done.26), channel_id=1, source_target_pairs={{0,1},{3,2},{4,5},{7,6},{8,9},{11,10},{12,13},{15,14},{16,17},{19,... | collective-permute-start | bytes 3145736 | tf_op jit(solution)/shard_map/ppermute | solution.py:612
  536.0 38.0 %collective-permute-start.95 = (bf16[512,1024]{1,0:T(8,128)(2,1)S(1)}, bf16[512,1024]{1,0:T(8,128)(2,1)}, u32[]{:S(2)}, u32[]{:S(2)}) collective-permute-start(bf16[512,1024]{1,0:T(8,128)(2,1)S(1)} %add_convert_fusion.8), channel_id=1, source_target_pairs={{1,2},{2,1},{5,6},{6,5},{9,10},{10,9},{13,14},{14,13},{17,18},{18,... | collective-permute-start | bytes 3145736 | tf_op jit(solution)/shard_map/ppermute | solution.py:612
  549.4 48.8 %collective-permute-start.110 = (bf16[512,1024]{1,0:T(8,128)(2,1)S(1)}, bf16[512,1024]{1,0:T(8,128)(2,1)S(1)}, u32[]{:S(2)}, u32[]{:S(2)}) collective-permute-start(bf16[512,1024]{1,0:T(8,128)(2,1)S(1)} %add_convert_fusion.7), channel_id=1, source_target_pairs={{1,0},{2,3},{5,4},{6,7},{9,8},{10,11},{13,12},{14,15},{17,16},{18,... | collective-permute-start | bytes 3145736 | tf_op jit(solution)/shard_map/ppermute | solution.py:612
  550.9 46.8 %collective-permute-start.109 = (bf16[512,1024]{1,0:T(8,128)(2,1)S(1)}, bf16[512,1024]{1,0:T(8,128)(2,1)S(1)}, u32[]{:S(2)}, u32[]{:S(2)}) collective-permute-start(bf16[512,1024]{1,0:T(8,128)(2,1)S(1)} %add_convert_fusion.6), channel_id=1, source_target_pairs={{1,0},{2,3},{5,4},{6,7},{9,8},{10,11},{13,12},{14,15},{17,16},{18,... | collective-permute-start | bytes 3145736 | tf_op jit(solution)/shard_map/ppermute | solution.py:612
  556.7 43.1 %collective-permute-start.94 = (bf16[400,1024]{1,0:T(8,128)(2,1)S(1)}, bf16[400,1024]{1,0:T(8,128)(2,1)S(1)}, u32[]{:S(2)}, u32[]{:S(2)}) collective-permute-start(bf16[400,1024]{1,0:T(8,128)(2,1)S(1)} %copy-done.39), channel_id=1, source_target_pairs={{0,16},{16,0},{1,17},{17,1},{2,18},{18,2},{3,19},{19,3},{4,20},{20... | collective-permute-start | bytes 2457608 | tf_op jit(solution)/shard_map/ppermute | solution.py:58
  568.2 33.5 %collective-permute-start.93 = (bf16[560,1024]{1,0:T(8,128)(2,1)S(1)}, bf16[560,1024]{1,0:T(8,128)(2,1)S(1)}, u32[]{:S(2)}, u32[]{:S(2)}) collective-permute-start(bf16[560,1024]{1,0:T(8,128)(2,1)S(1)} %add_convert_fusion.2), channel_id=1, source_target_pairs={{0,1},{3,2},{4,5},{7,6},{8,9},{11,10},{12,13},{15,14},{16,17},{19,... | collective-permute-start | bytes 3440648 | tf_op jit(solution)/shard_map/ppermute | solution.py:612
  574.0 32.8 %collective-permute-start.92 = (bf16[512,1024]{1,0:T(8,128)(2,1)S(1)}, bf16[512,1024]{1,0:T(8,128)(2,1)S(1)}, u32[]{:S(2)}, u32[]{:S(2)}) collective-permute-start(bf16[512,1024]{1,0:T(8,128)(2,1)S(1)} %add_convert_fusion.5), channel_id=1, source_target_pairs={{1,2},{2,1},{5,6},{6,5},{9,10},{10,9},{13,14},{14,13},{17,18},{18,... | collective-permute-start | bytes 3145736 | tf_op jit(solution)/shard_map/ppermute | solution.py:612
  637.7 63.8 %collective-permute-start.106 = (bf16[560,1024]{1,0:T(8,128)(2,1)S(1)}, bf16[560,1024]{1,0:T(8,128)(2,1)S(1)}, u32[]{:S(2)}, u32[]{:S(2)}) collective-permute-start(bf16[560,1024]{1,0:T(8,128)(2,1)S(1)} %add_convert_fusion), channel_id=1, source_target_pairs={{1,0},{2,3},{5,4},{6,7},{9,8},{10,11},{13,12},{14,15},{17,16},{18,... | collective-permute-start | bytes 3440648 | tf_op jit(solution)/shard_map/ppermute | solution.py:612
  640.8 60.7 %collective-permute-start.105 = (bf16[400,1024]{1,0:T(8,128)(2,1)S(1)}, bf16[400,1024]{1,0:T(8,128)(2,1)S(1)}, u32[]{:S(2)}, u32[]{:S(2)}) collective-permute-start(bf16[400,1024]{1,0:T(8,128)(2,1)S(1)} %add_convert_fusion.16), channel_id=1, source_target_pairs={{1,0},{2,3},{5,4},{6,7},{9,8},{10,11},{13,12},{14,15},{17,16},{18,... | collective-permute-start | bytes 2457608 | tf_op jit(solution)/shard_map/ppermute | solution.py:612
  659.8 51.3 %collective-permute-start.103 = (bf16[400,1024]{1,0:T(8,128)(2,1)S(1)}, bf16[400,1024]{1,0:T(8,128)(2,1)S(1)}, u32[]{:S(2)}, u32[]{:S(2)}) collective-permute-start(bf16[400,1024]{1,0:T(8,128)(2,1)S(1)} %add_convert_fusion.15), channel_id=1, source_target_pairs={{1,0},{2,3},{5,4},{6,7},{9,8},{10,11},{13,12},{14,15},{17,16},{18,... | collective-permute-start | bytes 2457608 | tf_op jit(solution)/shard_map/ppermute | solution.py:612
  663.6 47.5 %collective-permute-start.104 = (f32[8,1024]{1,0:T(8,128)S(1)}, f32[8,1024]{1,0:T(8,128)S(1)}, u32[]{:S(2)}, u32[]{:S(2)}) collective-permute-start(f32[8,1024]{1,0:T(8,128)S(1)} %add.263), channel_id=1, source_target_pairs={{1,0},{2,3},{5,4},{6,7},{9,8},{10,11},{13,12},{14,15},{17,16},{18,... | collective-permute-start | bytes 98312 | tf_op jit(solution)/shard_map/ppermute | solution.py:612
  (146 other events, 1964.5 us)

commit v3 on v2

--- a/solution.py
+++ b/solution.py
@@ -58,22 +58,30 @@
     return lax.ppermute(a, "section", [(0, 1), (1, 0)])
 
 
-def gather_slots(own):
+def after(a, *tokens):
+    return lax.optimization_barrier((a, tokens))[0]
+
+
+def gather_slots(own, work=None):
     from_chip = to_chip(own)
     from_core = to_core(own)
-    from_both = to_core(from_chip)
-    return [own, from_core, from_chip, from_both]
-
-
-def scatter_slots(parts, beside=None):
+    if work is None:
+        return [own, from_core, from_chip, to_core(from_chip)]
+    from_chip, done = lax.optimization_barrier((from_chip, work([own, from_core])))
+    return [own, from_core, from_chip, to_core(from_chip)], done
+
+
+def scatter_slots(parts, work=None, start_after=None):
     from_core_far = to_core(parts[3])
     from_core = to_core(parts[1])
     far = (parts[2].astype(f32) + from_core_far.astype(f32)).astype(bf16)
+    if start_after is not None:
+        far = after(far, start_after)
     from_chip = to_chip(far)
-    if beside is None:
+    if work is None:
         return parts[0], from_core, from_chip
-    from_chip, beside = lax.optimization_barrier((from_chip, beside))
-    return (parts[0], from_core, from_chip), beside
+    from_chip, done = lax.optimization_barrier((from_chip, work(far)))
+    return (parts[0], from_core, from_chip), done
 
 
 def norm_rows(x, gain, shift):
@@ -612,10 +620,6 @@
     return jax.tree.map(lambda one: lax.ppermute(one, axis, pairs), a)
 
 
-def after(a, token):
-    return lax.optimization_barrier((a, token))[0]
-
-
 class ChunkSums:
     def __init__(self):
         self.chunks = []
@@ -670,20 +674,25 @@
     return jnp.concatenate(parts, axis=0)
 
 
-def swap_weights(weights):
+def swap_weights(weights, start_after):
     size = lax.axis_size("dp")
-    if size % 2:
-        return [swap_section(a) for a in weights]
     odd = lax.axis_index("dp") % 2
     results = []
-    token = None
-    for a in weights:
-        rows = a.shape[0] // 2
-        half = lax.dynamic_slice_in_dim(a if token is None else after(a, token), odd * rows, rows, 0)
-        token = half
-        got = swap_section(half)
-        other = lax.ppermute(got, "dp", [(i, i ^ 1) for i in range(size)])
-        results.append(jnp.concatenate([jnp.where(odd == 0, got, other), jnp.where(odd == 0, other, got)], axis=0))
+    gots = []
+    for a, pieces in weights:
+        parts = []
+        for part in cut(a, pieces):
+            part = after(part, start_after, *gots[: max(0, len(gots) - 1)])
+            if size % 2:
+                gots.append(swap_section(part))
+                parts.append(gots[-1])
+                continue
+            rows = part.shape[0] // 2
+            gots.append(swap_section(lax.dynamic_slice_in_dim(part, odd * rows, rows, 0)))
+            got = gots[-1]
+            other = lax.ppermute(got, "dp", [(i, i ^ 1) for i in range(size)])
+            parts += [jnp.where(odd == 0, got, other), jnp.where(odd == 0, other, got)]
+        results.append(jnp.concatenate(parts, axis=0))
     return results
 
 
@@ -730,7 +739,8 @@
     value_rows = experts * head_width
     router_rows = [padded_rows(a[0, 0].T, out_lane) for a in (value_router, out_router)]
     kqr = jnp.concatenate([key_weight[0, 0].T, query_weight[0, 0].T, *router_rows])
-    weights = [kqr, value_weight[0, 0].T, output_weight[0, 0], up_weight[0], down_weight[0]]
+    weights = [value_weight[0, 0].T, kqr, output_weight[0, 0], up_weight[0], down_weight[0]]
+
     small = jnp.concatenate([ln1_gain, ln1_bias, ln2_gain, ln2_bias, up_bias, down_bias, ln1_gain, ln1_bias], axis=0)
     route_rows = jnp.concatenate(
         [
@@ -740,10 +750,7 @@
         axis=1,
     )
     sends = [small, pick(memory[0], 1 - sec), pick(route_rows, 1 - sec)]
-    sends, weights = lax.optimization_barrier((sends, weights))
-    gots = [swap_section(a) for a in sends]
-    weights, gots = lax.optimization_barrier((weights, gots))
-    small_got, memory_got, routes_got = gots
+    small_got, memory_got, routes_got = [swap_section(a) for a in sends]
 
     def both_layers(own, got):
         return jnp.where(first, own, got), jnp.where(first, got, own)
@@ -751,10 +758,14 @@
     smalls = both_layers(small, small_got)
     route_sets = both_layers(pick(route_rows, sec), routes_got)
     memories = both_layers(pick(memory[0], sec), memory_got)
-    weight_sets = [both_layers(a, got) for a, got in zip(weights, swap_weights(weights))]
+    weights_got = swap_weights(list(zip(weights, (1, 1, 1, 1, 1))), sends)
+    weight_sets = [both_layers(a, got) for a, got in zip(weights, weights_got)]
 
     x = pick(inputs, sec)
     cot = pick(out_cot, sec)
+    own_norm = norm_only(x, smalls[0][0:1], smalls[0][1:2])
+    slots = gather_slots(own_norm)
+    route_sets = after(route_sets, own_norm)
     topk = value_routes.shape[-1]
 
     layers = []
@@ -769,7 +780,7 @@
                 shift2=vec[3:4],
                 up_b=vec[4:5],
                 down_b=vec[5:6],
-                w=(weight_sets[1][number], weight_sets[0][number], weight_sets[2][number]),
+                w=(weight_sets[0][number], weight_sets[1][number], weight_sets[2][number]),
                 wu=weight_sets[3][number],
                 wd=weight_sets[4][number],
                 mask=route_mask(routes[:topk], routes[topk:, memory_len:], experts, memory_len),
@@ -778,11 +789,10 @@
         )
     no_add = jnp.zeros_like(layers[0]["gain1"])
 
-    own_norm = norm_only(x, layers[0]["gain1"], layers[0]["shift1"])
-    slots = gather_slots(own_norm)
     for layer in layers:
-        layer["mem_slots"] = gather_slots(norm_only(layer["mem"], layer["gain1"], layer["shift1"]))
-    cot_slots = gather_slots(cot)
+        layer["mem_slots"] = gather_slots(norm_only(after(layer["mem"], own_norm), layer["gain1"], layer["shift1"]))
+    cot_slots = gather_slots(after(cot, slots[2], layers[0]["mem_slots"][2]))
+    slots[3] = after(slots[3], layers[0]["mask"], layers[1]["mask"])
 
     saves = []
     rows_in = x
@@ -791,21 +801,28 @@
         *out, normed, q, k, v, ev, gate, att, mixed = attn_fwd(
             me, layer["mem_slots"], slots, layer["w"], layer["mask"], experts, head_width
         )
+        if number == 0:
+            out[3] = after(out[3], cot_slots[2], layers[1]["mem_slots"][2])
         terms = scatter_slots(out)
         hidden, own_norm2 = add_norm(rows_in, terms, no_add, layer["gain2"], layer["shift2"], f32)
-        n2_slots = gather_slots(own_norm2)
-        near_a, near_b, *kept = ffn_fwd(n2_slots[0:2], 0, layer["wu"], layer["up_b"], layer["wd"], ())
-        far_a, far_b, n2, upper, active = ffn_fwd(n2_slots[2:4], 1, layer["wu"], layer["up_b"], layer["wd"], kept)
-        terms = scatter_slots([near_a, near_b, far_a, far_b])
-        next_layer = layers[min(number + 1, 1)]
-        result, own_norm = add_norm(hidden, terms, layer["down_b"], next_layer["gain1"], next_layer["shift1"], bf16)
-        layer_outs.append(result)
+        wu, wd = layer["wu"], layer["wd"]
+
+        def near_work(near):
+            done = ffn_fwd(near, 0, wu, layer["up_b"], wd, ())
+            return done, (ffn_bwd(cot_slots[0:2], 0, done[3], wd, wu, ()) if number == 1 else ())
+
+        n2_slots, ((near_a, near_b, *kept), near_back) = gather_slots(own_norm2, near_work)
+        far_a, far_b, n2, upper, active = ffn_fwd(n2_slots[2:4], 1, wu, layer["up_b"], wd, kept)
         saves.append(
             dict(rows=rows_in, normed=normed, attn=(q, k, v, ev, gate, att), mixed=mixed, hidden=hidden, n2=n2, upper=upper, active=active)
         )
         if number == 0:
-            rows_in = result
+            terms = scatter_slots([near_a, near_b, far_a, far_b])
+            rows_in, own_norm = add_norm(hidden, terms, layer["down_b"], layers[1]["gain1"], layers[1]["shift1"], bf16)
+            layer_outs.append(rows_in)
             slots = gather_slots(own_norm)
+        else:
+            last_parts = [near_a, near_b, far_a, far_b]
 
     def by_layer(one, two):
         got = swap_section(jnp.where(first, two, one))
@@ -813,13 +830,13 @@
         return jnp.stack([jnp.where(first, kept, got), jnp.where(first, got, kept)])[None]
 
     def send_chunks(one, two, pieces):
-        gots, owns = [], []
+        chunks = []
         for part_one, part_two in zip(cut(one, pieces), cut(two, pieces)):
-            gots.append(jnp.where(first, part_two, part_one))
-            owns.append(jnp.where(first, part_one, part_two))
-        return gots, owns
-
-    layer_out = by_layer(*layer_outs)
+            send = jnp.where(first, part_two, part_one)
+            sums.add(jnp.where(first, part_one, part_two), swap_section(send))
+            chunks.append(send)
+        return chunks
+
     sums = ChunkSums()
     grads = [{}, {}]
     smalls_out = [None, None]
@@ -828,51 +845,59 @@
     g_slots = cot_slots
     for number in (1, 0):
         layer, saved, grad = layers[number], saves[number], grads[number]
-        near_a, near_b, near_bias, *kept = ffn_bwd(g_slots[0:2], 0, saved["upper"], layer["wd"], layer["wu"], ())
-        far_a, far_b, far_bias, g_all, upper_grad = ffn_bwd(g_slots[2:4], 1, saved["upper"], layer["wd"], layer["wu"], kept)
-        grad["down"] = t_dot(saved["active"], g_all).astype(bf16)
-        grad["up"] = t_dot(saved["n2"], upper_grad).astype(bf16)
+        wu, wd = layer["wu"], layer["wd"]
         if number == 0:
-            down_sends, down_owns = send_chunks(grads[0]["down"], grads[1]["down"], 2)
-            up_sends, up_owns = send_chunks(grads[0]["up"], grads[1]["up"], 2)
-            up_sends = after(up_sends, down_sends)
-            beside = (down_sends, up_sends)
-        else:
-            beside = (grad["down"], grad["up"])
-        terms, beside = scatter_slots([near_a, near_b, far_a, far_b], beside)
-        if number == 0:
-            for own, send in zip((*down_owns, *up_owns), (*down_sends, *up_sends)):
-                sums.add(own, swap_section(send))
-        else:
-            grad["down"], grad["up"] = beside
+            near_work = lambda near: ffn_bwd(near, 0, saved["upper"], wd, wu, ())
+            g_slots, near_back = gather_slots(g_rows, near_work)
+        near_a, near_b, near_bias, *kept = near_back
+        far_a, far_b, far_bias, g_all, upper_grad = ffn_bwd(g_slots[2:4], 1, saved["upper"], wd, wu, kept)
+
+        def feed_grads(token):
+            grad["down"] = t_dot(saved["active"], after(g_all, token)).astype(bf16)
+            sent = send_chunks(grad["down"], grads[1]["down"], 2) if number == 0 else grad["down"]
+            grad["up"] = t_dot(saved["n2"], after(upper_grad, token, sent)).astype(bf16)
+            return sent, (send_chunks(grad["up"], grads[1]["up"], 2) if number == 0 else grad["up"])
+
+        terms, (down_done, up_done) = scatter_slots([near_a, near_b, far_a, far_b], feed_grads)
+        if number == 1:
+            grad["down"], grad["up"] = down_done, up_done
         hidden_grad, hidden_low, small2 = norm_back(saved["hidden"], terms, layer["gain2"], g_rows)
         a_slots = gather_slots(hidden_low)
         if number == 0:
             sums.turn(0)
+            a_slots[3] = sums.before(a_slots[3])
+        else:
+            last_terms = scatter_slots(last_parts, start_after=a_slots[2])
+        *ngs, ngm, dproj, a_all = attn_bwd(me, a_slots, layer["w"], saved["attn"], experts, head_width)
+        if number == 1:
+            ngs[3] = after(ngs[3], last_terms[2])
+            last_out, _ = add_norm(saved["hidden"], last_terms, layer["down_b"], layer["gain1"], layer["shift1"], bf16)
+            layer_out = by_layer(layer_outs[0], last_out)
+
+        def attn_grads(token):
+            mixed = saved["mixed"] if token is None else after(saved["mixed"], token)
+            grad["out"] = squeeze_out(t_dot(mixed, a_all).astype(bf16), experts, head_width)
+            sent = send_chunks(grad["out"], grads[1]["out"], 1) if number == 0 else grad["out"]
+            grad["pack"] = squeeze(t_dot(after(dproj, sent), saved["normed"]).astype(bf16), experts, head_width)
+            return sent, (send_chunks(grad["pack"], grads[1]["pack"], 2) if number == 0 else grad["pack"])
+
+        if number == 1:
+            seq_terms, (grad["out"], grad["pack"], layer_out) = scatter_slots(ngs, lambda token: (*attn_grads(token), layer_out))
+        else:
+            sums.token = ngs[3]
+            sums.turn(0)
             sums.turn(1)
-            a_slots[3] = sums.before(a_slots[3])
-        *ngs, ngm, dproj, a_all = attn_bwd(me, a_slots, layer["w"], saved["attn"], experts, head_width)
-        grad["out"] = squeeze_out(t_dot(saved["mixed"], a_all).astype(bf16), experts, head_width)
-        grad["pack"] = squeeze(t_dot(dproj, saved["normed"]).astype(bf16), experts, head_width)
-        if number == 0:
-            out_sends, out_owns = send_chunks(grads[0]["out"], grads[1]["out"], 1)
-            pack_sends, pack_owns = send_chunks(grads[0]["pack"], grads[1]["pack"], 2)
-            pack_sends = after(pack_sends, out_sends)
-            beside = (out_sends, pack_sends)
-        else:
-            beside = (grad["out"], grad["pack"], layer_out)
-        seq_terms, beside = scatter_slots(ngs, beside)
+
+            def rest(token):
+                sent = attn_grads(token)
+                sums.token = sent
+                sums.turn(2)
+                sums.turn(0)
+                sums.turn(1)
+                return sums.token
+
+            seq_terms, _ = scatter_slots([*ngs[0:3], sums.before(ngs[3])], rest)
         mem_terms = scatter_slots(cut(ngm, 4))
-        if number == 0:
-            for own, send in zip((*out_owns, *pack_owns), (*out_sends, *pack_sends)):
-                sums.add(own, swap_section(send))
-            sums.token = ngs[0]
-            sums.turn(0)
-            sums.turn(2)
-            sums.turn(1)
-            seq_terms = (*seq_terms[0:2], sums.before(seq_terms[2]))
-        else:
-            grad["out"], grad["pack"], layer_out = beside
         input_grad, input_low, small1 = norm_back(saved["rows"], seq_terms, layer["gain1"], hidden_grad)
         small_mem = norm_back_small(layer["mem"], mem_terms)
         input_grads[number] = input_low
@@ -880,20 +905,20 @@
         vec = vec + to_core(vec)
         vec = vec + to_chip(vec)
         smalls_out[number] = jnp.concatenate([vec[0:5], near_bias + far_bias, vec[6:8]], axis=0)
-        if number == 1:
-            g_rows = input_low
-            g_slots = gather_slots(input_low)
+        g_rows = input_low
 
     vec_own = jnp.where(first, smalls_out[0], smalls_out[1])
     vec_got = swap_section(jnp.where(first, smalls_out[1], smalls_out[0]))
     last_chunk = sums.chunks[-1]
     last_chunk["own"], last_chunk["moving"] = (last_chunk["own"], vec_own), (last_chunk["moving"], vec_got)
     for newest in range(3, len(sums.chunks) + 3):
-        for number in range(min(newest, len(sums.chunks) - 1), -1, -1):
-            if sums.chunks[number]["step"] < 4:
+        for number in range(newest, newest - 4, -1):
+            if 0 <= number < len(sums.chunks):
                 sums.turn(number)
+        if newest == len(sums.chunks) - 1:
+            last_sum = sums.chunks[-1]["own"]
     *chunks, (last, vec) = [chunk["end"] for chunk in sums.chunks]
-    input_grad = by_layer(*input_grads)
+    input_grad = by_layer(*[after(a, last_sum) for a in input_grads])
     down_sum = jnp.concatenate(chunks[0:2], axis=0).astype(f32)
     up_sum = jnp.concatenate(chunks[2:4], axis=0).astype(f32)
     out_sum = chunks[4].astype(f32)

time: 721 us -> 625 us (0.87)
  waiting for transfers between devices: 333 us -> 237 us
    ppermute x22, waiting for transfers between devices: 148 us -> 73.3 us  [to_chip(): return lax.ppermute(a, 'head', chip_pairs)]
    ppermute x18, waiting for transfers between devices: 66.2 us -> 49.7 us  [swap_section(): return lax.ppermute(a, 'section', [(0, 1), (1, 0)])]
    ppermute x42, waiting for transfers between devices: 3.1 us -> 15.4 us  [to_core(): return lax.ppermute(a, 'head', core_pairs)]
    ppermute x24, waiting for transfers between devices: 89.9 us -> 79.7 us  [move(): return jax.tree.map(lambda one: lax.ppermute(one, axis, pairs), a)]
    ppermute x24, starting transfers between devices: 62.7 us -> 55.4 us  [move(): return jax.tree.map(lambda one: lax.ppermute(one, axis, pairs), a)]
  transfers between devices with their start and end apart: 111 -> 111, of which waited for: 40 -> 47; matrix products, arithmetic and copies ran while one was open for 13% -> 17% of each run, Pallas kernels for 12% -> 14%
where the time goes in v3:
time: 625 us; the launch traced here: 619 us
  waiting for transfers between devices  237 us (38%)
  Pallas kernels  134 us (21%)
  starting transfers between devices  124 us (20%)
  other arithmetic  71.8 us (11%)
  matrix products  28.5 us (5%)
  local copies, waits for them, and re-layouts  21.1 us (3%)
    ppermute x24, waiting for transfers between devices, move(): return jax.tree.map(lambda one: lax.ppermute(one, axis, pairs), a)  79.7 us
    ppermute x22, waiting for transfers between devices, to_chip(): return lax.ppermute(a, 'head', chip_pairs)  73.3 us
    ppermute x24, starting transfers between devices, move(): return jax.tree.map(lambda one: lax.ppermute(one, axis, pairs), a)  55.4 us
    ppermute x18, waiting for transfers between devices, swap_section(): return lax.ppermute(a, 'section', [(0, 1), (1, 0)])  49.7 us
    pallas_call x2, Pallas kernels, attn_fwd(): pl.pallas_call(functools.partial(attn_fwd_kernel, experts, head_width), g...  38.3 us
    pallas_call x2, Pallas kernels, attn_bwd(): pl.pallas_call(functools.partial(attn_bwd_kernel, experts, head_width), g...  32.2 us
    ppermute x22, starting transfers between devices, to_chip(): return lax.ppermute(a, 'head', chip_pairs)  29.9 us
    dot_general x8, matrix products, t_dot(): lax.dot_general(a, b, (((0,), (0,)), ((), ())), preferred_element_type=f32)  28.5 us
  transfers between devices with their start and end apart: 111, of which 47 were waited for; matrix products, arithmetic and copies ran while one was open for 17% of the time, Pallas kernels for 14%

profile of v3, /device:TPU:0, one launch (start us, length us, event | category | flops | bytes accessed | tf_op | source)
XLA Modules:
  0.0 619.0 jit_solution(16853393107606469073)
XLA Ops:
  56.2 7.3 %collective-permute-done.14 = bf16[280,1024]{1,0:T(8,128)(2,1)S(1)} collective-permute-done((bf16[280,1024]{1,0:T(8,128)(2,1)S(1)}, bf16[280,1024]{1,0:T(8,128)(2,1)S(1)}, u32[]{:S(2)}, u32[]{:S(2)}) %collective-permute-start.14) | collective-permute-done | bytes 573472 | tf_op jit(solution)/shard_map/ppermute | solution.py:693
  73.3 15.0 %attn_fwd.2 = (bf16[256,1024]{1,0:T(8,128)(2,1)S(1)}, bf16[256,1024]{1,0:T(8,128)(2,1)S(1)}, bf16[256,1024]{1,0:T(8,128)(2,1)S(1)}, bf16[256,1024]{1,0:T(8,128)(...) custom-call(s32[1]{0:T(128)} %bitcast.me_ref, ...), custom_call_target="tpu_custom_call" | custom-call | flops 3355443200 | bytes 16777216 | tf_op jit(solution)/shard_map/attn_fwd/pallas_call | solution.py:351
  100.3 9.4 %collective-permute-done.19.c_ref = bf16[256,1024]{1,0:T(8,128)(2,1)S(1)} collective-permute-done((bf16[256,1024]{1,0:T(8,128)(2,1)S(1)}, bf16[256,1024]{1,0:T(8,128)(2,1)S(1)}, u32[]{:S(2)}, u32[]{:S(2)}) %collective-permute-start.19) | collective-permute-done | bytes 524320 | tf_op jit(solution)/shard_map/ppermute | solution.py:54
  111.9 6.0 collective-permute-done.25
  130.1 6.0 ffn_fwd.5
  139.8 12.4 %collective-permute-done.29.c_ref = bf16[256,1024]{1,0:T(8,128)(2,1)S(1)} collective-permute-done((bf16[256,1024]{1,0:T(8,128)(2,1)S(1)}, bf16[256,1024]{1,0:T(8,128)(2,1)S(1)}, u32[]{:S(2)}, u32[]{:S(2)}) %collective-permute-start.29) | collective-permute-done | bytes 524320 | tf_op jit(solution)/shard_map/ppermute | solution.py:54
  154.4 11.6 %collective-permute-done.33.p2_ref = bf16[256,1024]{1,0:T(8,128)(2,1)S(1)} collective-permute-done((bf16[256,1024]{1,0:T(8,128)(2,1)S(1)}, bf16[256,1024]{1,0:T(8,128)(2,1)S(1)}, u32[]{:S(2)}, u32[]{:S(2)}) %collective-permute-start.33) | collective-permute-done | bytes 524320 | tf_op jit(solution)/shard_map/ppermute | solution.py:54
  169.3 23.2 %attn_fwd.3 = (bf16[256,1024]{1,0:T(8,128)(2,1)S(1)}, bf16[256,1024]{1,0:T(8,128)(2,1)S(1)}, bf16[256,1024]{1,0:T(8,128)(2,1)S(1)}, bf16[256,1024]{1,0:T(8,128)(...) custom-call(s32[1]{0:T(128)} %bitcast.me_ref, ...), custom_call_target="tpu_custom_call" | custom-call | flops 3355443200 | bytes 16777216 | tf_op jit(solution)/shard_map/attn_fwd/pallas_call | solution.py:351
  196.3 12.4 %collective-permute-done.37.c_ref = bf16[256,1024]{1,0:T(8,128)(2,1)S(1)} collective-permute-done((bf16[256,1024]{1,0:T(8,128)(2,1)S(1)}, bf16[256,1024]{1,0:T(8,128)(2,1)S(1)}, u32[]{:S(2)}, u32[]{:S(2)}) %collective-permute-start.37) | collective-permute-done | bytes 524320 | tf_op jit(solution)/shard_map/ppermute | solution.py:54
  225.8 6.0 ffn_fwd.7
  231.8 7.1 %ffn_bwd.5 = (bf16[256,1024]{1,0:T(8,128)(2,1)S(1)}, bf16[256,1024]{1,0:T(8,128)(2,1)S(1)}, f32[1,1024]{1,0:T(1,128)S(1)}, bf16[1024,1024]{1,0:T(8,128)(2,1)}, bf16[1024,1024]{1,0:T(8,128)(2,1)}) custom-call(bf16[256,1024]{1,0:T(8,128)(2,1)S(1)} %collective-permute-done.16.a_ref, ...), custom_call_target="tpu_custom_call", output_to_operand_aliasing={{3}: (5, {}), {4}: (6, {})} | custom-call | flops 2147483648 | bytes 9437184 | tf_op jit(solution)/shard_map/ffn_bwd/pallas_call | solution.py:595
  242.6 6.1 convolution_convert_fusion.5
  259.3 11.1 %collective-permute-done.47.d2_ref = bf16[256,1024]{1,0:T(8,128)(2,1)S(1)} collective-permute-done((bf16[256,1024]{1,0:T(8,128)(2,1)S(1)}, bf16[256,1024]{1,0:T(8,128)(2,1)S(1)}, u32[]{:S(2)}, u32[]{:S(2)}) %collective-permute-start.47) | collective-permute-done | bytes 524320 | tf_op jit(solution)/shard_map/ppermute | solution.py:54
  273.5 16.3 %attn_bwd.2 = (bf16[256,1024]{1,0:T(8,128)(2,1)S(1)}, bf16[256,1024]{1,0:T(8,128)(2,1)S(1)}, bf16[256,1024]{1,0:T(8,128)(2,1)S(1)}, bf16[256,1024]{1,0:T(8,128)(...) custom-call(s32[1]{0:T(128)} %bitcast.me_ref, ...), custom_call_target="tpu_custom_call" | custom-call | flops 3355443200 | bytes 16777216 | tf_op jit(solution)/shard_map/attn_bwd/pallas_call | solution.py:518
  319.2 6.5 %collective-permute-done.56.a_ref = bf16[256,1024]{1,0:T(8,128)(2,1)S(1)} collective-permute-done((bf16[256,1024]{1,0:T(8,128)(2,1)S(1)}, bf16[256,1024]{1,0:T(8,128)(2,1)S(1)}, u32[]{:S(2)}, u32[]{:S(2)}) %collective-permute-start.56) | collective-permute-done | bytes 524320 | tf_op jit(solution)/shard_map/ppermute | solution.py:54
  327.6 6.9 %ffn_bwd.7 = (bf16[256,1024]{1,0:T(8,128)(2,1)S(1)}, bf16[256,1024]{1,0:T(8,128)(2,1)S(1)}, f32[1,1024]{1,0:T(1,128)S(1)}, bf16[1024,1024]{1,0:T(8,128)(2,1)}, bf16[1024,1024]{1,0:T(8,128)(2,1)}) custom-call(bf16[256,1024]{1,0:T(8,128)(2,1)S(1)} %collective-permute-done.56.a_ref, ...), custom_call_target="tpu_custom_call", output_to_operand_aliasing={{3}: (5, {}), {4}: (6, {})} | custom-call | flops 2147483648 | bytes 9437184 | tf_op jit(solution)/shard_map/ffn_bwd/pallas_call | solution.py:595
  354.1 15.3 %collective-permute-done.65 = bf16[512,1024]{1,0:T(8,128)(2,1)} collective-permute-done((bf16[512,1024]{1,0:T(8,128)(2,1)}, bf16[512,1024]{1,0:T(8,128)(2,1)}, u32[]{:S(2)}, u32[]{:S(2)}) %collective-permute-start.65) | collective-permute-done | bytes 1048608 | tf_op jit(solution)/shard_map/ppermute | solution.py:58
  382.4 15.9 %attn_bwd.3 = (bf16[256,1024]{1,0:T(8,128)(2,1)S(1)}, bf16[256,1024]{1,0:T(8,128)(2,1)S(1)}, bf16[256,1024]{1,0:T(8,128)(2,1)S(1)}, bf16[256,1024]{1,0:T(8,128)(...) custom-call(s32[1]{0:T(128)} %bitcast.me_ref, ...), custom_call_target="tpu_custom_call" | custom-call | flops 3355443200 | bytes 16777216 | tf_op jit(solution)/shard_map/attn_bwd/pallas_call | solution.py:518
  474.6 8.4 %collective-permute-done.109 = bf16[512,1024]{1,0:T(8,128)(2,1)S(1)} collective-permute-done((bf16[512,1024]{1,0:T(8,128)(2,1)}, bf16[512,1024]{1,0:T(8,128)(2,1)S(1)}, u32[]{:S(2)}, u32[]{:S(2)}) %collective-permute-start.109) | collective-permute-done | bytes 1048608 | tf_op jit(solution)/shard_map/ppermute | solution.py:620
  501.5 6.4 %collective-permute-done.110 = bf16[512,1024]{1,0:T(8,128)(2,1)S(1)} collective-permute-done((bf16[512,1024]{1,0:T(8,128)(2,1)S(1)}, bf16[512,1024]{1,0:T(8,128)(2,1)S(1)}, u32[]{:S(2)}, u32[]{:S(2)}) %collective-permute-start.110) | collective-permute-done | bytes 1048608 | tf_op jit(solution)/shard_map/ppermute | solution.py:620
  521.8 9.5 %collective-permute-start.96 = (bf16[400,1024]{1,0:T(8,128)(2,1)S(1)}, bf16[400,1024]{1,0:T(8,128)(2,1)S(1)}, u32[]{:S(2)}, u32[]{:S(2)}) collective-permute-start(bf16[400,1024]{1,0:T(8,128)(2,1)S(1)} %add_convert_fusion.19), channel_id=1, source_target_pairs={{0,1},{3,2},{4,5},{7,6},{8,9},{11,10},{12,13},{15,14},{16,17},{19,... | collective-permute-start | bytes 2457608 | tf_op jit(solution)/shard_map/ppermute | solution.py:620
  540.6 8.6 %collective-permute-done.97 = f32[8,1024]{1,0:T(8,128)S(1)} collective-permute-done((f32[8,1024]{1,0:T(8,128)S(1)}, f32[8,1024]{1,0:T(8,128)S(1)}, u32[]{:S(2)}, u32[]{:S(2)}) %collective-permute-start.97) | collective-permute-done | bytes 32800 | tf_op jit(solution)/shard_map/ppermute | solution.py:620
  560.6 40.4 %collective-permute-done.105 = bf16[400,1024]{1,0:T(8,128)(2,1)S(1)} collective-permute-done((bf16[400,1024]{1,0:T(8,128)(2,1)S(1)}, bf16[400,1024]{1,0:T(8,128)(2,1)S(1)}, u32[]{:S(2)}, u32[]{:S(2)}) %collective-permute-start.105) | collective-permute-done | bytes 819232 | tf_op jit(solution)/shard_map/ppermute | solution.py:620
  602.7 11.2 %collective-permute-done.104 = f32[8,1024]{1,0:T(8,128)S(1)} collective-permute-done((f32[8,1024]{1,0:T(8,128)S(1)}, f32[8,1024]{1,0:T(8,128)S(1)}, u32[]{:S(2)}, u32[]{:S(2)}) %collective-permute-start.104) | collective-permute-done | bytes 32800 | tf_op jit(solution)/shard_map/ppermute | solution.py:620
  (500 shorter events, 337.5 us)
Async XLA Ops:
  7.6 26.5 %collective-permute-start = (bf16[64,1024]{1,0:T(8,128)(2,1)}, bf16[64,1024]{1,0:T(8,128)(2,1)}, u32[]{:S(2)}, u32[]{:S(2)}) collective-permute-start(bf16[64,1024]{1,0:T(8,128)(2,1)} %dynamic-slice_bitcast_fusion.2), channel_id=1, source_target_pairs={{0,16},{16,0},{1,17},{17,1},{2,18},{18,2},{3,19},{19,3},{4,20},{20... | collective-permute-start | bytes 393224 | tf_op jit(solution)/shard_map/ppermute | solution.py:58
  19.9 53.5 %collective-permute-start.5 = (bf16[256,1024]{1,0:T(8,128)(2,1)S(1)}, bf16[256,1024]{1,0:T(8,128)(2,1)}, u32[]{:S(2)}, u32[]{:S(2)}) collective-permute-start(bf16[256,1024]{1,0:T(8,128)(2,1)S(1)} %norm_only.3.p0_ref), channel_id=1, source_target_pairs={{0,4},{4,0},{8,12},{12,8},{1,5},{5,1},{9,13},{13,9},{2,6},{6,2},{1... | collective-permute-start | bytes 1572872 | tf_op jit(solution)/shard_map/ppermute | solution.py:50
  46.0 26.1 %collective-permute-start.22 = (bf16[512,1024]{1,0:T(8,128)(2,1)S(1)}, bf16[512,1024]{1,0:T(8,128)(2,1)S(1)}, u32[]{:S(2)}, u32[]{:S(2)}) collective-permute-start(bf16[512,1024]{1,0:T(8,128)(2,1)S(1)} %constant_dynamic-slice_fusion.1), channel_id=1, source_target_pairs={{0,16},{16,0},{1,17},{17,1},{2,18},{18,2},{3,19},{19,3},{4,20},{20... | collective-permute-start | bytes 3145736 | tf_op jit(solution)/shard_map/ppermute | solution.py:58
  65.1 28.1 %collective-permute-start.24 = (bf16[512,1024]{1,0:T(8,128)(2,1)}, bf16[512,1024]{1,0:T(8,128)(2,1)}, u32[]{:S(2)}, u32[]{:S(2)}) collective-permute-start(bf16[512,1024]{1,0:T(8,128)(2,1)} %constant_dynamic-slice_fusion), channel_id=1, source_target_pairs={{0,16},{16,0},{1,17},{17,1},{2,18},{18,2},{3,19},{19,3},{4,20},{20... | collective-permute-start | bytes 3145736 | tf_op jit(solution)/shard_map/ppermute | solution.py:58
  354.1 27.5 %collective-permute-start.62 = (bf16[256,1024]{1,0:T(8,128)(2,1)S(1)}, bf16[256,1024]{1,0:T(8,128)(2,1)S(1)}, u32[]{:S(2)}, u32[]{:S(2)}) collective-permute-start(bf16[256,1024]{1,0:T(8,128)(2,1)S(1)} %get-tuple-element.317.d0_ref), channel_id=1, source_target_pairs={{0,4},{4,0},{8,12},{12,8},{1,5},{5,1},{9,13},{13,9},{2,6},{6,2},{1... | collective-permute-start | bytes 1572872 | tf_op jit(solution)/shard_map/ppermute | solution.py:50
  377.8 29.9 %collective-permute-start.75 = (bf16[64,1024]{1,0:T(8,128)(2,1)S(1)}, bf16[64,1024]{1,0:T(8,128)(2,1)S(1)}, u32[]{:S(2)}, u32[]{:S(2)}) collective-permute-start(bf16[64,1024]{1,0:T(8,128)(2,1)S(1)} %get-tuple-element.450), channel_id=1, source_target_pairs={{0,4},{4,0},{8,12},{12,8},{1,5},{5,1},{9,13},{13,9},{2,6},{6,2},{1... | collective-permute-start | bytes 393224 | tf_op jit(solution)/shard_map/ppermute | solution.py:50
  380.8 26.9 %collective-permute-start.77 = (bf16[64,1024]{1,0:T(8,128)(2,1)S(1)}, bf16[64,1024]{1,0:T(8,128)(2,1)S(1)}, u32[]{:S(2)}, u32[]{:S(2)}) collective-permute-start(bf16[64,1024]{1,0:T(8,128)(2,1)S(1)} %add_convert_fusion.30), channel_id=1, source_target_pairs={{0,8},{8,0},{4,12},{12,4},{1,9},{9,1},{5,13},{13,5},{2,10},{10,2},... | collective-permute-start | bytes 393224 | tf_op jit(solution)/shard_map/ppermute | solution.py:54
  409.4 26.4 %collective-permute-start.73 = (bf16[512,1024]{1,0:T(8,128)(2,1)}, bf16[512,1024]{1,0:T(8,128)(2,1)}, u32[]{:S(2)}, u32[]{:S(2)}) collective-permute-start(bf16[512,1024]{1,0:T(8,128)(2,1)} %get-tuple-element.413), channel_id=1, source_target_pairs={{0,16},{16,0},{1,17},{17,1},{2,18},{18,2},{3,19},{19,3},{4,20},{20... | collective-permute-start | bytes 3145736 | tf_op jit(solution)/shard_map/ppermute | solution.py:58
  410.9 47.4 %collective-permute-start.86 = (bf16[512,1024]{1,0:T(8,128)(2,1)}, bf16[512,1024]{1,0:T(8,128)(2,1)}, u32[]{:S(2)}, u32[]{:S(2)}) collective-permute-start(bf16[512,1024]{1,0:T(8,128)(2,1)} %get-tuple-element.412), channel_id=1, source_target_pairs={{0,16},{16,0},{1,17},{17,1},{2,18},{18,2},{3,19},{19,3},{4,20},{20... | collective-permute-start | bytes 3145736 | tf_op jit(solution)/shard_map/ppermute | solution.py:58
  411.4 35.8 %collective-permute-start.66 = (bf16[256,1024]{1,0:T(8,128)(2,1)S(1)}, bf16[256,1024]{1,0:T(8,128)(2,1)S(1)}, u32[]{:S(2)}, u32[]{:S(2)}) collective-permute-start(bf16[256,1024]{1,0:T(8,128)(2,1)S(1)} %get-tuple-element.326), channel_id=1, source_target_pairs={{0,4},{4,0},{8,12},{12,8},{1,5},{5,1},{9,13},{13,9},{2,6},{6,2},{1... | collective-permute-start | bytes 1572872 | tf_op jit(solution)/shard_map/ppermute | solution.py:50
  415.0 28.7 %collective-permute-start.71 = (bf16[512,1024]{1,0:T(8,128)(2,1)}, bf16[512,1024]{1,0:T(8,128)(2,1)S(1)}, u32[]{:S(2)}, u32[]{:S(2)}) collective-permute-start(bf16[512,1024]{1,0:T(8,128)(2,1)} %add_convert_fusion.12), channel_id=1, source_target_pairs={{0,1},{3,2},{4,5},{7,6},{8,9},{11,10},{12,13},{15,14},{16,17},{19,... | collective-permute-start | bytes 3145736 | tf_op jit(solution)/shard_map/ppermute | solution.py:620
  440.0 28.3 %collective-permute-start.90 = (bf16[512,1024]{1,0:T(8,128)(2,1)}, bf16[512,1024]{1,0:T(8,128)(2,1)}, u32[]{:S(2)}, u32[]{:S(2)}) collective-permute-start(bf16[512,1024]{1,0:T(8,128)(2,1)} %add_convert_fusion.11), channel_id=1, source_target_pairs={{0,1},{3,2},{4,5},{7,6},{8,9},{11,10},{12,13},{15,14},{16,17},{19,... | collective-permute-start | bytes 3145736 | tf_op jit(solution)/shard_map/ppermute | solution.py:620
  445.1 26.7 %collective-permute-start.89 = (bf16[512,1024]{1,0:T(8,128)(2,1)}, bf16[512,1024]{1,0:T(8,128)(2,1)}, u32[]{:S(2)}, u32[]{:S(2)}) collective-permute-start(bf16[512,1024]{1,0:T(8,128)(2,1)} %add_convert_fusion.9), channel_id=1, source_target_pairs={{1,2},{2,1},{5,6},{6,5},{9,10},{10,9},{13,14},{14,13},{17,18},{18,... | collective-permute-start | bytes 3145736 | tf_op jit(solution)/shard_map/ppermute | solution.py:620
  451.7 32.8 %collective-permute-start.88 = (bf16[560,1024]{1,0:T(8,128)(2,1)}, bf16[560,1024]{1,0:T(8,128)(2,1)}, u32[]{:S(2)}, u32[]{:S(2)}) collective-permute-start(bf16[560,1024]{1,0:T(8,128)(2,1)} %broadcast_select_fusion.4), channel_id=1, source_target_pairs={{0,16},{16,0},{1,17},{17,1},{2,18},{18,2},{3,19},{19,3},{4,20},{20... | collective-permute-start | bytes 3440648 | tf_op jit(solution)/shard_map/ppermute | solution.py:58
  468.3 32.0 %collective-permute-start.93 = (bf16[400,1024]{1,0:T(8,128)(2,1)S(1)}, bf16[400,1024]{1,0:T(8,128)(2,1)S(1)}, u32[]{:S(2)}, u32[]{:S(2)}) collective-permute-start(bf16[400,1024]{1,0:T(8,128)(2,1)S(1)} %copy-done.44), channel_id=1, source_target_pairs={{0,16},{16,0},{1,17},{17,1},{2,18},{18,2},{3,19},{19,3},{4,20},{20... | collective-permute-start | bytes 2457608 | tf_op jit(solution)/shard_map/ppermute | solution.py:58
  483.0 38.3 %collective-permute-start.74 = (bf16[400,1024]{1,0:T(8,128)(2,1)S(1)}, bf16[400,1024]{1,0:T(8,128)(2,1)S(1)}, u32[]{:S(2)}, u32[]{:S(2)}) collective-permute-start(bf16[400,1024]{1,0:T(8,128)(2,1)S(1)} %copy-done.43), channel_id=1, source_target_pairs={{0,16},{16,0},{1,17},{17,1},{2,18},{18,2},{3,19},{19,3},{4,20},{20... | collective-permute-start | bytes 2457608 | tf_op jit(solution)/shard_map/ppermute | solution.py:58
  493.2 26.8 %collective-permute-start.85 = (f32[8,1024]{1,0:T(8,128)S(1)}, f32[8,1024]{1,0:T(8,128)S(1)}, u32[]{:S(2)}, u32[]{:S(2)}) collective-permute-start(f32[8,1024]{1,0:T(8,128)S(1)} %fusion.17), channel_id=1, source_target_pairs={{0,16},{16,0},{1,17},{17,1},{2,18},{18,2},{3,19},{19,3},{4,20},{20... | collective-permute-start | bytes 98312 | tf_op jit(solution)/shard_map/ppermute | solution.py:58
  508.0 31.0 %collective-permute-start.107 = (bf16[512,1024]{1,0:T(8,128)(2,1)S(1)}, bf16[512,1024]{1,0:T(8,128)(2,1)S(1)}, u32[]{:S(2)}, u32[]{:S(2)}) collective-permute-start(bf16[512,1024]{1,0:T(8,128)(2,1)S(1)} %add_convert_fusion.4), channel_id=1, source_target_pairs={{1,0},{2,3},{5,4},{6,7},{9,8},{10,11},{13,12},{14,15},{17,16},{18,... | collective-permute-start | bytes 3145736 | tf_op jit(solution)/shard_map/ppermute | solution.py:620
  520.0 35.1 %collective-permute-start.108 = (bf16[512,1024]{1,0:T(8,128)(2,1)S(1)}, bf16[512,1024]{1,0:T(8,128)(2,1)S(1)}, u32[]{:S(2)}, u32[]{:S(2)}) collective-permute-start(bf16[512,1024]{1,0:T(8,128)(2,1)S(1)} %add_convert_fusion.3), channel_id=1, source_target_pairs={{1,0},{2,3},{5,4},{6,7},{9,8},{10,11},{13,12},{14,15},{17,16},{18,... | collective-permute-start | bytes 3145736 | tf_op jit(solution)/shard_map/ppermute | solution.py:620
  521.8 27.5 %collective-permute-start.96 = (bf16[400,1024]{1,0:T(8,128)(2,1)S(1)}, bf16[400,1024]{1,0:T(8,128)(2,1)S(1)}, u32[]{:S(2)}, u32[]{:S(2)}) collective-permute-start(bf16[400,1024]{1,0:T(8,128)(2,1)S(1)} %add_convert_fusion.19), channel_id=1, source_target_pairs={{0,1},{3,2},{4,5},{7,6},{8,9},{11,10},{12,13},{15,14},{16,17},{19,... | collective-permute-start | bytes 2457608 | tf_op jit(solution)/shard_map/ppermute | solution.py:620
  550.4 50.7 %collective-permute-start.106 = (bf16[560,1024]{1,0:T(8,128)(2,1)S(1)}, bf16[560,1024]{1,0:T(8,128)(2,1)S(1)}, u32[]{:S(2)}, u32[]{:S(2)}) collective-permute-start(bf16[560,1024]{1,0:T(8,128)(2,1)S(1)} %add_convert_fusion), channel_id=1, source_target_pairs={{1,0},{2,3},{5,4},{6,7},{9,8},{10,11},{13,12},{14,15},{17,16},{18,... | collective-permute-start | bytes 3440648 | tf_op jit(solution)/shard_map/ppermute | solution.py:620
  552.1 48.9 %collective-permute-start.105 = (bf16[400,1024]{1,0:T(8,128)(2,1)S(1)}, bf16[400,1024]{1,0:T(8,128)(2,1)S(1)}, u32[]{:S(2)}, u32[]{:S(2)}) collective-permute-start(bf16[400,1024]{1,0:T(8,128)(2,1)S(1)} %add_convert_fusion.16), channel_id=1, source_target_pairs={{1,0},{2,3},{5,4},{6,7},{9,8},{10,11},{13,12},{14,15},{17,16},{18,... | collective-permute-start | bytes 2457608 | tf_op jit(solution)/shard_map/ppermute | solution.py:620
  555.6 58.3 %collective-permute-start.103 = (bf16[400,1024]{1,0:T(8,128)(2,1)S(1)}, bf16[400,1024]{1,0:T(8,128)(2,1)S(1)}, u32[]{:S(2)}, u32[]{:S(2)}) collective-permute-start(bf16[400,1024]{1,0:T(8,128)(2,1)S(1)} %add_convert_fusion.15), channel_id=1, source_target_pairs={{1,0},{2,3},{5,4},{6,7},{9,8},{10,11},{13,12},{14,15},{17,16},{18,... | collective-permute-start | bytes 2457608 | tf_op jit(solution)/shard_map/ppermute | solution.py:620
  559.3 54.5 %collective-permute-start.104 = (f32[8,1024]{1,0:T(8,128)S(1)}, f32[8,1024]{1,0:T(8,128)S(1)}, u32[]{:S(2)}, u32[]{:S(2)}) collective-permute-start(f32[8,1024]{1,0:T(8,128)S(1)} %add.263), channel_id=1, source_target_pairs={{1,0},{2,3},{5,4},{6,7},{9,8},{10,11},{13,12},{14,15},{17,16},{18,... | collective-permute-start | bytes 98312 | tf_op jit(solution)/shard_map/ppermute | solution.py:620
  (153 other events, 1695.5 us)

commit v4 on v3

v4 whole, which is shorter than its diff:
```python
import functools

import jax
import jax.numpy as jnp
from jax import lax
from jax.experimental import pallas as pl
from jax.experimental.pallas import tpu as pltpu
from jax.sharding import PartitionSpec as P

norm_eps = 1e-05
masked_score = -1e30
lanes = 128
out_lane = 8
log_lane = 16
bf16 = jnp.bfloat16
f32 = jnp.float32
gelu_c = 0.7978845608028654
gelu_a = 0.044715

core_pairs = [(0, 1), (1, 0), (2, 3), (3, 2)]
chip_pairs = [(0, 2), (2, 0), (1, 3), (3, 1)]


def dot(a, b):
    return lax.dot_general(a, b, (((1,), (0,)), ((), ())), preferred_element_type=f32)


def dot_t(a, b):
    return lax.dot_general(a, b, (((1,), (1,)), ((), ())), preferred_element_type=f32)


def t_dot(a, b):
    return lax.dot_general(a, b, (((0,), (0,)), ((), ())), preferred_element_type=f32)


def params(mebibytes=16):
    return pltpu.CompilerParams(vmem_limit_bytes=mebibytes * 1024 * 1024)


def whole_spec(shape):
    return pl.BlockSpec(shape, lambda *_: (0,) * len(shape))


def rows_spec(a, part, rows):
    index = part if a.shape[0] > rows else 0
    return pl.BlockSpec((rows, a.shape[1]), lambda *_: (index, 0))


in_vmem = pl.BlockSpec(memory_space=pltpu.VMEM)
in_smem = pl.BlockSpec(memory_space=pltpu.SMEM)
anywhere = pl.BlockSpec(memory_space=pl.ANY)


class Sender:
    def __init__(self, sems):
        self.sems, self.copies = sems, []

    def __call__(self, source, target):
        copy = pltpu.make_async_copy(source, target, self.sems.at[len(self.copies)])
        copy.start()
        self.copies.append(copy)

    def wait(self):
        for copy in self.copies:
            copy.wait()


def cost(flops, nbytes, trans=0):
    return pl.CostEstimate(flops=int(flops), bytes_accessed=int(nbytes), transcendentals=int(trans))


def to_core(a):
    return lax.ppermute(a, "head", core_pairs)


def to_chip(a):
    return lax.ppermute(a, "head", chip_pairs)


def swap_section(a):
    return lax.ppermute(a, "section", [(0, 1), (1, 0)])


def after(a, *tokens):
    return lax.optimization_barrier((a, tokens))[0]


def plus(a, b):
    return jax.tree.map(lambda one, two: (one.astype(f32) + two.astype(f32)).astype(one.dtype), a, b)


def gather_slots(own):
    from_chip = to_chip(own)
    from_core = to_core(own)
    return [own, from_core, from_chip, to_core(from_chip)]


def scatter_slots(parts):
    far = plus(parts[2], to_core(parts[3]))
    return (parts[0], to_core(parts[1]), to_chip(far)), far


def scatter_halves(parts, token=None):
    from_core_far = to_core(parts[3])
    from_core = to_core(parts[1])
    rows = parts[0].shape[0] // 2
    terms = []
    for part in range(2):
        here = slice(part * rows, (part + 1) * rows)
        far = plus(parts[2][here], from_core_far[here])
        if token is not None:
            far = after(far, token)
        token = far
        terms.append((parts[0], from_core, to_chip(far)))
    return terms, token


def norm_rows(x, gain, shift):
    average = jnp.mean(x, axis=-1, keepdims=True)
    centred = x - average
    variance = jnp.mean(centred * centred, axis=-1, keepdims=True)
    return centred * lax.rsqrt(variance + norm_eps) * gain + shift


def norm_kernel(x_ref, gain_ref, shift_ref, out_ref):
    out_ref[...] = norm_rows(x_ref[...].astype(f32), gain_ref[...], shift_ref[...]).astype(bf16)


def norm_only(x, gain, shift):
    return pl.pallas_call(
        norm_kernel,
        out_shape=jax.ShapeDtypeStruct(x.shape, bf16),
        compiler_params=params(),
        cost_estimate=cost(x.size * 8, x.size * 4),
        name="norm_only",
    )(x, gain, shift)


def add_norm_kernel(x_ref, a_ref, b_ref, c_ref, add_ref, gain_ref, shift_ref, sum_ref, out_ref):
    total = x_ref[...].astype(f32) + (a_ref[...].astype(f32) + b_ref[...].astype(f32) + c_ref[...].astype(f32))
    total = (total + add_ref[...]).astype(sum_ref.dtype)
    sum_ref[...] = total
    out_ref[...] = norm_rows(total.astype(f32), gain_ref[...], shift_ref[...]).astype(bf16)


def add_norm(x, terms, part, add, gain, shift, sum_type):
    rows, width = terms[2].shape
    return pl.pallas_call(
        add_norm_kernel,
        grid=(1,),
        in_specs=[rows_spec(a, part, rows) for a in (x, *terms)] + [whole_spec(add.shape)] * 3,
        out_specs=[whole_spec((rows, width))] * 2,
        out_shape=(jax.ShapeDtypeStruct((rows, width), sum_type), jax.ShapeDtypeStruct((rows, width), bf16)),
        compiler_params=params(),
        cost_estimate=cost(rows * width * 12, rows * width * 14),
        name="add_norm",
    )(x, *terms, add, gain, shift)


def norm_back_kernel(x_ref, a_ref, b_ref, c_ref, gain_ref, more_ref, dx_ref, low_ref, small_ref):
    x = x_ref[...].astype(f32)
    grad = a_ref[...].astype(f32) + b_ref[...].astype(f32) + c_ref[...].astype(f32)
    average = jnp.mean(x, axis=-1, keepdims=True)
    centred = x - average
    variance = jnp.mean(centred * centred, axis=-1, keepdims=True)
    scale = lax.rsqrt(variance + norm_eps)
    unit = centred * scale
    wide = grad * gain_ref[...]
    mean_wide = jnp.mean(wide, axis=-1, keepdims=True)
    mean_unit = jnp.mean(wide * unit, axis=-1, keepdims=True)
    more = more_ref[...].astype(f32)
    dx = more + scale * (wide - mean_wide - unit * mean_unit)
    dx_ref[...] = dx
    low_ref[...] = dx.astype(bf16)
    small_ref[0:1, :] = jnp.sum(grad * unit, axis=0, keepdims=True)
    small_ref[1:2, :] = jnp.sum(grad, axis=0, keepdims=True)
    small_ref[2:3, :] = jnp.sum(more, axis=0, keepdims=True)
    small_ref[3:8, :] = jnp.zeros((5, x.shape[1]), f32)


def norm_back(x, terms, part, gain, more):
    rows, width = terms[2].shape
    return pl.pallas_call(
        norm_back_kernel,
        grid=(1,),
        in_specs=[rows_spec(a, part, rows) for a in (x, *terms)] + [whole_spec(gain.shape), rows_spec(more, part, rows)],
        out_specs=[whole_spec((rows, width))] * 2 + [whole_spec((8, width))],
        out_shape=(
            jax.ShapeDtypeStruct((rows, width), f32),
            jax.ShapeDtypeStruct((rows, width), bf16),
            jax.ShapeDtypeStruct((8, width), f32),
        ),
        compiler_params=params(),
        cost_estimate=cost(rows * width * 20, rows * width * 20),
        name="norm_back",
    )(x, *terms, gain, more)


def norm_back_small_kernel(x_ref, a_ref, b_ref, c_ref, small_ref):
    x = x_ref[...].astype(f32)
    grad = a_ref[...].astype(f32) + b_ref[...].astype(f32) + c_ref[...].astype(f32)
    average = jnp.mean(x, axis=-1, keepdims=True)
    centred = x - average
    variance = jnp.mean(centred * centred, axis=-1, keepdims=True)
    unit = centred * lax.rsqrt(variance + norm_eps)
    small_ref[0:1, :] = jnp.sum(grad * unit, axis=0, keepdims=True)
    small_ref[1:2, :] = jnp.sum(grad, axis=0, keepdims=True)
    small_ref[2:8, :] = jnp.zeros((6, x.shape[1]), f32)


def norm_back_small(x, terms):
    return pl.pallas_call(
        norm_back_small_kernel,
        out_shape=jax.ShapeDtypeStruct((8, x.shape[1]), f32),
        compiler_params=params(),
        cost_estimate=cost(x.size * 10, x.size * 8),
        name="norm_back_small",
    )(x, *terms)


log2_e = 1.4426950408889634


def fill_experts(target, source, experts, width):
    for j in range(experts):
        target[j * lanes : j * lanes + width, :] = source[j * width : (j + 1) * width, :]
        target[j * lanes + width : (j + 1) * lanes, :] = jnp.zeros((lanes - width, target.shape[1]), bf16)


def fill_weights(w_s, wo_s, wv_ref, wk_ref, wo_ref, experts, width):
    fill_experts(w_s, wv_ref, experts, width)
    fill_experts(wo_s, wo_ref, experts, width)
    start = 0
    for place, rows in ((experts + 1, width), (experts + 2, width), (experts, 2 * out_lane)):
        w_s[place * lanes : place * lanes + rows, :] = wk_ref[start : start + rows, :]
        w_s[place * lanes + rows : (place + 1) * lanes, :] = jnp.zeros((lanes - rows, w_s.shape[1]), bf16)
        start += rows


def attn_fwd_kernel(experts, head_width, slot_count, me_ref, *refs):
    mem_refs, slot_refs, refs = refs[:4], refs[4 : 4 + slot_count], refs[4 + slot_count :]
    wv_ref, wk_ref, wo_ref, mask_ref = refs[:4]
    *out_refs, normed_out, q_out, k_out, v_out, ev_out, gate_out, att_out, mixed_out = refs[4:16]
    normed, q_s, k_s, v_s, ev_s, gate_s, att_s, mixed_s, w_s, wo_s, out_s, mask_s, sems = refs[16:]
    me = me_ref[0]
    block = out_s.shape[1]
    quarter = block // 4
    wide = experts * lanes
    send = Sender(sems)

    for slot, ref in enumerate(mem_refs):
        here = slice(slot * quarter, (slot + 1) * quarter)
        normed[here, :] = ref[...]
        mask_s[here, :] = mask_ref[pl.ds(pl.multiple_of((me ^ slot) * quarter, quarter), quarter), :]
    halves = slot_count // 4
    rows = block // halves
    for number, ref in enumerate(slot_refs):
        start = (me ^ (number // halves)) * block + block + number % halves * rows
        normed[pl.ds(pl.multiple_of(start, rows), rows), :] = ref[...]
    send(normed, normed_out)
    fill_weights(w_s, wo_s, wv_ref, wk_ref, wo_ref, experts, head_width)

    scale = head_width ** (-0.5) * log2_e
    for i in range(5):
        here = slice(i * block, (i + 1) * block)
        proj = dot_t(normed[here, :], w_s[...])
        gate = jax.nn.sigmoid(proj[:, wide : wide + lanes]) * (mask_ref[here, :] if i else mask_s[...])
        value = gate[:, 0:1] * proj[:, 0:lanes]
        for j in range(1, experts):
            value = value + gate[:, j : j + 1] * proj[:, j * lanes : (j + 1) * lanes]
        k_s[here, :] = proj[:, wide + lanes : wide + 2 * lanes].astype(bf16)
        v_s[here, :] = value.astype(bf16)
        ev_s[here, :] = proj[:, :wide].astype(bf16)
        q_s[here, :] = (proj[:, wide + 2 * lanes :] * scale).astype(bf16)
        gate_s[here, :] = gate
    send(ev_s, ev_out)
    send(q_s, q_out)
    send(k_s, k_out)
    send(v_s, v_out)

    row = lax.broadcasted_iota(jnp.int32, (block, block), 0)
    col = lax.broadcasted_iota(jnp.int32, (block, block), 1)
    lane = lax.broadcasted_iota(jnp.int32, (block, lanes), 1)
    for i in range(1, 5):
        here, before = slice(i * block, (i + 1) * block), slice(0, i * block)
        own = slice((i - 1) * block, i * block)
        queries = q_s[here, :]
        early = dot_t(queries, k_s[before, :])
        late = jnp.where(col <= row, dot_t(queries, k_s[here, :]), masked_score)
        top = jnp.maximum(jnp.max(early, axis=-1, keepdims=True), jnp.max(late, axis=-1, keepdims=True))
        early = jnp.exp2(early - top)
        late = jnp.exp2(late - top)
        total = jnp.sum(early, axis=-1, keepdims=True) + jnp.sum(late, axis=-1, keepdims=True)
        attended = dot(early.astype(bf16), v_s[before, :]) + dot(late.astype(bf16), v_s[here, :])
        attended = attended * (1.0 / total)
        att_s[own, :] = attended
        gate = gate_s[here, :]
        gate_s[here, :] = jnp.where(lane == log_lane, top + jnp.log2(total), gate)
        for j in range(experts):
            opened = gate[:, out_lane + j : out_lane + j + 1] * attended
            mixed_s[own, j * lanes : (j + 1) * lanes] = opened.astype(bf16)
    send(gate_s, gate_out)
    send(att_s, att_out)
    send(mixed_s, mixed_out)
    for slot in (3, 2, 1, 0):
        start = pl.multiple_of((me ^ slot) * block, block)
        out_s[slot] = dot(mixed_s[pl.ds(start, block), :], wo_s[...]).astype(bf16)
        send(out_s.at[slot], out_refs[slot])
    send.wait()


def attn_fwd(me, mems, slots, w, mask, experts, head_width):
    width = mems[0].shape[1]
    block = 4 * mems[0].shape[0]
    total = 5 * block
    wide = experts * lanes
    shape = lambda rows, cols, kind: jax.ShapeDtypeStruct((rows, cols), kind)
    kept = [
        shape(total, width, bf16),
        *[shape(total, lanes, bf16)] * 3,
        shape(total, wide, bf16),
        shape(total, lanes, f32),
        shape(4 * block, lanes, f32),
        shape(4 * block, wide, bf16),
    ]
    outs = [shape(block, width, bf16)] * 4 + kept
    operands = (*mems, *slots, *w, mask)
    return pl.pallas_call(
        functools.partial(attn_fwd_kernel, experts, head_width, len(slots)),
        in_specs=[in_smem] + [in_vmem] * len(operands),
        out_specs=[anywhere] * len(outs),
        out_shape=outs,
        scratch_shapes=[pltpu.VMEM(a.shape, a.dtype) for a in kept]
        + [
            pltpu.VMEM((wide + 3 * lanes, width), bf16),
            pltpu.VMEM((wide, width), bf16),
            pltpu.VMEM((4, block, width), bf16),
            pltpu.VMEM((block, lanes), f32),
            pltpu.SemaphoreType.DMA((12,)),
        ],
        compiler_params=params(30),
        cost_estimate=cost(4 * total * width * wide, 16 * 1024 * 1024, total * total),
        name="attn_fwd",
    )(me, *operands)


def attn_bwd_kernel(experts, head_width, slot_count, me_ref, *refs):
    slot_refs, refs = refs[:slot_count], refs[slot_count:]
    wv_ref, wk_ref, wo_ref, q_ref, k_ref, v_ref, ev_ref, gate_ref, att_ref = refs[:9]
    *grad_outs, mem_out, dproj_out, rows_out = refs[9:16]
    w_s, wo_s, rows_s, dproj_s, grad_s, mem_s, dk_s, dv_s, sems = refs[16:]
    me = me_ref[0]
    block = mem_s.shape[0]
    wide = experts * lanes
    scale = head_width ** (-0.5)
    send = Sender(sems)

    halves = slot_count // 4
    rows = block // halves
    for number, ref in enumerate(slot_refs):
        start = (me ^ (number // halves)) * block + number % halves * rows
        rows_s[pl.ds(pl.multiple_of(start, rows), rows), :] = ref[...]
    send(rows_s, rows_out)
    fill_weights(w_s, wo_s, wv_ref, wk_ref, wo_ref, experts, head_width)

    row = lax.broadcasted_iota(jnp.int32, (block, block), 0)
    col = lax.broadcasted_iota(jnp.int32, (block, block), 1)
    lane = lax.broadcasted_iota(jnp.int32, (block, lanes), 1)
    for i in range(4, -1, -1):
        here = slice(i * block, (i + 1) * block)
        gate = gate_ref[here, :]
        logit_grad = jnp.zeros((block, lanes), f32)
        if i > 0:
            own = slice((i - 1) * block, i * block)
            mixed_grad = dot_t(rows_s[own, :], wo_s[...])
            attended = att_ref[own, :]
            att_grad = jnp.zeros((block, lanes), f32)
            for j in range(experts):
                part = mixed_grad[:, j * lanes : (j + 1) * lanes]
                att_grad = att_grad + gate[:, out_lane + j : out_lane + j + 1] * part
                inner = jnp.sum(part * attended, axis=-1, keepdims=True)
                logit_grad = jnp.where(lane == out_lane + j, inner, logit_grad)
            grad_low = att_grad.astype(bf16)
            row_sum = jnp.sum(att_grad * attended, axis=-1, keepdims=True)
            log_total = gate[:, log_lane : log_lane + 1]
            queries = q_ref[here, :]
            query_grad = jnp.zeros((block, lanes), f32)
            for span in (slice(0, i * block), here):
                keys = k_ref[span, :]
                scores = dot_t(queries, keys)
                if span is here:
                    scores = jnp.where(col <= row, scores, masked_score)
                probs = jnp.exp2(scores - log_total)
                score_grad = (probs * (dot_t(grad_low, v_ref[span, :]) - row_sum)).astype(bf16)
                query_grad = query_grad + dot(score_grad, keys)
                key_part = t_dot(score_grad, queries)
                value_part = t_dot(probs.astype(bf16), grad_low)
                if i == 4:
                    dk_s[span, :] = key_part
                    dv_s[span, :] = value_part
                else:
                    dk_s[span, :] += key_part
                    dv_s[span, :] += value_part
            dproj_s[here, wide + 2 * lanes :] = (query_grad * scale).astype(bf16)
        else:
            dproj_s[here, wide + 2 * lanes :] = jnp.zeros((block, lanes), bf16)
        value_grad = dv_s[here, :].astype(bf16).astype(f32)
        for j in range(experts):
            cols = slice(j * lanes, (j + 1) * lanes)
            dproj_s[here, cols] = (gate[:, j : j + 1] * value_grad).astype(bf16)
            inner = jnp.sum(value_grad * ev_ref[here, cols].astype(f32), axis=-1, keepdims=True)
            logit_grad = jnp.where(lane == j, inner, logit_grad)
        slope = jnp.where(lane < log_lane, gate * (1.0 - gate), 0.0)
        dproj_s[here, wide : wide + lanes] = (logit_grad * slope).astype(bf16)
        dproj_s[here, wide + lanes : wide + 2 * lanes] = (dk_s[here, :] * (1.0 / log2_e)).astype(bf16)
        normed_grad = dot(dproj_s[here, :], w_s[...]).astype(bf16)
        if i > 0:
            grad_s[pl.ds((i - 1) ^ me, 1)] = normed_grad[None]
        else:
            mem_s[...] = normed_grad
    for slot in (3, 2, 1, 0):
        send(grad_s.at[slot], grad_outs[slot])
    send(dproj_s, dproj_out)
    send(mem_s, mem_out)
    send.wait()


def attn_bwd(me, slots, w, saved, experts, head_width):
    width = slots[0].shape[1]
    block = sum(a.shape[0] for a in slots) // 4
    total = 5 * block
    wide = experts * lanes
    shape = lambda rows, cols: jax.ShapeDtypeStruct((rows, cols), bf16)
    outs = [shape(block, width)] * 5 + [shape(total, wide + 3 * lanes), shape(4 * block, width)]
    operands = (*slots, *w, *saved)
    return pl.pallas_call(
        functools.partial(attn_bwd_kernel, experts, head_width, len(slots)),
        in_specs=[in_smem] + [in_vmem] * len(operands),
        out_specs=[anywhere] * len(outs),
        out_shape=outs,
        scratch_shapes=[
            pltpu.VMEM((wide + 3 * lanes, width), bf16),
            pltpu.VMEM((wide, width), bf16),
            pltpu.VMEM((4 * block, width), bf16),
            pltpu.VMEM((total, wide + 3 * lanes), bf16),
            pltpu.VMEM((4, block, width), bf16),
            pltpu.VMEM((block, width), bf16),
            pltpu.VMEM((total, lanes), f32),
            pltpu.VMEM((total, lanes), f32),
            pltpu.SemaphoreType.DMA((7,)),
        ],
        compiler_params=params(32),
        cost_estimate=cost(4 * total * width * wide, 16 * 1024 * 1024, total * total),
        name="attn_bwd",
    )(me, *operands)


def gelu_parts(u):
    square = u * u
    t = jnp.tanh(gelu_c * u * (1.0 + gelu_a * square))
    slope = 0.5 * (1.0 + t) + 0.5 * gelu_c * u * (1.0 - t * t) * (1.0 + 3.0 * gelu_a * square)
    return 0.5 * u * (1.0 + t), slope


def load_pieces(target, refs, part):
    rows = target.shape[0] // len(refs)
    for number, ref in enumerate(refs):
        start = part * rows if ref.shape[0] > rows else 0
        target[number * rows : (number + 1) * rows, :] = ref[start : start + rows, :]


def send_rows(send, source, outs, span):
    rows = source.shape[0] // len(outs)
    for number in range(len(outs) - 1, -1, -1):
        if span.start <= number * rows < span.stop:
            send(source.at[pl.ds(number * rows, rows)], outs[number])


def two_spans(rows):
    return slice(0, rows // 2), slice(rows // 2, rows)


def ffn_fwd_kernel(part, *refs):
    pieces, (wu_ref, bu_ref, wd_ref) = refs[:4], refs[4:7]
    *outs, rows_out, upper_out, active_out = refs[-12:-5]
    rows_s, upper_s, active_s, out_s, sems = refs[-5:]
    send = Sender(sems)
    total = rows_s.shape[0]
    here = pl.ds(part * total, total)
    load_pieces(rows_s, pieces, part)
    send(rows_s, rows_out.at[here])
    for span in two_spans(total):
        upper = dot(rows_s[span, :], wu_ref[...]) + bu_ref[...]
        upper_s[span, :] = upper.astype(bf16)
        active_s[span, :] = jax.nn.gelu(upper).astype(bf16)
    send(upper_s, upper_out.at[here])
    send(active_s, active_out.at[here])
    for span in two_spans(total)[::-1]:
        out_s[span, :] = dot(active_s[span, :], wd_ref[...]).astype(bf16)
        send_rows(send, out_s, outs, span)
    send.wait()


def ffn_fwd(pieces, part, wu, bu, wd, earlier):
    rows, width = pieces[0].shape
    hidden = wu.shape[1]
    total = 4 * rows
    shape = lambda *dims: jax.ShapeDtypeStruct(dims, bf16)
    operands = (*pieces, wu, bu, wd)
    outs = [shape(rows, width)] * 4 + [shape(2 * total, width), shape(2 * total, hidden), shape(2 * total, hidden)]
    return pl.pallas_call(
        functools.partial(ffn_fwd_kernel, part),
        in_specs=[in_vmem] * len(operands) + [anywhere] * len(earlier),
        out_specs=[anywhere] * len(outs),
        out_shape=outs,
        input_output_aliases={len(operands) + i: 4 + i for i in range(len(earlier))},
        scratch_shapes=[
            pltpu.VMEM((total, width), bf16),
            pltpu.VMEM((total, hidden), bf16),
            pltpu.VMEM((total, hidden), bf16),
            pltpu.VMEM((total, width), bf16),
            pltpu.SemaphoreType.DMA((7,)),
        ],
        compiler_params=params(24),
        cost_estimate=cost(4 * total * width * hidden, 9 * 1024 * 1024, total * hidden),
        name="ffn_fwd",
    )(*operands, *earlier)


def ffn_bwd_kernel(part, forward, *refs):
    pieces, refs = refs[:4], refs[4:]
    if forward:
        normed_refs, (bu_ref, wd_ref, wu_ref), refs = refs[:4], refs[4:7], refs[7:]
        *outs, bias_out, rows_out, grad_out, normed_out, active_out = refs[-15:-6]
    else:
        (upper_ref, wd_ref, wu_ref), refs = refs[:3], refs[3:]
        *outs, bias_out, rows_out, grad_out = refs[-13:-6]
    rows_s, grad_s, out_s, normed_s, active_s, sems = refs[-6:]
    send = Sender(sems)
    total = rows_s.shape[0]
    here = pl.ds(part * total, total)
    load_pieces(rows_s, pieces, part)
    send(rows_s, rows_out.at[here])
    if forward:
        load_pieces(normed_s, normed_refs, part)
        send(normed_s, normed_out.at[here])
    sums = jnp.zeros((1, grad_s.shape[1]), f32)
    for span in two_spans(total):
        if forward:
            upper = dot(normed_s[span, :], wu_ref[...]) + bu_ref[...]
        else:
            upper = upper_ref[span, :].astype(f32)
        active_grad = dot_t(rows_s[span, :], wd_ref[...])
        active, slope = gelu_parts(upper)
        if forward:
            active_s[span, :] = active.astype(bf16)
        upper_grad = (active_grad * slope).astype(bf16)
        grad_s[span, :] = upper_grad
        sums = sums + jnp.sum(upper_grad.astype(f32), axis=0, keepdims=True)
    bias_out[...] = sums
    send(grad_s, grad_out.at[here])
    if forward:
        send(active_s, active_out.at[here])
    for span in two_spans(total)[::-1]:
        out_s[span, :] = dot_t(grad_s[span, :], wu_ref[...]).astype(bf16)
        send_rows(send, out_s, outs, span)
    send.wait()


def ffn_bwd(pieces, part, wd, wu, earlier, upper=None, normed=None, bu=None):
    forward = normed is not None
    width, hidden = wu.shape
    rows = min(a.shape[0] for a in (normed if forward else pieces))
    total = 4 * rows
    shape = lambda *dims: jax.ShapeDtypeStruct(dims, bf16)
    kept = [shape(2 * total, width), shape(2 * total, hidden)]
    outs = [shape(rows, width)] * 4 + [jax.ShapeDtypeStruct((1, hidden), f32)] + kept + (kept if forward else [])
    operands = (*pieces, *normed, bu, wd, wu) if forward else (*pieces, upper, wd, wu)
    specs = [whole_spec(a.shape) for a in operands]
    if not forward:
        specs[4] = rows_spec(upper, part, total)
    spare = (total, width) if forward else (8, lanes)
    return pl.pallas_call(
        functools.partial(ffn_bwd_kernel, part, forward),
        grid=(1,),
        in_specs=specs + [anywhere] * len(earlier),
        out_specs=[anywhere] * 4 + [whole_spec((1, hidden))] + [anywhere] * (len(outs) - 5),
        out_shape=outs,
        input_output_aliases={len(operands) + i: 5 + i for i in range(len(earlier))},
        scratch_shapes=[
            pltpu.VMEM((total, width), bf16),
            pltpu.VMEM((total, hidden), bf16),
            pltpu.VMEM((total, width), bf16),
            pltpu.VMEM(spare, bf16),
            pltpu.VMEM(spare, bf16),
            pltpu.SemaphoreType.DMA((8,)),
        ],
        compiler_params=params(36),
        cost_estimate=cost(4 * total * width * hidden, 9 * 1024 * 1024, total * hidden),
        name="ffn_bwd",
    )(*operands, *earlier)


def attn_grads_kernel(experts, head_width, *refs):
    sources, (out_ref, dproj_s, normed_s, mixed_s, rows_s, grad_s, loads, sems) = refs[:4], refs[4:]
    send = Sender(sems)
    fetch = Sender(loads)
    for source, target in zip(sources, (dproj_s, normed_s, mixed_s, rows_s)):
        fetch(source, target)

    def fill(start, left, right, counts):
        for pair in range(0, len(counts), 2):
            here = counts[pair : pair + 2]
            wide = t_dot(left[:, pair * lanes : (pair + len(here)) * lanes], right[...]).astype(bf16)
            for number, count in enumerate(here):
                grad_s[start : start + count, :] = wide[number * lanes : number * lanes + count]
                start += count
        return start

    fetch.copies[0].wait()
    fetch.copies[1].wait()
    pack = fill(0, dproj_s, normed_s, [head_width] * experts + [2 * out_lane] + [head_width] * 2)
    send(grad_s.at[pl.ds(0, pack)], out_ref.at[pl.ds(0, pack)])
    fetch.copies[2].wait()
    fetch.copies[3].wait()
    total = fill(pack, mixed_s, rows_s, [head_width] * experts)
    send(grad_s.at[pl.ds(pack, total - pack)], out_ref.at[pl.ds(pack, total - pack)])
    send.wait()


def attn_grads(dproj, normed, mixed, rows, experts, head_width):
    count = (2 * experts + 2) * head_width + 2 * out_lane
    width = normed.shape[1]
    operands = (dproj, normed, mixed, rows)
    return pl.pallas_call(
        functools.partial(attn_grads_kernel, experts, head_width),
        in_specs=[anywhere] * len(operands),
        out_specs=anywhere,
        out_shape=jax.ShapeDtypeStruct((count, width), bf16),
        scratch_shapes=[pltpu.VMEM(a.shape, a.dtype) for a in operands]
        + [pltpu.VMEM((count, width), bf16), pltpu.SemaphoreType.DMA((4,)), pltpu.SemaphoreType.DMA((2,))],
        compiler_params=params(28),
        cost_estimate=cost(0, 0),
        name="attn_grads",
    )(*operands)


class DpSums:
    def __init__(self):
        self.chunks = {}
        self.token = ()
        self.direct = lax.axis_size("dp") != 4
        place = lax.axis_index("dp")
        self.middle = (place == 1) | (place == 2)

    def add(self, name, own, got):
        self.chunks[name] = dict(own=own, moving=got, step=0)

    def turns(self, *names):
        for name in names:
            self.turn(self.chunks[name])

    def turn(self, chunk):
        step = chunk["step"]
        chunk["step"] += 1
        if self.direct:
            if step == 0:
                chunk["end"] = lax.psum(plus(chunk["own"], chunk["moving"]), "dp")
            return
        got = after(chunk["moving"], self.token)
        if step == 3:
            chunk["end"] = jax.tree.map(lambda full, far: jnp.where(self.middle, full, far), chunk["own"], got)
            return
        total = plus(chunk["own"], got)
        pairs = ([(0, 1), (3, 2)], [(1, 2), (2, 1)], [(1, 0), (2, 3)])[step]
        chunk["own"] = self.token = total
        chunk["moving"] = jax.tree.map(lambda a: lax.ppermute(a, "dp", pairs), total)


def split_tiles(rows, pieces):
    size = rows // 16 // pieces * 16
    return [rows - size * (pieces - 1)] + [size] * (pieces - 1)


def cut(a, pieces):
    rows = a.shape[0] // pieces
    return [a[i * rows : (i + 1) * rows] for i in range(pieces)]


def padded_rows(a, rows):
    return jnp.pad(a, ((0, rows - a.shape[0]), (0, 0)))


def swap_weights(weights, start_after):
    size = lax.axis_size("dp")
    odd = lax.axis_index("dp") % 2
    results = []
    gots = []
    for a, pieces in weights:
        parts = []
        for part in cut(a, pieces):
            part = after(part, start_after, *gots[: max(0, len(gots) - 1)])
            if size % 2:
                gots.append(swap_section(part))
                parts.append(gots[-1])
                continue
            rows = part.shape[0] // 2
            gots.append(swap_section(lax.dynamic_slice_in_dim(part, odd * rows, rows, 0)))
            got = gots[-1]
            other = lax.ppermute(got, "dp", [(i, i ^ 1) for i in range(size)])
            parts += [jnp.where(odd == 0, got, other), jnp.where(odd == 0, other, got)]
        results.append(jnp.concatenate(parts, axis=0))
    return results


def route_mask(value_ids, out_ids, experts, memory_len):
    lane = jnp.arange(lanes, dtype=jnp.int32)[None, :]
    out_full = jnp.pad(out_ids, ((0, 0), (memory_len, 0)), constant_values=-1)
    hit = jnp.zeros((value_ids.shape[1], lanes), jnp.bool_)
    for k in range(value_ids.shape[0]):
        hit = hit | (lane == value_ids[k][:, None])
        hit = hit | ((lane == out_full[k][:, None] + out_lane) & (out_full[k][:, None] >= 0))
    return hit.astype(f32)


def on_device(
    inputs,
    memory,
    value_routes,
    out_routes,
    ln1_gain,
    ln1_bias,
    query_weight,
    key_weight,
    value_weight,
    value_router,
    out_router,
    output_weight,
    ln2_gain,
    ln2_bias,
    up_weight,
    up_bias,
    down_weight,
    down_bias,
    out_cot,
):
    experts = value_router.shape[-1]
    head_width = query_weight.shape[-1]
    sec = lax.axis_index("section")
    head = lax.axis_index("head")
    me = head.astype(jnp.int32).reshape(1)
    first = sec == 0
    pick = lambda a, index: lax.dynamic_index_in_dim(a, index, 0, keepdims=False)
    memory_len = memory.shape[2] * lax.axis_size("head")

    value_rows = experts * head_width
    router_rows = [padded_rows(a[0, 0].T, out_lane) for a in (value_router, out_router)]
    kqr = jnp.concatenate([key_weight[0, 0].T, query_weight[0, 0].T, *router_rows])
    weights = [value_weight[0, 0].T, kqr, output_weight[0, 0], up_weight[0], down_weight[0]]

    small = jnp.concatenate([ln1_gain, ln1_bias, ln2_gain, ln2_bias, up_bias, down_bias, ln1_gain, ln1_bias], axis=0)
    route_rows = jnp.concatenate(
        [
            jnp.transpose(value_routes[0, :, :, 0, :], (0, 2, 1)),
            jnp.pad(jnp.transpose(out_routes[0, :, :, 0, :], (0, 2, 1)), ((0, 0), (0, 0), (memory_len, 0)), constant_values=-1),
        ],
        axis=1,
    )
    sends = [small, pick(memory[0], 1 - sec), pick(route_rows, 1 - sec)]
    small_got, memory_got, routes_got = [swap_section(a) for a in sends]

    def both_layers(own, got):
        return jnp.where(first, own, got), jnp.where(first, got, own)

    smalls = both_layers(small, small_got)
    route_sets = both_layers(pick(route_rows, sec), routes_got)
    memories = both_layers(pick(memory[0], sec), memory_got)
    weights_got = swap_weights(list(zip(weights, (1, 1, 1, 1, 1))), sends)
    weight_sets = [both_layers(a, got) for a, got in zip(weights, weights_got)]

    x = pick(inputs, sec)
    cot = pick(out_cot, sec)
    own_norm = norm_only(x, smalls[0][0:1], smalls[0][1:2])
    slots = gather_slots(own_norm)
    route_sets = after(route_sets, own_norm)
    topk = value_routes.shape[-1]

    layers = []
    for number in range(2):
        vec = smalls[number]
        routes = route_sets[number]
        layers.append(
            dict(
                gain1=vec[0:1],
                shift1=vec[1:2],
                gain2=vec[2:3],
                shift2=vec[3:4],
                up_b=vec[4:5],
                down_b=vec[5:6],
                w=(weight_sets[0][number], weight_sets[1][number], weight_sets[2][number]),
                wu=weight_sets[3][number],
                wd=weight_sets[4][number],
                mask=route_mask(routes[:topk], routes[topk:, memory_len:], experts, memory_len),
                mem=memories[number],
            )
        )
    one, two = layers
    no_add = jnp.zeros_like(one["gain1"])
    for layer in layers:
        layer["mem_slots"] = gather_slots(norm_only(after(layer["mem"], own_norm), layer["gain1"], layer["shift1"]))
    cot_slots = gather_slots(after(cot, slots[2], one["mem_slots"][2]))
    slots[3] = after(slots[3], one["mask"], two["mask"])

    def attention(layer, rows_in, slots):
        *out, layer["normed"], q, k, v, ev, gate, att, layer["mixed"] = attn_fwd(
            me, layer["mem_slots"], slots, layer["w"], layer["mask"], experts, head_width
        )
        layer["saved"] = (q, k, v, ev, gate, att)
        if layer is one:
            out[3] = after(out[3], cot_slots[2], two["mem_slots"][2])
        terms, _ = scatter_halves(out)
        layer["hidden"], slots = [], []
        for part in range(2):
            hidden, normed = add_norm(rows_in[part], terms[part], part, no_add, layer["gain2"], layer["shift2"], f32)
            layer["hidden"].append(hidden)
            slots.append(gather_slots(normed))
        return slots

    one["rows"] = [x, x]
    halves = attention(one, one["rows"], slots)
    kept = ()
    two["rows"], slots = [], []
    for part in range(2):
        *out, n2, upper, active = ffn_fwd(halves[part], part, one["wu"], one["up_b"], one["wd"], kept)
        kept = (n2, upper, active)
        terms, _ = scatter_slots(out)
        rows, normed = add_norm(one["hidden"][part], terms, part, one["down_b"], two["gain1"], two["shift1"], bf16)
        two["rows"].append(rows)
        slots.append(gather_slots(normed))
    one["n2"], one["upper"], one["active"] = kept
    slots = [half[slot] for slot in range(4) for half in slots]
    halves = attention(two, two["rows"], slots)

    def by_layer(one, two):
        got = swap_section(jnp.where(first, two, one))
        kept = jnp.where(first, one, two)
        return jnp.stack([jnp.where(first, kept, got), jnp.where(first, got, kept)])[None]

    def send_chunks(one, two, names, sizes):
        start = 0
        for name, size in zip(names, sizes):
            part_one, part_two = one[start : start + size], two[start : start + size]
            start += size
            send = jnp.where(first, part_two, part_one)
            if sums.chunks:
                send = after(send, list(sums.chunks.values())[-1]["moving"])
            sums.add(name, jnp.where(first, part_one, part_two), swap_section(send))

    sums = DpSums()
    grads = [{}, {}]
    smalls_out, mem_grads = [None, None], [None, None]
    input_grads = [None, None]
    for number in (1, 0):
        layer, grad = layers[number], grads[number]
        wu, wd = layer["wu"], layer["wd"]
        if number == 1:
            g_rows = [cot, cot]
        kept = ()
        terms, bias = [], []
        for part in range(2):
            if number == 1:
                *out, sums_here, g_all, upper_grad, n2, active = ffn_bwd(
                    cot_slots, part, wd, wu, kept, normed=halves[part], bu=layer["up_b"]
                )
                kept = (g_all, upper_grad, n2, active)
            else:
                *out, sums_here, g_all, upper_grad = ffn_bwd(halves[part], part, wd, wu, kept, upper=layer["upper"])
                kept = (g_all, upper_grad)
                n2, active = layer["n2"], layer["active"]
            bias.append(sums_here)
            terms_here, token = scatter_slots(out)
            terms.append(terms_here)
        grad["down"] = t_dot(active, after(g_all, token)).astype(bf16)
        grad["up"] = t_dot(after(n2, grad["down"]), upper_grad).astype(bf16)
        if number == 0:
            halved = [wd.shape[0] // 2] * 2
            send_chunks(grad["down"], grads[1]["down"], ("down0", "down1"), halved)
            send_chunks(grad["up"], grads[1]["up"], ("up0", "up1"), halved)
        terms[1] = (*terms[1][0:2], after(terms[1][2], grad["up"]))
        hidden_grads, a_halves, small2 = [], [], []
        for part in range(2):
            dx, low, small_here = norm_back(layer["hidden"][part], terms[part], part, layer["gain2"], g_rows[part])
            hidden_grads.append(dx)
            small2.append(small_here)
            a_halves.append(gather_slots(low))
        a_slots = [half[slot] for slot in range(4) for half in a_halves]
        if number == 0:
            sums.turns("down0")
            a_slots[7] = after(a_slots[7], sums.token)
        else:
            down_out = dot(active, after(wd, a_halves[1][0])).astype(bf16)
            rows = down_out.shape[0] // 8
            last_parts = [
                jnp.concatenate([down_out[s * rows : (s + 1) * rows], down_out[(4 + s) * rows : (5 + s) * rows]])
                for s in range(4)
            ]
            last_terms, _ = scatter_halves(last_parts, a_halves[1][2])
        *ngs, ngm, dproj, a_all = attn_bwd(me, a_slots, layer["w"], layer["saved"], experts, head_width)
        if number == 1:
            ngs[3] = after(ngs[3], [here[2] for here in last_terms])
            near, from_core, _ = last_terms[0]
            last_out = jnp.concatenate(layer["hidden"]) + layer["down_b"] + near.astype(f32) + from_core.astype(f32)
            last_out = (last_out + jnp.concatenate([here[2] for here in last_terms]).astype(f32)).astype(bf16)
            layer_out = by_layer(jnp.concatenate(layer["rows"]), last_out)
        terms, token = scatter_halves(ngs)
        grad["attn"] = attn_grads(after(dproj, token), layer["normed"], layer["mixed"], a_all, experts, head_width)
        token = grad["attn"]
        if number == 0:
            sizes = split_tiles(token.shape[0], 4)
            send_chunks(token, grads[1]["attn"], ("attn0", "attn1", "attn2", "attn3"), sizes)
            sums.token = token
            sums.turns("down0", "down1")
            token = sums.token
        terms[1] = (*terms[1][0:2], after(terms[1][2], token))
        rows_grads, low_grads, small1, halves = [], [], [], []
        for part in range(2):
            dx, low, small_here = norm_back(layer["rows"][part], terms[part], part, layer["gain1"], hidden_grads[part])
            rows_grads.append(dx)
            low_grads.append(low)
            small1.append(small_here)
            if number == 1:
                halves.append(gather_slots(low))
        g_rows = rows_grads if number == 0 else low_grads
        mem_grads[number] = cut(ngm, 4)
        input_grads[number] = jnp.concatenate(low_grads)
        smalls_out[number] = (small1[0] + small1[1], small2[0] + small2[1], bias[0] + bias[1])

    mem_terms, _ = scatter_slots([jnp.concatenate(pair) for pair in zip(*mem_grads)])
    rows = memories[0].shape[0]
    vecs = []
    for number, (small1, small2, bias) in enumerate(smalls_out):
        here = slice(number * rows, (number + 1) * rows)
        small_mem = norm_back_small(layers[number]["mem"], [a[here] for a in mem_terms])
        vecs.append(jnp.concatenate([(small1 + small_mem)[0:2], small2[0:6]]))
    vec = jnp.concatenate(vecs)
    vec = vec + to_core(vec)
    vec = vec + to_chip(vec)
    vecs = [jnp.concatenate([part[0:5], bias, part[6:8]]) for part, (_, _, bias) in zip(cut(vec, 2), smalls_out)]
    last_chunk = sums.chunks["attn3"]
    last_chunk["own"] = (last_chunk["own"], jnp.where(first, vecs[0], vecs[1]))
    last_chunk["moving"] = (last_chunk["moving"], swap_section(jnp.where(first, vecs[1], vecs[0])))
    sums.turns("down0", "down1", "up0", "down0", "down1", "up0", "up1", "down1", "attn0", "up0", "up1", "attn0", "attn1")
    sums.turns("up0", "up1", "attn1", "attn2", "attn0", "up1", "attn2", "attn1", "attn3")
    last_sum = sums.token
    sums.turns("attn0", "attn2", "attn3", "attn1", "attn3", "attn2", "attn3")
    ends = {name: chunk["end"] for name, chunk in sums.chunks.items()}
    ends["attn3"], vec = ends["attn3"]
    input_grad = by_layer(*[after(a, last_sum) for a in input_grads])
    join = lambda *names: jnp.concatenate([ends[name] for name in names]).astype(f32)
    down_sum, up_sum = join("down0", "down1"), join("up0", "up1")
    attn_sum = join("attn0", "attn1", "attn2", "attn3")

    def take(start, count):
        return attn_sum[start : start + count]

    routers = value_rows + 2 * out_lane
    value_sum, vroute_sum, oroute_sum = take(0, value_rows), take(value_rows, experts), take(value_rows + out_lane, experts)
    key_sum, query_sum = take(routers, head_width), take(routers + head_width, head_width)
    out_sum = take(routers + 2 * head_width, value_rows)

    return (
        layer_out,
        input_grad,
        vec[0:1],
        vec[1:2],
        query_sum.T[None, None],
        key_sum.T[None, None],
        value_sum.T[None, None],
        vroute_sum.T[None, None],
        oroute_sum.T[None, None],
        out_sum[None, None],
        vec[2:3],
        vec[3:4],
        up_sum[None],
        vec[5:6],
        down_sum[None],
        vec[4:5],
    )


def solution(mesh):
    placed = (
        P("dp", "head", None),
        P("section", "dp", "head", None),
        P("section", "dp", None, "head", None),
        P("section", "dp", None, "head", None),
        P("section", None),
        P("section", None),
        P("section", "head", None, None),
        P("section", "head", None, None),
        P("section", "head", None, None),
        P("section", "head", None, None),
        P("section", "head", None, None),
        P("section", "head", None, None),
        P("section", None),
        P("section", None),
        P("section", None, "head"),
        P("section", "head"),
        P("section", "head", None),
        P("section", None),
        P("dp", "head", None),
    )
    return jax.shard_map(
        on_device,
        mesh=mesh,
        in_specs=placed,
        out_specs=(
            P("section", "dp", "head", None),
            P("section", "dp", "head", None),
            P("section", None),
            P("section", None),
            P("section", "head", None, None),
            P("section", "head", None, None),
            P("section", "head", None, None),
            P("section", "head", None, None),
            P("section", "head", None, None),
            P("section", "head", None, None),
            P("section", None),
            P("section", None),
            P("section", None, "head"),
            P("section", "head"),
            P("section", "head", None),
            P("section", None),
        ),
        check_vma=False,
    )
```

time: 625 us -> 594 us (0.950)
  waiting for transfers between devices: 237 us -> 278 us
  Pallas kernels: 134 us -> 93.6 us
  other arithmetic: 71.8 us -> 42.5 us
  matrix products: 28.5 us -> 14.7 us
  starting transfers between devices: 124 us -> 131 us
    pallas_call x20 -> x26, Pallas kernels: 133 us -> 92.3 us  [the longest x2 21.7 us: attn_bwd(): pl.pallas_call(functools.partial(attn_bwd_kernel, experts, head_width, le...]
    ppermute x22 -> x34, waiting for transfers between devices: 73.3 us -> 96.9 us  [to_chip(): return lax.ppermute(a, 'head', chip_pairs)]
    ppermute x18 -> x19, waiting for transfers between devices: 49.7 us -> 71.7 us  [swap_section(): return lax.ppermute(a, 'section', [(0, 1), (1, 0)])]
    dot_general x8 -> x4, matrix products: 28.5 us -> 12.4 us  [t_dot(): lax.dot_general(a, b, (((0,), (0,)), ((), ())), preferred_element_type=f32)]
    convert_element_type x21 -> x36, other arithmetic: 27.3 us -> 12.7 us  [plus(): (one.astype(f32) + two.astype(f32)).astype(one.dtype)]
    ppermute x24 -> x27, waiting for transfers between devices: 79.7 us -> 94.1 us  [turn(): lax.ppermute(a, 'dp', pairs)]
    ppermute x22 -> x34, starting transfers between devices: 29.9 us -> 39.8 us  [to_chip(): return lax.ppermute(a, 'head', chip_pairs)]
    ppermute x42 -> x57, waiting for transfers between devices: 15.4 us -> 6.08 us  [to_core(): return lax.ppermute(a, 'head', core_pairs)]
  transfers between devices with their start and end apart: 111 -> 142, of which waited for: 47 -> 55; matrix products, arithmetic and copies ran while one was open for 17% -> 10% of each run, Pallas kernels for 14% -> 13%
where the time goes in v4:
time: 594 us; the launch traced here: 587 us
  waiting for transfers between devices  278 us (47%)
  starting transfers between devices  131 us (22%)
  Pallas kernels  93.6 us (16%)
  other arithmetic  42.5 us (7%)
  local copies, waits for them, and re-layouts  23.3 us (4%)
  matrix products  14.7 us (2%)
    ppermute x34, waiting for transfers between devices, to_chip(): return lax.ppermute(a, 'head', chip_pairs)  96.9 us
    ppermute x27, waiting for transfers between devices, turn(): lax.ppermute(a, 'dp', pairs)  94.1 us
    ppermute x19, waiting for transfers between devices, swap_section(): return lax.ppermute(a, 'section', [(0, 1), (1, 0)])  71.7 us
    ppermute x27, starting transfers between devices, turn(): lax.ppermute(a, 'dp', pairs)  52.4 us
    ppermute x34, starting transfers between devices, to_chip(): return lax.ppermute(a, 'head', chip_pairs)  39.8 us
    pallas_call x2, Pallas kernels, attn_bwd(): pl.pallas_call(functools.partial(attn_bwd_kernel, experts, head_width, le...  21.7 us
    ppermute x19, starting transfers between devices, swap_section(): return lax.ppermute(a, 'section', [(0, 1), (1, 0)])  21.6 us
    pallas_call x2, Pallas kernels, attn_fwd(): pl.pallas_call(functools.partial(attn_fwd_kernel, experts, head_width, le...  20.1 us
  transfers between devices with their start and end apart: 142, of which 55 were waited for; matrix products, arithmetic and copies ran while one was open for 10% of the time, Pallas kernels for 13%

profile of v4, /device:TPU:0, one launch (start us, length us, event | category | flops | bytes accessed | tf_op | source)
XLA Modules:
  0.0 587.2 jit_solution(18394758306585884391)
XLA Ops:
  21.2 8.7 %collective-permute-done.9 = bf16[280,1024]{1,0:T(8,128)(2,1)} collective-permute-done((bf16[280,1024]{1,0:T(8,128)(2,1)}, bf16[280,1024]{1,0:T(8,128)(2,1)}, u32[]{:S(2)}, u32[]{:S(2)}) %collective-permute-start.9) | collective-permute-done | bytes 573472 | tf_op jit(solution)/shard_map/ppermute | solution.py:81
  48.5 9.4 %collective-permute-done.14 = bf16[280,1024]{1,0:T(8,128)(2,1)S(1)} collective-permute-done((bf16[280,1024]{1,0:T(8,128)(2,1)S(1)}, bf16[280,1024]{1,0:T(8,128)(2,1)S(1)}, u32[]{:S(2)}, u32[]{:S(2)}) %collective-permute-start.14) | collective-permute-done | bytes 573472 | tf_op jit(solution)/shard_map/ppermute | solution.py:710
  61.1 8.5 %collective-permute-done.23 = bf16[512,1024]{1,0:T(8,128)(2,1)S(1)} collective-permute-done((bf16[512,1024]{1,0:T(8,128)(2,1)S(1)}, bf16[512,1024]{1,0:T(8,128)(2,1)S(1)}, u32[]{:S(2)}, u32[]{:S(2)}) %collective-permute-start.23) | collective-permute-done | bytes 1048608 | tf_op jit(solution)/shard_map/ppermute | solution.py:81
  71.0 10.2 %attn_fwd.2 = (bf16[256,1024]{1,0:T(8,128)(2,1)S(1)}, bf16[256,1024]{1,0:T(8,128)(2,1)S(1)}, bf16[256,1024]{1,0:T(8,128)(2,1)S(1)}, bf16[256,1024]{1,0:T(8,128)(...) custom-call(s32[1]{0:T(128)} %bitcast.1.me_ref, ...), custom_call_target="tpu_custom_call" | custom-call | flops 3355443200 | bytes 16777216 | tf_op jit(solution)/shard_map/attn_fwd/pallas_call | solution.py:328
  92.6 7.2 %collective-permute-done.30.c_ref = bf16[128,1024]{1,0:T(8,128)(2,1)S(1)} collective-permute-done((bf16[128,1024]{1,0:T(8,128)(2,1)S(1)}, bf16[128,1024]{1,0:T(8,128)(2,1)S(1)}, u32[]{:S(2)}, u32[]{:S(2)}) %collective-permute-start.30) | collective-permute-done | bytes 262176 | tf_op jit(solution)/shard_map/ppermute | solution.py:77
  126.6 6.7 %collective-permute-done.29.c_ref = bf16[128,1024]{1,0:T(8,128)(2,1)S(1)} collective-permute-done((bf16[128,1024]{1,0:T(8,128)(2,1)S(1)}, bf16[128,1024]{1,0:T(8,128)(2,1)S(1)}, u32[]{:S(2)}, u32[]{:S(2)}) %collective-permute-start.29) | collective-permute-done | bytes 262176 | tf_op jit(solution)/shard_map/ppermute | solution.py:77
  151.5 10.0 %attn_fwd.3 = (bf16[256,1024]{1,0:T(8,128)(2,1)S(1)}, bf16[256,1024]{1,0:T(8,128)(2,1)S(1)}, bf16[256,1024]{1,0:T(8,128)(2,1)S(1)}, bf16[256,1024]{1,0:T(8,128)(...) custom-call(s32[1]{0:T(128)} %bitcast.1.me_ref, ...), custom_call_target="tpu_custom_call" | custom-call | flops 3355443200 | bytes 16777216 | tf_op jit(solution)/shard_map/attn_fwd/pallas_call | solution.py:328
  168.3 6.6 %collective-permute-done.47.c_ref = bf16[128,1024]{1,0:T(8,128)(2,1)S(1)} collective-permute-done((bf16[128,1024]{1,0:T(8,128)(2,1)S(1)}, bf16[128,1024]{1,0:T(8,128)(2,1)S(1)}, u32[]{:S(2)}, u32[]{:S(2)}) %collective-permute-start.47) | collective-permute-done | bytes 262176 | tf_op jit(solution)/shard_map/ppermute | solution.py:77
  220.8 5.9 %collective-permute-done.62.refs_5_ = bf16[128,1024]{1,0:T(8,128)(2,1)S(1)} collective-permute-done((bf16[128,1024]{1,0:T(8,128)(2,1)S(1)}, bf16[128,1024]{1,0:T(8,128)(2,1)S(1)}, u32[]{:S(2)}, u32[]{:S(2)}) %collective-permute-start.62) | collective-permute-done | bytes 262176 | tf_op jit(solution)/shard_map/ppermute | solution.py:77
  234.3 11.1 %attn_bwd.2 = (bf16[256,1024]{1,0:T(8,128)(2,1)S(1)}, bf16[256,1024]{1,0:T(8,128)(2,1)}, bf16[256,1024]{1,0:T(8,128)(2,1)S(1)}, bf16[256,1024]{1,0:T(8,128)(2,1)...) custom-call(s32[1]{0:T(128)} %bitcast.1.me_ref, ...), custom_call_target="tpu_custom_call" | custom-call | flops 3355443200 | bytes 16777216 | tf_op jit(solution)/shard_map/attn_bwd/pallas_call | solution.py:436
  261.2 5.7 attn_grads.2
  330.2 10.5 %attn_bwd.3 = (bf16[256,1024]{1,0:T(8,128)(2,1)S(1)}, bf16[256,1024]{1,0:T(8,128)(2,1)S(1)}, bf16[256,1024]{1,0:T(8,128)(2,1)S(1)}, bf16[256,1024]{1,0:T(8,128)(...) custom-call(s32[1]{0:T(128)} %bitcast.1.me_ref, ...), custom_call_target="tpu_custom_call" | custom-call | flops 3355443200 | bytes 16777216 | tf_op jit(solution)/shard_map/attn_bwd/pallas_call | solution.py:436
  345.2 5.7 attn_grads.3
  353.3 13.8 %collective-permute-done.101 = bf16[512,1024]{1,0:T(8,128)(2,1)S(1)} collective-permute-done((bf16[512,1024]{1,0:T(8,128)(2,1)S(1)}, bf16[512,1024]{1,0:T(8,128)(2,1)S(1)}, u32[]{:S(2)}, u32[]{:S(2)}) %collective-permute-start.101) | collective-permute-done | bytes 1048608 | tf_op jit(solution)/shard_map/ppermute | solution.py:81
  380.1 11.1 %collective-permute-done.115 = bf16[512,1024]{1,0:T(8,128)(2,1)S(1)} collective-permute-done((bf16[512,1024]{1,0:T(8,128)(2,1)S(1)}, bf16[512,1024]{1,0:T(8,128)(2,1)S(1)}, u32[]{:S(2)}, u32[]{:S(2)}) %collective-permute-start.115) | collective-permute-done | bytes 1048608 | tf_op jit(solution)/shard_map/ppermute | solution.py:677
  395.8 5.7 collective-permute-start.117
  409.0 13.3 %collective-permute-done.117 = bf16[512,1024]{1,0:T(8,128)(2,1)S(1)} collective-permute-done((bf16[512,1024]{1,0:T(8,128)(2,1)S(1)}, bf16[512,1024]{1,0:T(8,128)(2,1)S(1)}, u32[]{:S(2)}, u32[]{:S(2)}) %collective-permute-start.117) | collective-permute-done | bytes 1048608 | tf_op jit(solution)/shard_map/ppermute | solution.py:677
  430.5 14.4 %collective-permute-done.105 = bf16[352,1024]{1,0:T(8,128)(2,1)S(1)} collective-permute-done((bf16[352,1024]{1,0:T(8,128)(2,1)S(1)}, bf16[352,1024]{1,0:T(8,128)(2,1)S(1)}, u32[]{:S(2)}, u32[]{:S(2)}) %collective-permute-start.105) | collective-permute-done | bytes 720928 | tf_op jit(solution)/shard_map/ppermute | solution.py:81
  455.1 12.0 %collective-permute-done.119 = bf16[352,1024]{1,0:T(8,128)(2,1)S(1)} collective-permute-done((bf16[352,1024]{1,0:T(8,128)(2,1)S(1)}, bf16[352,1024]{1,0:T(8,128)(2,1)S(1)}, u32[]{:S(2)}, u32[]{:S(2)}) %collective-permute-start.119) | collective-permute-done | bytes 720928 | tf_op jit(solution)/shard_map/ppermute | solution.py:677
  476.9 7.9 %collective-permute-done.122 = bf16[336,1024]{1,0:T(8,128)(2,1)S(1)} collective-permute-done((bf16[336,1024]{1,0:T(8,128)(2,1)S(1)}, bf16[336,1024]{1,0:T(8,128)(2,1)S(1)}, u32[]{:S(2)}, u32[]{:S(2)}) %collective-permute-start.122) | collective-permute-done | bytes 688160 | tf_op jit(solution)/shard_map/ppermute | solution.py:677
  512.1 9.4 %collective-permute-start.128 = (bf16[336,1024]{1,0:T(8,128)(2,1)S(1)}, bf16[336,1024]{1,0:T(8,128)(2,1)S(1)}, u32[]{:S(2)}, u32[]{:S(2)}) collective-permute-start(bf16[336,1024]{1,0:T(8,128)(2,1)S(1)} %add_convert_fusion.18), channel_id=1, source_target_pairs={{0,1},{3,2},{4,5},{7,6},{8,9},{11,10},{12,13},{15,14},{16,17},{19,... | collective-permute-start | bytes 2064392 | tf_op jit(solution)/shard_map/ppermute | solution.py:677
  521.6 17.8 %collective-permute-done.135 = bf16[352,1024]{1,0:T(8,128)(2,1)S(1)} collective-permute-done((bf16[352,1024]{1,0:T(8,128)(2,1)S(1)}, bf16[352,1024]{1,0:T(8,128)(2,1)S(1)}, u32[]{:S(2)}, u32[]{:S(2)}) %collective-permute-start.135) | collective-permute-done | bytes 720928 | tf_op jit(solution)/shard_map/ppermute | solution.py:677
  555.7 15.6 %collective-permute-done.137 = bf16[336,1024]{1,0:T(8,128)(2,1)S(1)} collective-permute-done((bf16[336,1024]{1,0:T(8,128)(2,1)S(1)}, bf16[336,1024]{1,0:T(8,128)(2,1)S(1)}, u32[]{:S(2)}, u32[]{:S(2)}) %collective-permute-start.137) | collective-permute-done | bytes 688160 | tf_op jit(solution)/shard_map/ppermute | solution.py:677
  571.3 8.4 %collective-permute-done.134 = f32[8,1024]{1,0:T(8,128)S(1)} collective-permute-done((f32[8,1024]{1,0:T(8,128)S(1)}, f32[8,1024]{1,0:T(8,128)S(1)}, u32[]{:S(2)}, u32[]{:S(2)}) %collective-permute-start.134) | collective-permute-done | bytes 32800 | tf_op jit(solution)/shard_map/ppermute | solution.py:677
  (579 shorter events, 348.1 us)
Async XLA Ops:
  16.8 54.1 %collective-permute-start.5 = (bf16[256,1024]{1,0:T(8,128)(2,1)S(1)}, bf16[256,1024]{1,0:T(8,128)(2,1)S(1)}, u32[]{:S(2)}, u32[]{:S(2)}) collective-permute-start(bf16[256,1024]{1,0:T(8,128)(2,1)S(1)} %norm_only.3.refs_4_), channel_id=1, source_target_pairs={{0,4},{4,0},{8,12},{12,8},{1,5},{5,1},{9,13},{13,9},{2,6},{6,2},{1... | collective-permute-start | bytes 1572872 | tf_op jit(solution)/shard_map/ppermute | solution.py:73
  43.5 26.1 %collective-permute-start.23 = (bf16[512,1024]{1,0:T(8,128)(2,1)S(1)}, bf16[512,1024]{1,0:T(8,128)(2,1)S(1)}, u32[]{:S(2)}, u32[]{:S(2)}) collective-permute-start(bf16[512,1024]{1,0:T(8,128)(2,1)S(1)} %constant_dynamic-slice_fusion.1), channel_id=1, source_target_pairs={{0,16},{16,0},{1,17},{17,1},{2,18},{18,2},{3,19},{19,3},{4,20},{20... | collective-permute-start | bytes 3145736 | tf_op jit(solution)/shard_map/ppermute | solution.py:81
  57.9 26.6 %collective-permute-start.16 = (bf16[256,1024]{1,0:T(8,128)(2,1)S(1)}, bf16[256,1024]{1,0:T(8,128)(2,1)S(1)}, u32[]{:S(2)}, u32[]{:S(2)}) collective-permute-start(bf16[256,1024]{1,0:T(8,128)(2,1)S(1)} %dynamic-slice_bitcast_fusion.refs_0_.more_ref), channel_id=1, source_target_pairs={{0,8},{8,0},{4,12},{12,4},{1,9},{9,1},{5,13},{13,5},{2,10},{10,2},... | collective-permute-start | bytes 1572872 | tf_op jit(solution)/shard_map/ppermute | solution.py:77
  59.2 29.9 %collective-permute-start.25 = (bf16[512,1024]{1,0:T(8,128)(2,1)S(1)}, bf16[512,1024]{1,0:T(8,128)(2,1)S(1)}, u32[]{:S(2)}, u32[]{:S(2)}) collective-permute-start(bf16[512,1024]{1,0:T(8,128)(2,1)S(1)} %constant_dynamic-slice_fusion), channel_id=1, source_target_pairs={{0,16},{16,0},{1,17},{17,1},{2,18},{18,2},{3,19},{19,3},{4,20},{20... | collective-permute-start | bytes 3145736 | tf_op jit(solution)/shard_map/ppermute | solution.py:81
  69.6 36.4 %collective-permute-start.24 = (bf16[512,1024]{1,0:T(8,128)(2,1)S(1)}, bf16[512,1024]{1,0:T(8,128)(2,1)S(1)}, u32[]{:S(2)}, u32[]{:S(2)}) collective-permute-start(bf16[512,1024]{1,0:T(8,128)(2,1)S(1)} %collective-permute-done.23), channel_id=1, source_target_pairs={{0,1},{1,0},{2,3},{3,2},{4,5},{5,4},{6,7},{7,6},{8,9},{9,8},{10,11... | collective-permute-start | bytes 3145736 | tf_op jit(solution)/shard_map/ppermute | solution.py:710
  253.0 29.6 %collective-permute-start.65 = (bf16[256,1024]{1,0:T(8,128)(2,1)}, bf16[256,1024]{1,0:T(8,128)(2,1)}, u32[]{:S(2)}, u32[]{:S(2)}) collective-permute-start(bf16[256,1024]{1,0:T(8,128)(2,1)} %get-tuple-element.426), channel_id=1, source_target_pairs={{0,16},{16,0},{1,17},{17,1},{2,18},{18,2},{3,19},{19,3},{4,20},{20... | collective-permute-start | bytes 1572872 | tf_op jit(solution)/shard_map/ppermute | solution.py:81
  342.5 28.6 %collective-permute-start.97 = (bf16[256,1024]{1,0:T(8,128)(2,1)S(1)}, bf16[256,1024]{1,0:T(8,128)(2,1)S(1)}, u32[]{:S(2)}, u32[]{:S(2)}) collective-permute-start(bf16[256,1024]{1,0:T(8,128)(2,1)S(1)} %get-tuple-element.326), channel_id=1, source_target_pairs={{0,4},{4,0},{8,12},{12,8},{1,5},{5,1},{9,13},{13,9},{2,6},{6,2},{1... | collective-permute-start | bytes 1572872 | tf_op jit(solution)/shard_map/ppermute | solution.py:73
  342.8 26.7 %collective-permute-start.111 = (bf16[128,1024]{1,0:T(8,128)(2,1)S(1)}, bf16[128,1024]{1,0:T(8,128)(2,1)S(1)}, u32[]{:S(2)}, u32[]{:S(2)}) collective-permute-start(bf16[128,1024]{1,0:T(8,128)(2,1)S(1)} %add_convert_fusion.24), channel_id=1, source_target_pairs={{0,8},{8,0},{4,12},{12,4},{1,9},{9,1},{5,13},{13,5},{2,10},{10,2},... | collective-permute-start | bytes 786440 | tf_op jit(solution)/shard_map/ppermute | solution.py:77
  344.1 34.3 %collective-permute-start.100 = (bf16[128,1024]{1,0:T(8,128)(2,1)S(1)}, bf16[128,1024]{1,0:T(8,128)(2,1)S(1)}, u32[]{:S(2)}, u32[]{:S(2)}) collective-permute-start(bf16[128,1024]{1,0:T(8,128)(2,1)S(1)} %get-tuple-element.331), channel_id=1, source_target_pairs={{0,8},{8,0},{4,12},{12,4},{1,9},{9,1},{5,13},{13,5},{2,10},{10,2},... | collective-permute-start | bytes 786440 | tf_op jit(solution)/shard_map/ppermute | solution.py:77
  352.6 27.2 %collective-permute-start.116 = (bf16[512,1024]{1,0:T(8,128)(2,1)S(1)}, bf16[512,1024]{1,0:T(8,128)(2,1)S(1)}, u32[]{:S(2)}, u32[]{:S(2)}) collective-permute-start(bf16[512,1024]{1,0:T(8,128)(2,1)S(1)} %add_convert_fusion.10), channel_id=1, source_target_pairs={{1,2},{2,1},{5,6},{6,5},{9,10},{10,9},{13,14},{14,13},{17,18},{18,... | collective-permute-start | bytes 3145736 | tf_op jit(solution)/shard_map/ppermute | solution.py:677
  395.8 26.5 %collective-permute-start.117 = (bf16[512,1024]{1,0:T(8,128)(2,1)S(1)}, bf16[512,1024]{1,0:T(8,128)(2,1)S(1)}, u32[]{:S(2)}, u32[]{:S(2)}) collective-permute-start(bf16[512,1024]{1,0:T(8,128)(2,1)S(1)} %add_convert_fusion.6), channel_id=1, source_target_pairs={{0,1},{3,2},{4,5},{7,6},{8,9},{11,10},{12,13},{15,14},{16,17},{19,... | collective-permute-start | bytes 3145736 | tf_op jit(solution)/shard_map/ppermute | solution.py:677
  401.6 25.6 %collective-permute-start.104 = (bf16[512,1024]{1,0:T(8,128)(2,1)S(1)}, bf16[512,1024]{1,0:T(8,128)(2,1)S(1)}, u32[]{:S(2)}, u32[]{:S(2)}) collective-permute-start(bf16[512,1024]{1,0:T(8,128)(2,1)S(1)} %copy-done.70), channel_id=1, source_target_pairs={{0,16},{16,0},{1,17},{17,1},{2,18},{18,2},{3,19},{19,3},{4,20},{20... | collective-permute-start | bytes 3145736 | tf_op jit(solution)/shard_map/ppermute | solution.py:81
  407.2 39.8 %collective-permute-start.140 = (bf16[512,1024]{1,0:T(8,128)(2,1)S(1)}, bf16[512,1024]{1,0:T(8,128)(2,1)S(1)}, u32[]{:S(2)}, u32[]{:S(2)}) collective-permute-start(bf16[512,1024]{1,0:T(8,128)(2,1)S(1)} %add_convert_fusion.8), channel_id=1, source_target_pairs={{1,0},{2,3},{5,4},{6,7},{9,8},{10,11},{13,12},{14,15},{17,16},{18,... | collective-permute-start | bytes 3145736 | tf_op jit(solution)/shard_map/ppermute | solution.py:677
  422.7 25.6 %collective-permute-start.121 = (bf16[512,1024]{1,0:T(8,128)(2,1)S(1)}, bf16[512,1024]{1,0:T(8,128)(2,1)S(1)}, u32[]{:S(2)}, u32[]{:S(2)}) collective-permute-start(bf16[512,1024]{1,0:T(8,128)(2,1)S(1)} %add_convert_fusion.4), channel_id=1, source_target_pairs={{1,2},{2,1},{5,6},{6,5},{9,10},{10,9},{13,14},{14,13},{17,18},{18,... | collective-permute-start | bytes 3145736 | tf_op jit(solution)/shard_map/ppermute | solution.py:677
  428.2 25.8 %collective-permute-start.120 = (bf16[512,1024]{1,0:T(8,128)(2,1)S(1)}, bf16[512,1024]{1,0:T(8,128)(2,1)S(1)}, u32[]{:S(2)}, u32[]{:S(2)}) collective-permute-start(bf16[512,1024]{1,0:T(8,128)(2,1)S(1)} %add_convert_fusion.3), channel_id=1, source_target_pairs={{0,1},{3,2},{4,5},{7,6},{8,9},{11,10},{12,13},{15,14},{16,17},{19,... | collective-permute-start | bytes 3145736 | tf_op jit(solution)/shard_map/ppermute | solution.py:677
  446.7 60.7 %collective-permute-start.114 = (f32[8,1024]{1,0:T(8,128)S(1)}, f32[8,1024]{1,0:T(8,128)S(1)}, u32[]{:S(2)}, u32[]{:S(2)}) collective-permute-start(f32[8,1024]{1,0:T(8,128)S(1)} %fusion.21), channel_id=1, source_target_pairs={{0,16},{16,0},{1,17},{17,1},{2,18},{18,2},{3,19},{19,3},{4,20},{20... | collective-permute-start | bytes 98312 | tf_op jit(solution)/shard_map/ppermute | solution.py:81
  447.0 26.8 %collective-permute-start.141 = (bf16[512,1024]{1,0:T(8,128)(2,1)S(1)}, bf16[512,1024]{1,0:T(8,128)(2,1)S(1)}, u32[]{:S(2)}, u32[]{:S(2)}) collective-permute-start(bf16[512,1024]{1,0:T(8,128)(2,1)S(1)} %add_convert_fusion.5), channel_id=1, source_target_pairs={{1,0},{2,3},{5,4},{6,7},{9,8},{10,11},{13,12},{14,15},{17,16},{18,... | collective-permute-start | bytes 3145736 | tf_op jit(solution)/shard_map/ppermute | solution.py:677
  496.0 45.0 %collective-permute-start.139 = (bf16[512,1024]{1,0:T(8,128)(2,1)S(1)}, bf16[512,1024]{1,0:T(8,128)(2,1)S(1)}, u32[]{:S(2)}, u32[]{:S(2)}) collective-permute-start(bf16[512,1024]{1,0:T(8,128)(2,1)S(1)} %add_convert_fusion), channel_id=1, source_target_pairs={{1,0},{2,3},{5,4},{6,7},{9,8},{10,11},{13,12},{14,15},{17,16},{18,... | collective-permute-start | bytes 3145736 | tf_op jit(solution)/shard_map/ppermute | solution.py:677
  504.7 34.7 %collective-permute-start.135 = (bf16[352,1024]{1,0:T(8,128)(2,1)S(1)}, bf16[352,1024]{1,0:T(8,128)(2,1)S(1)}, u32[]{:S(2)}, u32[]{:S(2)}) collective-permute-start(bf16[352,1024]{1,0:T(8,128)(2,1)S(1)} %add_convert_fusion.12), channel_id=1, source_target_pairs={{1,0},{2,3},{5,4},{6,7},{9,8},{10,11},{13,12},{14,15},{17,16},{18,... | collective-permute-start | bytes 2162696 | tf_op jit(solution)/shard_map/ppermute | solution.py:677
  506.3 36.5 %collective-permute-start.130 = (bf16[336,1024]{1,0:T(8,128)(2,1)S(1)}, bf16[336,1024]{1,0:T(8,128)(2,1)S(1)}, u32[]{:S(2)}, u32[]{:S(2)}) collective-permute-start(bf16[336,1024]{1,0:T(8,128)(2,1)S(1)} %add_convert_fusion.20), channel_id=1, source_target_pairs={{1,2},{2,1},{5,6},{6,5},{9,10},{10,9},{13,14},{14,13},{17,18},{18,... | collective-permute-start | bytes 2064392 | tf_op jit(solution)/shard_map/ppermute | solution.py:677
  507.4 46.9 %collective-permute-start.136 = (bf16[336,1024]{1,0:T(8,128)(2,1)S(1)}, bf16[336,1024]{1,0:T(8,128)(2,1)S(1)}, u32[]{:S(2)}, u32[]{:S(2)}) collective-permute-start(bf16[336,1024]{1,0:T(8,128)(2,1)S(1)} %add_convert_fusion.19), channel_id=1, source_target_pairs={{1,0},{2,3},{5,4},{6,7},{9,8},{10,11},{13,12},{14,15},{17,16},{18,... | collective-permute-start | bytes 2064392 | tf_op jit(solution)/shard_map/ppermute | solution.py:677
  512.1 31.0 %collective-permute-start.128 = (bf16[336,1024]{1,0:T(8,128)(2,1)S(1)}, bf16[336,1024]{1,0:T(8,128)(2,1)S(1)}, u32[]{:S(2)}, u32[]{:S(2)}) collective-permute-start(bf16[336,1024]{1,0:T(8,128)(2,1)S(1)} %add_convert_fusion.18), channel_id=1, source_target_pairs={{0,1},{3,2},{4,5},{7,6},{8,9},{11,10},{12,13},{15,14},{16,17},{19,... | collective-permute-start | bytes 2064392 | tf_op jit(solution)/shard_map/ppermute | solution.py:677
  551.9 27.8 %collective-permute-start.133 = (bf16[336,1024]{1,0:T(8,128)(2,1)S(1)}, bf16[336,1024]{1,0:T(8,128)(2,1)S(1)}, u32[]{:S(2)}, u32[]{:S(2)}) collective-permute-start(bf16[336,1024]{1,0:T(8,128)(2,1)S(1)} %add_convert_fusion.15), channel_id=1, source_target_pairs={{1,0},{2,3},{5,4},{6,7},{9,8},{10,11},{13,12},{14,15},{17,16},{18,... | collective-permute-start | bytes 2064392 | tf_op jit(solution)/shard_map/ppermute | solution.py:677
  554.4 25.3 %collective-permute-start.134 = (f32[8,1024]{1,0:T(8,128)S(1)}, f32[8,1024]{1,0:T(8,128)S(1)}, u32[]{:S(2)}, u32[]{:S(2)}) collective-permute-start(f32[8,1024]{1,0:T(8,128)S(1)} %add.336), channel_id=1, source_target_pairs={{1,0},{2,3},{5,4},{6,7},{9,8},{10,11},{13,12},{14,15},{17,16},{18,... | collective-permute-start | bytes 98312 | tf_op jit(solution)/shard_map/ppermute | solution.py:677
  (195 other events, 2298.8 us)

commit v5 on v4

--- a/solution.py
+++ b/solution.py
@@ -1,4 +1,5 @@
 import functools
+from types import SimpleNamespace
 
 import jax
 import jax.numpy as jnp
@@ -9,6 +10,7 @@
 
 norm_eps = 1e-05
 masked_score = -1e30
+section_axis, head_axis, dp_axis = "section", "head", "dp"
 lanes = 128
 out_lane = 8
 log_lane = 16
@@ -70,15 +72,15 @@
 
 
 def to_core(a):
-    return lax.ppermute(a, "head", core_pairs)
+    return lax.ppermute(a, head_axis, core_pairs)
 
 
 def to_chip(a):
-    return lax.ppermute(a, "head", chip_pairs)
+    return lax.ppermute(a, head_axis, chip_pairs)
 
 
 def swap_section(a):
-    return lax.ppermute(a, "section", [(0, 1), (1, 0)])
+    return lax.ppermute(a, section_axis, [(0, 1), (1, 0)])
 
 
 def after(a, *tokens):
@@ -90,8 +92,16 @@
 
 
 def gather_slots(own):
+    return receive_half(send_half(own))
+
+
+def send_half(own):
     from_chip = to_chip(own)
-    from_core = to_core(own)
+    return own, to_core(own), from_chip
+
+
+def receive_half(half):
+    own, from_core, from_chip = half
     return [own, from_core, from_chip, to_core(from_chip)]
 
 
@@ -645,41 +655,47 @@
     )(*operands)
 
 
-class DpSums:
+class Chunk:
+    def __init__(self, own, moving):
+        self.own, self.moving, self.step, self.end = own, moving, 0, None
+
+
+class Turns:
     def __init__(self):
-        self.chunks = {}
         self.token = ()
-        self.direct = lax.axis_size("dp") != 4
-        place = lax.axis_index("dp")
+        self.direct = lax.axis_size(dp_axis) != 4
+        place = lax.axis_index(dp_axis)
         self.middle = (place == 1) | (place == 2)
 
-    def add(self, name, own, got):
-        self.chunks[name] = dict(own=own, moving=got, step=0)
-
-    def turns(self, *names):
-        for name in names:
-            self.turn(self.chunks[name])
+    def __call__(self, *chunks):
+        for chunk in chunks:
+            self.turn(chunk)
 
     def turn(self, chunk):
-        step = chunk["step"]
-        chunk["step"] += 1
+        step = chunk.step
+        chunk.step += 1
         if self.direct:
             if step == 0:
-                chunk["end"] = lax.psum(plus(chunk["own"], chunk["moving"]), "dp")
+                chunk.end = lax.psum(plus(chunk.own, chunk.moving), dp_axis)
             return
-        got = after(chunk["moving"], self.token)
+        got = after(chunk.moving, self.token)
         if step == 3:
-            chunk["end"] = jax.tree.map(lambda full, far: jnp.where(self.middle, full, far), chunk["own"], got)
+            chunk.end = jax.tree.map(lambda full, far: jnp.where(self.middle, full, far), chunk.own, got)
             return
-        total = plus(chunk["own"], got)
+        chunk.own = self.token = plus(chunk.own, got)
         pairs = ([(0, 1), (3, 2)], [(1, 2), (2, 1)], [(1, 0), (2, 3)])[step]
-        chunk["own"] = self.token = total
-        chunk["moving"] = jax.tree.map(lambda a: lax.ppermute(a, "dp", pairs), total)
-
-
-def split_tiles(rows, pieces):
-    size = rows // 16 // pieces * 16
-    return [rows - size * (pieces - 1)] + [size] * (pieces - 1)
+        chunk.moving = jax.tree.map(lambda a: lax.ppermute(a, dp_axis, pairs), chunk.own)
+
+
+def order_turns(chunks):
+    lags = (0, 1.5, 2.5, 3.5)
+    left = [(number + lags[step], step, number) for number, chunk in enumerate(chunks) for step in range(chunk.step, 4)]
+    return [chunks[number] for _, _, number in sorted(left)]
+
+
+def split_tiles(rows):
+    size = rows // 32 * 16
+    return [rows - size, size]
 
 
 def cut(a, pieces):
@@ -692,24 +708,20 @@
 
 
 def swap_weights(weights, start_after):
-    size = lax.axis_size("dp")
-    odd = lax.axis_index("dp") % 2
-    results = []
-    gots = []
-    for a, pieces in weights:
-        parts = []
-        for part in cut(a, pieces):
-            part = after(part, start_after, *gots[: max(0, len(gots) - 1)])
-            if size % 2:
-                gots.append(swap_section(part))
-                parts.append(gots[-1])
-                continue
-            rows = part.shape[0] // 2
-            gots.append(swap_section(lax.dynamic_slice_in_dim(part, odd * rows, rows, 0)))
-            got = gots[-1]
-            other = lax.ppermute(got, "dp", [(i, i ^ 1) for i in range(size)])
-            parts += [jnp.where(odd == 0, got, other), jnp.where(odd == 0, other, got)]
-        results.append(jnp.concatenate(parts, axis=0))
+    size = lax.axis_size(dp_axis)
+    odd = lax.axis_index(dp_axis) % 2
+    results, gots = [], []
+    for a in weights:
+        a = after(a, start_after, *gots[: max(0, len(gots) - 1)])
+        if size % 2:
+            gots.append(swap_section(a))
+            results.append(gots[-1])
+            continue
+        rows = a.shape[0] // 2
+        got = swap_section(lax.dynamic_slice_in_dim(a, odd * rows, rows, 0))
+        gots.append(got)
+        other = lax.ppermute(got, dp_axis, [(i, i ^ 1) for i in range(size)])
+        results.append(jnp.concatenate([jnp.where(odd == 0, got, other), jnp.where(odd == 0, other, got)], axis=0))
     return results
 
 
@@ -746,12 +758,12 @@
 ):
     experts = value_router.shape[-1]
     head_width = query_weight.shape[-1]
-    sec = lax.axis_index("section")
-    head = lax.axis_index("head")
+    sec = lax.axis_index(section_axis)
+    head = lax.axis_index(head_axis)
     me = head.astype(jnp.int32).reshape(1)
     first = sec == 0
     pick = lambda a, index: lax.dynamic_index_in_dim(a, index, 0, keepdims=False)
-    memory_len = memory.shape[2] * lax.axis_size("head")
+    memory_len = memory.shape[2] * lax.axis_size(head_axis)
 
     value_rows = experts * head_width
     router_rows = [padded_rows(a[0, 0].T, out_lane) for a in (value_router, out_router)]
@@ -775,8 +787,7 @@
     smalls = both_layers(small, small_got)
     route_sets = both_layers(pick(route_rows, sec), routes_got)
     memories = both_layers(pick(memory[0], sec), memory_got)
-    weights_got = swap_weights(list(zip(weights, (1, 1, 1, 1, 1))), sends)
-    weight_sets = [both_layers(a, got) for a, got in zip(weights, weights_got)]
+    weight_sets = [both_layers(a, got) for a, got in zip(weights, swap_weights(weights, sends))]
 
     x = pick(inputs, sec)
     cot = pick(out_cot, sec)
@@ -787,250 +798,205 @@
 
     layers = []
     for number in range(2):
+        layer = SimpleNamespace(mem=memories[number], w=[a[number] for a in weight_sets[:3]])
+        layer.wu, layer.wd = [a[number] for a in weight_sets[3:]]
         vec = smalls[number]
+        layer.gain1, layer.shift1, layer.gain2, layer.shift2, layer.up_b, layer.down_b = (vec[i : i + 1] for i in range(6))
         routes = route_sets[number]
-        layers.append(
-            dict(
-                gain1=vec[0:1],
-                shift1=vec[1:2],
-                gain2=vec[2:3],
-                shift2=vec[3:4],
-                up_b=vec[4:5],
-                down_b=vec[5:6],
-                w=(weight_sets[0][number], weight_sets[1][number], weight_sets[2][number]),
-                wu=weight_sets[3][number],
-                wd=weight_sets[4][number],
-                mask=route_mask(routes[:topk], routes[topk:, memory_len:], experts, memory_len),
-                mem=memories[number],
-            )
+        layer.mask = route_mask(routes[:topk], routes[topk:, memory_len:], experts, memory_len)
+        layers.append(layer)
+    one, two = layers
+    no_add = jnp.zeros_like(one.gain1)
+    for layer in layers:
+        layer.mem_slots = gather_slots(norm_only(after(layer.mem, own_norm), layer.gain1, layer.shift1))
+    cot_slots = gather_slots(after(cot, slots[2], one.mem_slots[2]))
+    slots[3] = after(slots[3], one.mask, two.mask)
+
+    def attention(layer, slots):
+        *out, layer.normed, q, k, v, ev, gate, att, layer.mixed = attn_fwd(
+            me, layer.mem_slots, slots, layer.w, layer.mask, experts, head_width
         )
-    one, two = layers
-    no_add = jnp.zeros_like(one["gain1"])
-    for layer in layers:
-        layer["mem_slots"] = gather_slots(norm_only(after(layer["mem"], own_norm), layer["gain1"], layer["shift1"]))
-    cot_slots = gather_slots(after(cot, slots[2], one["mem_slots"][2]))
-    slots[3] = after(slots[3], one["mask"], two["mask"])
-
-    def attention(layer, rows_in, slots):
-        *out, layer["normed"], q, k, v, ev, gate, att, layer["mixed"] = attn_fwd(
-            me, layer["mem_slots"], slots, layer["w"], layer["mask"], experts, head_width
-        )
-        layer["saved"] = (q, k, v, ev, gate, att)
+        layer.saved = (q, k, v, ev, gate, att)
         if layer is one:
-            out[3] = after(out[3], cot_slots[2], two["mem_slots"][2])
+            out[3] = after(out[3], cot_slots[2], two.mem_slots[2])
         terms, _ = scatter_halves(out)
-        layer["hidden"], slots = [], []
+        layer.hidden, halves = [], []
         for part in range(2):
-            hidden, normed = add_norm(rows_in[part], terms[part], part, no_add, layer["gain2"], layer["shift2"], f32)
-            layer["hidden"].append(hidden)
-            slots.append(gather_slots(normed))
-        return slots
-
-    one["rows"] = [x, x]
-    halves = attention(one, one["rows"], slots)
+            hidden, normed = add_norm(layer.rows[part], terms[part], part, no_add, layer.gain2, layer.shift2, f32)
+            layer.hidden.append(hidden)
+            halves.append(send_half(normed))
+        return [receive_half(half) for half in halves]
+
+    one.rows = [x, x]
+    halves = attention(one, slots)
     kept = ()
-    two["rows"], slots = [], []
+    two.rows, sent = [], []
     for part in range(2):
-        *out, n2, upper, active = ffn_fwd(halves[part], part, one["wu"], one["up_b"], one["wd"], kept)
+        pieces = halves[part]
+        *out, n2, upper, active = ffn_fwd(pieces, part, one.wu, one.up_b, one.wd, kept)
         kept = (n2, upper, active)
         terms, _ = scatter_slots(out)
-        rows, normed = add_norm(one["hidden"][part], terms, part, one["down_b"], two["gain1"], two["shift1"], bf16)
-        two["rows"].append(rows)
-        slots.append(gather_slots(normed))
-    one["n2"], one["upper"], one["active"] = kept
-    slots = [half[slot] for slot in range(4) for half in slots]
-    halves = attention(two, two["rows"], slots)
+        rows, normed = add_norm(one.hidden[part], terms, part, one.down_b, two.gain1, two.shift1, bf16)
+        two.rows.append(rows)
+        sent.append(send_half(normed))
+    one.n2, one.upper, one.active = kept
+    sent = [receive_half(half) for half in sent]
+    halves = attention(two, [half[slot] for slot in range(4) for half in sent])
 
     def by_layer(one, two):
         got = swap_section(jnp.where(first, two, one))
         kept = jnp.where(first, one, two)
         return jnp.stack([jnp.where(first, kept, got), jnp.where(first, got, kept)])[None]
 
-    def send_chunks(one, two, names, sizes):
+    def send_chunks(one, two, sizes):
         start = 0
-        for name, size in zip(names, sizes):
+        for size in sizes:
             part_one, part_two = one[start : start + size], two[start : start + size]
             start += size
             send = jnp.where(first, part_two, part_one)
-            if sums.chunks:
-                send = after(send, list(sums.chunks.values())[-1]["moving"])
-            sums.add(name, jnp.where(first, part_one, part_two), swap_section(send))
-
-    sums = DpSums()
-    grads = [{}, {}]
-    smalls_out, mem_grads = [None, None], [None, None]
-    input_grads = [None, None]
+            if chunks:
+                send = after(send, chunks[-1].moving)
+            chunks.append(Chunk(jnp.where(first, part_one, part_two), swap_section(send)))
+
+    chunks = []
+    turns = Turns()
     for number in (1, 0):
-        layer, grad = layers[number], grads[number]
-        wu, wd = layer["wu"], layer["wd"]
+        layer = layers[number]
         if number == 1:
             g_rows = [cot, cot]
         kept = ()
-        terms, bias = [], []
+        terms, layer.bias = [], []
         for part in range(2):
+            pieces = halves[part]
             if number == 1:
                 *out, sums_here, g_all, upper_grad, n2, active = ffn_bwd(
-                    cot_slots, part, wd, wu, kept, normed=halves[part], bu=layer["up_b"]
+                    cot_slots, part, layer.wd, layer.wu, kept, normed=pieces, bu=layer.up_b
                 )
                 kept = (g_all, upper_grad, n2, active)
             else:
-                *out, sums_here, g_all, upper_grad = ffn_bwd(halves[part], part, wd, wu, kept, upper=layer["upper"])
+                *out, sums_here, g_all, upper_grad = ffn_bwd(pieces, part, layer.wd, layer.wu, kept, upper=layer.upper)
                 kept = (g_all, upper_grad)
-                n2, active = layer["n2"], layer["active"]
-            bias.append(sums_here)
+                n2, active = layer.n2, layer.active
+            layer.bias.append(sums_here)
             terms_here, token = scatter_slots(out)
             terms.append(terms_here)
-        grad["down"] = t_dot(active, after(g_all, token)).astype(bf16)
-        grad["up"] = t_dot(after(n2, grad["down"]), upper_grad).astype(bf16)
+        layer.down = t_dot(active, after(g_all, token)).astype(bf16)
+        layer.up = t_dot(after(n2, layer.down), upper_grad).astype(bf16)
         if number == 0:
-            halved = [wd.shape[0] // 2] * 2
-            send_chunks(grad["down"], grads[1]["down"], ("down0", "down1"), halved)
-            send_chunks(grad["up"], grads[1]["up"], ("up0", "up1"), halved)
-        terms[1] = (*terms[1][0:2], after(terms[1][2], grad["up"]))
-        hidden_grads, a_halves, small2 = [], [], []
+            for grad, second in ((layer.down, two.down), (layer.up, two.up)):
+                send_chunks(grad, second, [grad.shape[0] // 2] * 2)
+        terms[1] = (*terms[1][0:2], after(terms[1][2], layer.up))
+        hidden_grads, layer.small2, sent = [], [], []
         for part in range(2):
-            dx, low, small_here = norm_back(layer["hidden"][part], terms[part], part, layer["gain2"], g_rows[part])
+            dx, low, small_here = norm_back(layer.hidden[part], terms[part], part, layer.gain2, g_rows[part])
             hidden_grads.append(dx)
-            small2.append(small_here)
-            a_halves.append(gather_slots(low))
-        a_slots = [half[slot] for slot in range(4) for half in a_halves]
+            layer.small2.append(small_here)
+            sent.append(send_half(low))
+        sent = [receive_half(half) for half in sent]
+        slots = [half[slot] for slot in range(4) for half in sent]
         if number == 0:
-            sums.turns("down0")
-            a_slots[7] = after(a_slots[7], sums.token)
+            turns(chunks[0])
+            slots[7] = after(slots[7], turns.token)
         else:
-            down_out = dot(active, after(wd, a_halves[1][0])).astype(bf16)
+            down_out = dot(active, after(layer.wd, low)).astype(bf16)
             rows = down_out.shape[0] // 8
             last_parts = [
                 jnp.concatenate([down_out[s * rows : (s + 1) * rows], down_out[(4 + s) * rows : (5 + s) * rows]])
                 for s in range(4)
             ]
-            last_terms, _ = scatter_halves(last_parts, a_halves[1][2])
-        *ngs, ngm, dproj, a_all = attn_bwd(me, a_slots, layer["w"], layer["saved"], experts, head_width)
+            last_terms, _ = scatter_halves(last_parts, sent[1][2])
+        *ngs, ngm, dproj, a_all = attn_bwd(me, slots, layer.w, layer.saved, experts, head_width)
         if number == 1:
             ngs[3] = after(ngs[3], [here[2] for here in last_terms])
             near, from_core, _ = last_terms[0]
-            last_out = jnp.concatenate(layer["hidden"]) + layer["down_b"] + near.astype(f32) + from_core.astype(f32)
+            last_out = jnp.concatenate(layer.hidden) + layer.down_b + near.astype(f32) + from_core.astype(f32)
             last_out = (last_out + jnp.concatenate([here[2] for here in last_terms]).astype(f32)).astype(bf16)
-            layer_out = by_layer(jnp.concatenate(layer["rows"]), last_out)
+            layer_out = by_layer(jnp.concatenate(layer.rows), last_out)
         terms, token = scatter_halves(ngs)
-        grad["attn"] = attn_grads(after(dproj, token), layer["normed"], layer["mixed"], a_all, experts, head_width)
-        token = grad["attn"]
+        layer.attn = attn_grads(after(dproj, token), layer.normed, layer.mixed, a_all, experts, head_width)
+        token = layer.attn
         if number == 0:
-            sizes = split_tiles(token.shape[0], 4)
-            send_chunks(token, grads[1]["attn"], ("attn0", "attn1", "attn2", "attn3"), sizes)
-            sums.token = token
-            sums.turns("down0", "down1")
-            token = sums.token
+            pack = (experts + 2) * head_width + 2 * out_lane
+            send_chunks(layer.attn, two.attn, split_tiles(pack) + split_tiles(value_rows))
+            turns.token = layer.attn
+            turns(chunks[0], chunks[1])
+            token = turns.token
         terms[1] = (*terms[1][0:2], after(terms[1][2], token))
-        rows_grads, low_grads, small1, halves = [], [], [], []
+        rows_grads, low_grads, layer.small1, halves = [], [], [], []
         for part in range(2):
-            dx, low, small_here = norm_back(layer["rows"][part], terms[part], part, layer["gain1"], hidden_grads[part])
+            dx, low, small_here = norm_back(layer.rows[part], terms[part], part, layer.gain1, hidden_grads[part])
             rows_grads.append(dx)
             low_grads.append(low)
-            small1.append(small_here)
-            if number == 1:
-                halves.append(gather_slots(low))
-        g_rows = rows_grads if number == 0 else low_grads
-        mem_grads[number] = cut(ngm, 4)
-        input_grads[number] = jnp.concatenate(low_grads)
-        smalls_out[number] = (small1[0] + small1[1], small2[0] + small2[1], bias[0] + bias[1])
-
-    mem_terms, _ = scatter_slots([jnp.concatenate(pair) for pair in zip(*mem_grads)])
-    rows = memories[0].shape[0]
+            layer.small1.append(small_here)
+            halves.append(send_half(low) if number == 1 else (low,))
+        if number == 1:
+            halves = [receive_half(half) for half in halves]
+        g_rows = low_grads
+        layer.mem_grads = cut(ngm, 4)
+        layer.input_grad = jnp.concatenate(low_grads)
+
+    mem_terms, _ = scatter_slots([jnp.concatenate(pair) for pair in zip(one.mem_grads, two.mem_grads)])
+    rows = one.mem.shape[0]
     vecs = []
-    for number, (small1, small2, bias) in enumerate(smalls_out):
-        here = slice(number * rows, (number + 1) * rows)
-        small_mem = norm_back_small(layers[number]["mem"], [a[here] for a in mem_terms])
-        vecs.append(jnp.concatenate([(small1 + small_mem)[0:2], small2[0:6]]))
+    for number, layer in enumerate(layers):
+        small_mem = norm_back_small(layer.mem, [a[number * rows : (number + 1) * rows] for a in mem_terms])
+        vecs.append((layer.small1[0] + layer.small1[1] + small_mem)[0:2])
+        vecs.append((layer.small2[0] + layer.small2[1])[0:6])
     vec = jnp.concatenate(vecs)
     vec = vec + to_core(vec)
     vec = vec + to_chip(vec)
-    vecs = [jnp.concatenate([part[0:5], bias, part[6:8]]) for part, (_, _, bias) in zip(cut(vec, 2), smalls_out)]
-    last_chunk = sums.chunks["attn3"]
-    last_chunk["own"] = (last_chunk["own"], jnp.where(first, vecs[0], vecs[1]))
-    last_chunk["moving"] = (last_chunk["moving"], swap_section(jnp.where(first, vecs[1], vecs[0])))
-    sums.turns("down0", "down1", "up0", "down0", "down1", "up0", "up1", "down1", "attn0", "up0", "up1", "attn0", "attn1")
-    sums.turns("up0", "up1", "attn1", "attn2", "attn0", "up1", "attn2", "attn1", "attn3")
-    last_sum = sums.token
-    sums.turns("attn0", "attn2", "attn3", "attn1", "attn3", "attn2", "attn3")
-    ends = {name: chunk["end"] for name, chunk in sums.chunks.items()}
-    ends["attn3"], vec = ends["attn3"]
-    input_grad = by_layer(*[after(a, last_sum) for a in input_grads])
-    join = lambda *names: jnp.concatenate([ends[name] for name in names]).astype(f32)
-    down_sum, up_sum = join("down0", "down1"), join("up0", "up1")
-    attn_sum = join("attn0", "attn1", "attn2", "attn3")
+    vecs = [
+        jnp.concatenate([part[0:5], layer.bias[0] + layer.bias[1], part[6:8]]) for part, layer in zip(cut(vec, 2), layers)
+    ]
+    down0, down1, up0, up1, pack0, pack1, out0, out1 = chunks
+    out1.own = (out1.own, jnp.where(first, vecs[0], vecs[1]))
+    out1.moving = (out1.moving, swap_section(jnp.where(first, vecs[1], vecs[0])))
+    for chunk in order_turns(chunks):
+        turns(chunk)
+        if chunk is out1 and chunk.step == 1:
+            last_sum = turns.token
+    out_end, vec = out1.end
+    input_grad = by_layer(*[after(layer.input_grad, last_sum) for layer in layers])
+    join = lambda *parts: jnp.concatenate(parts).astype(f32)
+    pack_sum = join(pack0.end, pack1.end)
 
     def take(start, count):
-        return attn_sum[start : start + count]
-
-    routers = value_rows + 2 * out_lane
-    value_sum, vroute_sum, oroute_sum = take(0, value_rows), take(value_rows, experts), take(value_rows + out_lane, experts)
-    key_sum, query_sum = take(routers, head_width), take(routers + head_width, head_width)
-    out_sum = take(routers + 2 * head_width, value_rows)
+        return pack_sum[start : start + count].T[None, None]
+
+    keys = value_rows + 2 * out_lane
 
     return (
         layer_out,
         input_grad,
         vec[0:1],
         vec[1:2],
-        query_sum.T[None, None],
-        key_sum.T[None, None],
-        value_sum.T[None, None],
-        vroute_sum.T[None, None],
-        oroute_sum.T[None, None],
-        out_sum[None, None],
+        take(keys + head_width, head_width),
+        take(keys, head_width),
+        take(0, value_rows),
+        take(value_rows, experts),
+        take(value_rows + out_lane, experts),
+        join(out0.end, out_end)[None, None],
         vec[2:3],
         vec[3:4],
-        up_sum[None],
+        join(up0.end, up1.end)[None],
         vec[5:6],
-        down_sum[None],
+        join(down0.end, down1.end)[None],
         vec[4:5],
     )
 
 
 def solution(mesh):
-    placed = (
-        P("dp", "head", None),
-        P("section", "dp", "head", None),
-        P("section", "dp", None, "head", None),
-        P("section", "dp", None, "head", None),
-        P("section", None),
-        P("section", None),
-        P("section", "head", None, None),
-        P("section", "head", None, None),
-        P("section", "head", None, None),
-        P("section", "head", None, None),
-        P("section", "head", None, None),
-        P("section", "head", None, None),
-        P("section", None),
-        P("section", None),
-        P("section", None, "head"),
-        P("section", "head"),
-        P("section", "head", None),
-        P("section", None),
-        P("dp", "head", None),
-    )
+    rows = P(dp_axis, head_axis, None)
+    layer_rows = P(section_axis, dp_axis, head_axis, None)
+    routes = P(section_axis, dp_axis, None, head_axis, None)
+    by_layer = P(section_axis, None)
+    by_head = P(section_axis, head_axis, None, None)
+    up, up_shift, down = P(section_axis, None, head_axis), P(section_axis, head_axis), P(section_axis, head_axis, None)
+    params = [by_layer] * 2 + [by_head] * 6 + [by_layer] * 2 + [up, up_shift, down, by_layer]
     return jax.shard_map(
         on_device,
         mesh=mesh,
-        in_specs=placed,
-        out_specs=(
-            P("section", "dp", "head", None),
-            P("section", "dp", "head", None),
-            P("section", None),
-            P("section", None),
-            P("section", "head", None, None),
-            P("section", "head", None, None),
-            P("section", "head", None, None),
-            P("section", "head", None, None),
-            P("section", "head", None, None),
-            P("section", "head", None, None),
-            P("section", None),
-            P("section", None),
-            P("section", None, "head"),
-            P("section", "head"),
-            P("section", "head", None),
-            P("section", None),
-        ),
+        in_specs=(rows, layer_rows, routes, routes, *params, rows),
+        out_specs=(layer_rows, layer_rows, *params),
         check_vma=False,
     )

time: 594 us -> 568 us (0.956)
  waiting for transfers between devices: 278 us -> 251 us
    ppermute x142, waiting for transfers between devices: 278 us -> 251 us  [the longest x34 101 us: to_chip(): return lax.ppermute(a, head_axis, chip_pairs)]
  transfers between devices with their start and end apart: 142 -> 142, of which waited for: 55 -> 52; matrix products, arithmetic and copies ran while one was open for 10% -> 11% of each run, Pallas kernels for 13% -> 11%
where the time goes in v5:
time: 568 us; the launch traced here: 561 us
  waiting for transfers between devices  251 us (44%)
  starting transfers between devices  135 us (24%)
  Pallas kernels  93.6 us (16%)
  other arithmetic  41.1 us (7%)
  local copies, waits for them, and re-layouts  22.9 us (4%)
  matrix products  14.7 us (3%)
    ppermute x34, waiting for transfers between devices, to_chip(): return lax.ppermute(a, head_axis, chip_pairs)  101 us
    ppermute x19, waiting for transfers between devices, swap_section(): return lax.ppermute(a, section_axis, [(0, 1), (1, 0)])  78.2 us
    ppermute x27, waiting for transfers between devices, turn(): lax.ppermute(a, dp_axis, pairs)  57 us
    ppermute x27, starting transfers between devices, turn(): lax.ppermute(a, dp_axis, pairs)  53.5 us
    ppermute x34, starting transfers between devices, to_chip(): return lax.ppermute(a, head_axis, chip_pairs)  39.8 us
    ppermute x19, starting transfers between devices, swap_section(): return lax.ppermute(a, section_axis, [(0, 1), (1, 0)])  24 us
    pallas_call x2, Pallas kernels, attn_bwd(): pl.pallas_call(functools.partial(attn_bwd_kernel, experts, head_width, le...  21.7 us
    pallas_call x2, Pallas kernels, attn_fwd(): pl.pallas_call(functools.partial(attn_fwd_kernel, experts, head_width, le...  20.1 us
  transfers between devices with their start and end apart: 142, of which 52 were waited for; matrix products, arithmetic and copies ran while one was open for 11% of the time, Pallas kernels for 11%

profile of v5, /device:TPU:0, one launch (start us, length us, event | category | flops | bytes accessed | tf_op | source)
XLA Modules:
  0.0 561.3 jit_solution(10650855014975054436)
XLA Ops:
  21.2 8.7 %collective-permute-done.9 = bf16[280,1024]{1,0:T(8,128)(2,1)} collective-permute-done((bf16[280,1024]{1,0:T(8,128)(2,1)}, bf16[280,1024]{1,0:T(8,128)(2,1)}, u32[]{:S(2)}, u32[]{:S(2)}) %collective-permute-start.9) | collective-permute-done | bytes 573472 | tf_op jit(solution)/shard_map/ppermute | solution.py:83
  48.5 9.4 %collective-permute-done.14 = bf16[280,1024]{1,0:T(8,128)(2,1)S(1)} collective-permute-done((bf16[280,1024]{1,0:T(8,128)(2,1)S(1)}, bf16[280,1024]{1,0:T(8,128)(2,1)S(1)}, u32[]{:S(2)}, u32[]{:S(2)}) %collective-permute-start.14) | collective-permute-done | bytes 573472 | tf_op jit(solution)/shard_map/ppermute | solution.py:723
  61.1 8.5 %collective-permute-done.23 = bf16[512,1024]{1,0:T(8,128)(2,1)S(1)} collective-permute-done((bf16[512,1024]{1,0:T(8,128)(2,1)S(1)}, bf16[512,1024]{1,0:T(8,128)(2,1)S(1)}, u32[]{:S(2)}, u32[]{:S(2)}) %collective-permute-start.23) | collective-permute-done | bytes 1048608 | tf_op jit(solution)/shard_map/ppermute | solution.py:83
  71.0 10.2 %attn_fwd.2 = (bf16[256,1024]{1,0:T(8,128)(2,1)S(1)}, bf16[256,1024]{1,0:T(8,128)(2,1)S(1)}, bf16[256,1024]{1,0:T(8,128)(2,1)S(1)}, bf16[256,1024]{1,0:T(8,128)(...) custom-call(s32[1]{0:T(128)} %bitcast.1.me_ref, ...), custom_call_target="tpu_custom_call" | custom-call | flops 3355443200 | bytes 16777216 | tf_op jit(solution)/shard_map/attn_fwd/pallas_call | solution.py:338
  92.6 7.2 %collective-permute-done.30.c_ref = bf16[128,1024]{1,0:T(8,128)(2,1)S(1)} collective-permute-done((bf16[128,1024]{1,0:T(8,128)(2,1)S(1)}, bf16[128,1024]{1,0:T(8,128)(2,1)S(1)}, u32[]{:S(2)}, u32[]{:S(2)}) %collective-permute-start.30) | collective-permute-done | bytes 262176 | tf_op jit(solution)/shard_map/ppermute | solution.py:79
  126.6 6.7 %collective-permute-done.29.c_ref = bf16[128,1024]{1,0:T(8,128)(2,1)S(1)} collective-permute-done((bf16[128,1024]{1,0:T(8,128)(2,1)S(1)}, bf16[128,1024]{1,0:T(8,128)(2,1)S(1)}, u32[]{:S(2)}, u32[]{:S(2)}) %collective-permute-start.29) | collective-permute-done | bytes 262176 | tf_op jit(solution)/shard_map/ppermute | solution.py:79
  151.5 10.0 %attn_fwd.3 = (bf16[256,1024]{1,0:T(8,128)(2,1)S(1)}, bf16[256,1024]{1,0:T(8,128)(2,1)S(1)}, bf16[256,1024]{1,0:T(8,128)(2,1)S(1)}, bf16[256,1024]{1,0:T(8,128)(...) custom-call(s32[1]{0:T(128)} %bitcast.1.me_ref, ...), custom_call_target="tpu_custom_call" | custom-call | flops 3355443200 | bytes 16777216 | tf_op jit(solution)/shard_map/attn_fwd/pallas_call | solution.py:338
  168.3 6.6 %collective-permute-done.47.c_ref = bf16[128,1024]{1,0:T(8,128)(2,1)S(1)} collective-permute-done((bf16[128,1024]{1,0:T(8,128)(2,1)S(1)}, bf16[128,1024]{1,0:T(8,128)(2,1)S(1)}, u32[]{:S(2)}, u32[]{:S(2)}) %collective-permute-start.47) | collective-permute-done | bytes 262176 | tf_op jit(solution)/shard_map/ppermute | solution.py:79
  196.3 5.6 %ffn_bwd.5 = (bf16[128,1024]{1,0:T(8,128)(2,1)S(1)}, bf16[128,1024]{1,0:T(8,128)(2,1)S(1)}, bf16[128,1024]{1,0:T(8,128)(2,1)S(1)}, bf16[128,1024]{1,0:T(8,128)(2...) custom-call(bf16[256,1024]{1,0:T(8,128)(2,1)S(1)} %dynamic-slice_bit, ...), custom_call_target="tpu_custom_call", output_to_operand_aliasing={{5}: (11, {}), {6}: (12, {}), {7}: (13, {}), {8}: (14, {})} | custom-call | flops 2147483648 | bytes 9437184 | tf_op jit(solution)/shard_map/ffn_bwd/pallas_call | solution.py:593
  220.8 5.9 %collective-permute-done.62.refs_5_ = bf16[128,1024]{1,0:T(8,128)(2,1)S(1)} collective-permute-done((bf16[128,1024]{1,0:T(8,128)(2,1)S(1)}, bf16[128,1024]{1,0:T(8,128)(2,1)S(1)}, u32[]{:S(2)}, u32[]{:S(2)}) %collective-permute-start.62) | collective-permute-done | bytes 262176 | tf_op jit(solution)/shard_map/ppermute | solution.py:79
  234.3 11.1 %attn_bwd.2 = (bf16[256,1024]{1,0:T(8,128)(2,1)S(1)}, bf16[256,1024]{1,0:T(8,128)(2,1)}, bf16[256,1024]{1,0:T(8,128)(2,1)S(1)}, bf16[256,1024]{1,0:T(8,128)(2,1)...) custom-call(s32[1]{0:T(128)} %bitcast.1.me_ref, ...), custom_call_target="tpu_custom_call" | custom-call | flops 3355443200 | bytes 16777216 | tf_op jit(solution)/shard_map/attn_bwd/pallas_call | solution.py:446
  261.2 5.7 %attn_grads.2 = bf16[1360,1024]{1,0:T(8,128)(2,1)S(1)} custom-call(bf16[1280,1024]{1,0:T(8,128)(2,1)S(1)} %copy-done.13, bf16[1280,1024]{1,0:T(8,128)(2,1)S(1)} %copy-done.11, bf16[1024,640]{1,0:T(8,128)(2,1)S(1)} %copy-done.23, bf16[1024,1024]{1,0:T(8,128)(2,1)S(1)} %copy-done.15), custom_call_target="tpu_custom_call" | custom-call | tf_op jit(solution)/shard_map/attn_grads/pallas_call | solution.py:645
  304.6 5.5 collective-permute-done.82.c_ref
  326.8 10.6 %attn_bwd.3 = (bf16[256,1024]{1,0:T(8,128)(2,1)S(1)}, bf16[256,1024]{1,0:T(8,128)(2,1)S(1)}, bf16[256,1024]{1,0:T(8,128)(2,1)S(1)}, bf16[256,1024]{1,0:T(8,128)(...) custom-call(s32[1]{0:T(128)} %bitcast.1.me_ref, ...), custom_call_target="tpu_custom_call" | custom-call | flops 3355443200 | bytes 16777216 | tf_op jit(solution)/shard_map/attn_bwd/pallas_call | solution.py:446
  343.8 5.7 %attn_grads.3 = bf16[1360,1024]{1,0:T(8,128)(2,1)S(1)} custom-call(bf16[1280,1024]{1,0:T(8,128)(2,1)S(1)} %get-tuple-element.334.refs_0_, bf16[1280,1024]{1,0:T(8,128)(2,1)S(1)} %copy-done.9, bf16[1024,640]{1,0:T(8,128)(2,1)S(1)} %copy-done.21, bf16[1024,1024]{1,0:T(8,128)(2,1)S(1)} %get-tuple-element.337.refs_3_), custom_call_target="tpu_custom_call" | custom-call | tf_op jit(solution)/shard_map/attn_grads/pallas_call | solution.py:645
  352.2 8.9 %collective-permute-done.99.c_ref = bf16[128,1024]{1,0:T(8,128)(2,1)S(1)} collective-permute-done((bf16[128,1024]{1,0:T(8,128)(2,1)S(1)}, bf16[128,1024]{1,0:T(8,128)(2,1)S(1)}, u32[]{:S(2)}, u32[]{:S(2)}) %collective-permute-start.99) | collective-permute-done | bytes 262176 | tf_op jit(solution)/shard_map/ppermute | solution.py:79
  369.8 5.9 %collective-permute-start.115 = (bf16[512,1024]{1,0:T(8,128)(2,1)S(1)}, bf16[512,1024]{1,0:T(8,128)(2,1)S(1)}, u32[]{:S(2)}, u32[]{:S(2)}) collective-permute-start(bf16[512,1024]{1,0:T(8,128)(2,1)S(1)} %add_convert_fusion.9), channel_id=1, source_target_pairs={{0,1},{3,2},{4,5},{7,6},{8,9},{11,10},{12,13},{15,14},{16,17},{19,... | collective-permute-start | bytes 3145736 | tf_op jit(solution)/shard_map/ppermute | solution.py:687
  380.1 14.1 %collective-permute-done.103 = bf16[512,1024]{1,0:T(8,128)(2,1)S(1)} collective-permute-done((bf16[512,1024]{1,0:T(8,128)(2,1)S(1)}, bf16[512,1024]{1,0:T(8,128)(2,1)S(1)}, u32[]{:S(2)}, u32[]{:S(2)}) %collective-permute-start.103) | collective-permute-done | bytes 1048608 | tf_op jit(solution)/shard_map/ppermute | solution.py:83
  403.9 15.4 %collective-permute-done.104 = bf16[512,1024]{1,0:T(8,128)(2,1)S(1)} collective-permute-done((bf16[512,1024]{1,0:T(8,128)(2,1)S(1)}, bf16[512,1024]{1,0:T(8,128)(2,1)S(1)}, u32[]{:S(2)}, u32[]{:S(2)}) %collective-permute-start.104) | collective-permute-done | bytes 1048608 | tf_op jit(solution)/shard_map/ppermute | solution.py:83
  428.9 11.4 %collective-permute-done.105 = bf16[400,1024]{1,0:T(8,128)(2,1)S(1)} collective-permute-done((bf16[400,1024]{1,0:T(8,128)(2,1)S(1)}, bf16[400,1024]{1,0:T(8,128)(2,1)S(1)}, u32[]{:S(2)}, u32[]{:S(2)}) %collective-permute-start.105) | collective-permute-done | bytes 819232 | tf_op jit(solution)/shard_map/ppermute | solution.py:83
  455.6 7.4 %collective-permute-done.106 = bf16[400,1024]{1,0:T(8,128)(2,1)S(1)} collective-permute-done((bf16[400,1024]{1,0:T(8,128)(2,1)S(1)}, bf16[400,1024]{1,0:T(8,128)(2,1)S(1)}, u32[]{:S(2)}, u32[]{:S(2)}) %collective-permute-start.106) | collective-permute-done | bytes 819232 | tf_op jit(solution)/shard_map/ppermute | solution.py:83
  490.4 9.2 %collective-permute-start.127 = (f32[8,1024]{1,0:T(8,128)S(1)}, f32[8,1024]{1,0:T(8,128)S(1)}, u32[]{:S(2)}, u32[]{:S(2)}) collective-permute-start(f32[8,1024]{1,0:T(8,128)S(1)} %select_add_fusion.1), channel_id=1, source_target_pairs={{0,1},{3,2},{4,5},{7,6},{8,9},{11,10},{12,13},{15,14},{16,17},{19,... | collective-permute-start | bytes 98312 | tf_op jit(solution)/shard_map/ppermute | solution.py:687
  508.7 7.6 %collective-permute-done.135 = bf16[400,1024]{1,0:T(8,128)(2,1)S(1)} collective-permute-done((bf16[400,1024]{1,0:T(8,128)(2,1)S(1)}, bf16[400,1024]{1,0:T(8,128)(2,1)S(1)}, u32[]{:S(2)}, u32[]{:S(2)}) %collective-permute-start.135) | collective-permute-done | bytes 819232 | tf_op jit(solution)/shard_map/ppermute | solution.py:687
  524.8 27.1 %collective-permute-done.137 = bf16[288,1024]{1,0:T(8,128)(2,1)S(1)} collective-permute-done((bf16[288,1024]{1,0:T(8,128)(2,1)S(1)}, bf16[288,1024]{1,0:T(8,128)(2,1)S(1)}, u32[]{:S(2)}, u32[]{:S(2)}) %collective-permute-start.137) | collective-permute-done | bytes 589856 | tf_op jit(solution)/shard_map/ppermute | solution.py:687
  (580 shorter events, 333.5 us)
Async XLA Ops:
  6.5 24.8 %collective-permute-start = (bf16[64,1024]{1,0:T(8,128)(2,1)S(1)}, bf16[64,1024]{1,0:T(8,128)(2,1)}, u32[]{:S(2)}, u32[]{:S(2)}) collective-permute-start(bf16[64,1024]{1,0:T(8,128)(2,1)S(1)} %dynamic-slice_bitcast_fusion.2), channel_id=1, source_target_pairs={{0,16},{16,0},{1,17},{17,1},{2,18},{18,2},{3,19},{19,3},{4,20},{20... | collective-permute-start | bytes 393224 | tf_op jit(solution)/shard_map/ppermute | solution.py:83
  16.8 54.1 %collective-permute-start.5 = (bf16[256,1024]{1,0:T(8,128)(2,1)S(1)}, bf16[256,1024]{1,0:T(8,128)(2,1)S(1)}, u32[]{:S(2)}, u32[]{:S(2)}) collective-permute-start(bf16[256,1024]{1,0:T(8,128)(2,1)S(1)} %norm_only.3.refs_4_), channel_id=1, source_target_pairs={{0,4},{4,0},{8,12},{12,8},{1,5},{5,1},{9,13},{13,9},{2,6},{6,2},{1... | collective-permute-start | bytes 1572872 | tf_op jit(solution)/shard_map/ppermute | solution.py:75
  43.5 26.1 %collective-permute-start.23 = (bf16[512,1024]{1,0:T(8,128)(2,1)S(1)}, bf16[512,1024]{1,0:T(8,128)(2,1)S(1)}, u32[]{:S(2)}, u32[]{:S(2)}) collective-permute-start(bf16[512,1024]{1,0:T(8,128)(2,1)S(1)} %constant_dynamic-slice_fusion.1), channel_id=1, source_target_pairs={{0,16},{16,0},{1,17},{17,1},{2,18},{18,2},{3,19},{19,3},{4,20},{20... | collective-permute-start | bytes 3145736 | tf_op jit(solution)/shard_map/ppermute | solution.py:83
  57.9 26.6 %collective-permute-start.16 = (bf16[256,1024]{1,0:T(8,128)(2,1)S(1)}, bf16[256,1024]{1,0:T(8,128)(2,1)S(1)}, u32[]{:S(2)}, u32[]{:S(2)}) collective-permute-start(bf16[256,1024]{1,0:T(8,128)(2,1)S(1)} %dynamic-slice_bitcast_fusion.refs_0_.more_ref), channel_id=1, source_target_pairs={{0,8},{8,0},{4,12},{12,4},{1,9},{9,1},{5,13},{13,5},{2,10},{10,2},... | collective-permute-start | bytes 1572872 | tf_op jit(solution)/shard_map/ppermute | solution.py:79
  59.2 29.9 %collective-permute-start.25 = (bf16[512,1024]{1,0:T(8,128)(2,1)S(1)}, bf16[512,1024]{1,0:T(8,128)(2,1)S(1)}, u32[]{:S(2)}, u32[]{:S(2)}) collective-permute-start(bf16[512,1024]{1,0:T(8,128)(2,1)S(1)} %constant_dynamic-slice_fusion), channel_id=1, source_target_pairs={{0,16},{16,0},{1,17},{17,1},{2,18},{18,2},{3,19},{19,3},{4,20},{20... | collective-permute-start | bytes 3145736 | tf_op jit(solution)/shard_map/ppermute | solution.py:83
  69.6 36.4 %collective-permute-start.24 = (bf16[512,1024]{1,0:T(8,128)(2,1)S(1)}, bf16[512,1024]{1,0:T(8,128)(2,1)S(1)}, u32[]{:S(2)}, u32[]{:S(2)}) collective-permute-start(bf16[512,1024]{1,0:T(8,128)(2,1)S(1)} %collective-permute-done.23), channel_id=1, source_target_pairs={{0,1},{1,0},{2,3},{3,2},{4,5},{5,4},{6,7},{7,6},{8,9},{9,8},{10,11... | collective-permute-start | bytes 3145736 | tf_op jit(solution)/shard_map/ppermute | solution.py:723
  253.0 29.6 %collective-permute-start.65 = (bf16[256,1024]{1,0:T(8,128)(2,1)}, bf16[256,1024]{1,0:T(8,128)(2,1)}, u32[]{:S(2)}, u32[]{:S(2)}) collective-permute-start(bf16[256,1024]{1,0:T(8,128)(2,1)} %get-tuple-element.426), channel_id=1, source_target_pairs={{0,16},{16,0},{1,17},{17,1},{2,18},{18,2},{3,19},{19,3},{4,20},{20... | collective-permute-start | bytes 1572872 | tf_op jit(solution)/shard_map/ppermute | solution.py:83
  301.1 24.9 %collective-permute-start.96 = (bf16[512,1024]{1,0:T(8,128)(2,1)S(1)}, bf16[512,1024]{1,0:T(8,128)(2,1)S(1)}, u32[]{:S(2)}, u32[]{:S(2)}) collective-permute-start(bf16[512,1024]{1,0:T(8,128)(2,1)S(1)} %get-tuple-element.431), channel_id=1, source_target_pairs={{0,16},{16,0},{1,17},{17,1},{2,18},{18,2},{3,19},{19,3},{4,20},{20... | collective-permute-start | bytes 3145736 | tf_op jit(solution)/shard_map/ppermute | solution.py:83
  338.2 25.4 %collective-permute-start.102 = (bf16[512,1024]{1,0:T(8,128)(2,1)S(1)}, bf16[512,1024]{1,0:T(8,128)(2,1)S(1)}, u32[]{:S(2)}, u32[]{:S(2)}) collective-permute-start(bf16[512,1024]{1,0:T(8,128)(2,1)S(1)} %add_convert_fusion.11), channel_id=1, source_target_pairs={{0,1},{3,2},{4,5},{7,6},{8,9},{11,10},{12,13},{15,14},{16,17},{19,... | collective-permute-start | bytes 3145736 | tf_op jit(solution)/shard_map/ppermute | solution.py:687
  340.9 25.6 %collective-permute-start.101 = (bf16[512,1024]{1,0:T(8,128)(2,1)S(1)}, bf16[512,1024]{1,0:T(8,128)(2,1)S(1)}, u32[]{:S(2)}, u32[]{:S(2)}) collective-permute-start(bf16[512,1024]{1,0:T(8,128)(2,1)S(1)} %copy-done.72), channel_id=1, source_target_pairs={{0,16},{16,0},{1,17},{17,1},{2,18},{18,2},{3,19},{19,3},{4,20},{20... | collective-permute-start | bytes 3145736 | tf_op jit(solution)/shard_map/ppermute | solution.py:83
  368.6 25.6 %collective-permute-start.103 = (bf16[512,1024]{1,0:T(8,128)(2,1)S(1)}, bf16[512,1024]{1,0:T(8,128)(2,1)S(1)}, u32[]{:S(2)}, u32[]{:S(2)}) collective-permute-start(bf16[512,1024]{1,0:T(8,128)(2,1)S(1)} %copy-done.71), channel_id=1, source_target_pairs={{0,16},{16,0},{1,17},{17,1},{2,18},{18,2},{3,19},{19,3},{4,20},{20... | collective-permute-start | bytes 3145736 | tf_op jit(solution)/shard_map/ppermute | solution.py:83
  369.1 31.2 %collective-permute-start.118 = (bf16[512,1024]{1,0:T(8,128)(2,1)S(1)}, bf16[512,1024]{1,0:T(8,128)(2,1)S(1)}, u32[]{:S(2)}, u32[]{:S(2)}) collective-permute-start(bf16[512,1024]{1,0:T(8,128)(2,1)S(1)} %add_convert_fusion.10), channel_id=1, source_target_pairs={{1,2},{2,1},{5,6},{6,5},{9,10},{10,9},{13,14},{14,13},{17,18},{18,... | collective-permute-start | bytes 3145736 | tf_op jit(solution)/shard_map/ppermute | solution.py:687
  369.8 29.4 %collective-permute-start.115 = (bf16[512,1024]{1,0:T(8,128)(2,1)S(1)}, bf16[512,1024]{1,0:T(8,128)(2,1)S(1)}, u32[]{:S(2)}, u32[]{:S(2)}) collective-permute-start(bf16[512,1024]{1,0:T(8,128)(2,1)S(1)} %add_convert_fusion.9), channel_id=1, source_target_pairs={{0,1},{3,2},{4,5},{7,6},{8,9},{11,10},{12,13},{15,14},{16,17},{19,... | collective-permute-start | bytes 3145736 | tf_op jit(solution)/shard_map/ppermute | solution.py:687
  394.2 25.1 %collective-permute-start.104 = (bf16[512,1024]{1,0:T(8,128)(2,1)S(1)}, bf16[512,1024]{1,0:T(8,128)(2,1)S(1)}, u32[]{:S(2)}, u32[]{:S(2)}) collective-permute-start(bf16[512,1024]{1,0:T(8,128)(2,1)S(1)} %copy-done.70), channel_id=1, source_target_pairs={{0,16},{16,0},{1,17},{17,1},{2,18},{18,2},{3,19},{19,3},{4,20},{20... | collective-permute-start | bytes 3145736 | tf_op jit(solution)/shard_map/ppermute | solution.py:83
  395.2 26.8 %collective-permute-start.117 = (bf16[512,1024]{1,0:T(8,128)(2,1)S(1)}, bf16[512,1024]{1,0:T(8,128)(2,1)S(1)}, u32[]{:S(2)}, u32[]{:S(2)}) collective-permute-start(bf16[512,1024]{1,0:T(8,128)(2,1)S(1)} %add_convert_fusion.8), channel_id=1, source_target_pairs={{0,1},{3,2},{4,5},{7,6},{8,9},{11,10},{12,13},{15,14},{16,17},{19,... | collective-permute-start | bytes 3145736 | tf_op jit(solution)/shard_map/ppermute | solution.py:687
  400.7 26.5 %collective-permute-start.140 = (bf16[512,1024]{1,0:T(8,128)(2,1)S(1)}, bf16[512,1024]{1,0:T(8,128)(2,1)S(1)}, u32[]{:S(2)}, u32[]{:S(2)}) collective-permute-start(bf16[512,1024]{1,0:T(8,128)(2,1)S(1)} %add_convert_fusion.6), channel_id=1, source_target_pairs={{1,0},{2,3},{5,4},{6,7},{9,8},{10,11},{13,12},{14,15},{17,16},{18,... | collective-permute-start | bytes 3145736 | tf_op jit(solution)/shard_map/ppermute | solution.py:687
  402.1 87.0 %collective-permute-start.114 = (f32[8,1024]{1,0:T(8,128)S(1)}, f32[8,1024]{1,0:T(8,128)S(1)}, u32[]{:S(2)}, u32[]{:S(2)}) collective-permute-start(f32[8,1024]{1,0:T(8,128)S(1)} %fusion.21), channel_id=1, source_target_pairs={{0,16},{16,0},{1,17},{17,1},{2,18},{18,2},{3,19},{19,3},{4,20},{20... | collective-permute-start | bytes 98312 | tf_op jit(solution)/shard_map/ppermute | solution.py:83
  475.4 28.0 %collective-permute-start.139 = (bf16[512,1024]{1,0:T(8,128)(2,1)S(1)}, bf16[512,1024]{1,0:T(8,128)(2,1)S(1)}, u32[]{:S(2)}, u32[]{:S(2)}) collective-permute-start(bf16[512,1024]{1,0:T(8,128)(2,1)S(1)} %add_convert_fusion), channel_id=1, source_target_pairs={{1,0},{2,3},{5,4},{6,7},{9,8},{10,11},{13,12},{14,15},{17,16},{18,... | collective-permute-start | bytes 3145736 | tf_op jit(solution)/shard_map/ppermute | solution.py:687
  489.1 27.2 %collective-permute-start.135 = (bf16[400,1024]{1,0:T(8,128)(2,1)S(1)}, bf16[400,1024]{1,0:T(8,128)(2,1)S(1)}, u32[]{:S(2)}, u32[]{:S(2)}) collective-permute-start(bf16[400,1024]{1,0:T(8,128)(2,1)S(1)} %add_convert_fusion.13), channel_id=1, source_target_pairs={{1,0},{2,3},{5,4},{6,7},{9,8},{10,11},{13,12},{14,15},{17,16},{18,... | collective-permute-start | bytes 2457608 | tf_op jit(solution)/shard_map/ppermute | solution.py:687
  490.4 27.3 %collective-permute-start.127 = (f32[8,1024]{1,0:T(8,128)S(1)}, f32[8,1024]{1,0:T(8,128)S(1)}, u32[]{:S(2)}, u32[]{:S(2)}) collective-permute-start(f32[8,1024]{1,0:T(8,128)S(1)} %select_add_fusion.1), channel_id=1, source_target_pairs={{0,1},{3,2},{4,5},{7,6},{8,9},{11,10},{12,13},{15,14},{16,17},{19,... | collective-permute-start | bytes 98312 | tf_op jit(solution)/shard_map/ppermute | solution.py:687
  516.3 35.8 %collective-permute-start.136 = (bf16[400,1024]{1,0:T(8,128)(2,1)S(1)}, bf16[400,1024]{1,0:T(8,128)(2,1)S(1)}, u32[]{:S(2)}, u32[]{:S(2)}) collective-permute-start(bf16[400,1024]{1,0:T(8,128)(2,1)S(1)} %add_convert_fusion.12), channel_id=1, source_target_pairs={{1,0},{2,3},{5,4},{6,7},{9,8},{10,11},{13,12},{14,15},{17,16},{18,... | collective-permute-start | bytes 2457608 | tf_op jit(solution)/shard_map/ppermute | solution.py:687
  518.9 33.1 %collective-permute-start.137 = (bf16[288,1024]{1,0:T(8,128)(2,1)S(1)}, bf16[288,1024]{1,0:T(8,128)(2,1)S(1)}, u32[]{:S(2)}, u32[]{:S(2)}) collective-permute-start(bf16[288,1024]{1,0:T(8,128)(2,1)S(1)} %add_convert_fusion.18), channel_id=1, source_target_pairs={{1,0},{2,3},{5,4},{6,7},{9,8},{10,11},{13,12},{14,15},{17,16},{18,... | collective-permute-start | bytes 1769480 | tf_op jit(solution)/shard_map/ppermute | solution.py:687
  522.0 34.4 %collective-permute-start.134 = (f32[8,1024]{1,0:T(8,128)S(1)}, f32[8,1024]{1,0:T(8,128)S(1)}, u32[]{:S(2)}, u32[]{:S(2)}) collective-permute-start(f32[8,1024]{1,0:T(8,128)S(1)} %add.336), channel_id=1, source_target_pairs={{1,0},{2,3},{5,4},{6,7},{9,8},{10,11},{13,12},{14,15},{17,16},{18,... | collective-permute-start | bytes 98312 | tf_op jit(solution)/shard_map/ppermute | solution.py:687
  523.5 34.9 %collective-permute-start.133 = (bf16[272,1024]{1,0:T(8,128)(2,1)S(1)}, bf16[272,1024]{1,0:T(8,128)(2,1)S(1)}, u32[]{:S(2)}, u32[]{:S(2)}) collective-permute-start(bf16[272,1024]{1,0:T(8,128)(2,1)S(1)} %add_convert_fusion.21), channel_id=1, source_target_pairs={{1,0},{2,3},{5,4},{6,7},{9,8},{10,11},{13,12},{14,15},{17,16},{18,... | collective-permute-start | bytes 1671176 | tf_op jit(solution)/shard_map/ppermute | solution.py:687
  (195 other events, 2278.2 us)

commit v6 on v5

--- a/solution.py
+++ b/solution.py
@@ -103,6 +103,10 @@
 def receive_half(half):
     own, from_core, from_chip = half
     return [own, from_core, from_chip, to_core(from_chip)]
+
+
+def in_order(terms, sent):
+    return (*terms[0:2], after(terms[2], sent[-1][0])) if sent else terms
 
 
 def scatter_slots(parts):
@@ -881,10 +885,13 @@
             terms_here, token = scatter_slots(out)
             terms.append(terms_here)
         layer.down = t_dot(active, after(g_all, token)).astype(bf16)
-        layer.up = t_dot(after(n2, layer.down), upper_grad).astype(bf16)
+        layer.up = t_dot(after(n2, token), upper_grad).astype(bf16)
+        if number == 1:
+            layer.up = after(layer.up, layer.down)
         if number == 0:
-            for grad, second in ((layer.down, two.down), (layer.up, two.up)):
-                send_chunks(grad, second, [grad.shape[0] // 2] * 2)
+            quarter = layer.down.shape[0] // 4
+            send_chunks(layer.down, two.down, [quarter, quarter, 2 * quarter])
+            send_chunks(layer.up, two.up, [layer.up.shape[0] // 2] * 2)
         terms[1] = (*terms[1][0:2], after(terms[1][2], layer.up))
         hidden_grads, layer.small2, sent = [], [], []
         for part in range(2):
@@ -898,7 +905,7 @@
             turns(chunks[0])
             slots[7] = after(slots[7], turns.token)
         else:
-            down_out = dot(active, after(layer.wd, low)).astype(bf16)
+            down_out = dot(active, after(layer.wd, sent[1][2])).astype(bf16)
             rows = down_out.shape[0] // 8
             last_parts = [
                 jnp.concatenate([down_out[s * rows : (s + 1) * rows], down_out[(4 + s) * rows : (5 + s) * rows]])
@@ -913,18 +920,22 @@
             last_out = (last_out + jnp.concatenate([here[2] for here in last_terms]).astype(f32)).astype(bf16)
             layer_out = by_layer(jnp.concatenate(layer.rows), last_out)
         terms, token = scatter_halves(ngs)
-        layer.attn = attn_grads(after(dproj, token), layer.normed, layer.mixed, a_all, experts, head_width)
-        token = layer.attn
+        layer.dproj, layer.a_all = dproj, a_all
+        for here in (two, one) if number == 0 else ():
+            here.attn = attn_grads(after(here.dproj, token), here.normed, here.mixed, here.a_all, experts, head_width)
+            token = here.attn
         if number == 0:
             pack = (experts + 2) * head_width + 2 * out_lane
             send_chunks(layer.attn, two.attn, split_tiles(pack) + split_tiles(value_rows))
             turns.token = layer.attn
             turns(chunks[0], chunks[1])
             token = turns.token
-        terms[1] = (*terms[1][0:2], after(terms[1][2], token))
+        if number == 0:
+            terms[1] = (*terms[1][0:2], after(terms[1][2], token))
         rows_grads, low_grads, layer.small1, halves = [], [], [], []
         for part in range(2):
-            dx, low, small_here = norm_back(layer.rows[part], terms[part], part, layer.gain1, hidden_grads[part])
+            here = in_order(terms[part], halves)
+            dx, low, small_here = norm_back(layer.rows[part], here, part, layer.gain1, hidden_grads[part])
             rows_grads.append(dx)
             low_grads.append(low)
             layer.small1.append(small_here)
@@ -948,17 +959,17 @@
     vecs = [
         jnp.concatenate([part[0:5], layer.bias[0] + layer.bias[1], part[6:8]]) for part, layer in zip(cut(vec, 2), layers)
     ]
-    down0, down1, up0, up1, pack0, pack1, out0, out1 = chunks
-    out1.own = (out1.own, jnp.where(first, vecs[0], vecs[1]))
-    out1.moving = (out1.moving, swap_section(jnp.where(first, vecs[1], vecs[0])))
+    down0, down1, down2, up0, up1, pack0, pack1, out0, out1 = chunks
+    pack1.own = (pack1.own, jnp.where(first, vecs[0], vecs[1]))
+    pack1.moving = (pack1.moving, swap_section(jnp.where(first, vecs[1], vecs[0])))
     for chunk in order_turns(chunks):
         turns(chunk)
         if chunk is out1 and chunk.step == 1:
             last_sum = turns.token
-    out_end, vec = out1.end
+    pack_end, vec = pack1.end
     input_grad = by_layer(*[after(layer.input_grad, last_sum) for layer in layers])
     join = lambda *parts: jnp.concatenate(parts).astype(f32)
-    pack_sum = join(pack0.end, pack1.end)
+    pack_sum = join(pack0.end, pack_end)
 
     def take(start, count):
         return pack_sum[start : start + count].T[None, None]
@@ -975,12 +986,12 @@
         take(0, value_rows),
         take(value_rows, experts),
         take(value_rows + out_lane, experts),
-        join(out0.end, out_end)[None, None],
+        join(out0.end, out1.end)[None, None],
         vec[2:3],
         vec[3:4],
         join(up0.end, up1.end)[None],
         vec[5:6],
-        join(down0.end, down1.end)[None],
+        join(down0.end, down1.end, down2.end)[None],
         vec[4:5],
     )
 

time: 568 us -> 558 us (0.982)
  waiting for transfers between devices: 251 us -> 241 us
    ppermute x34, waiting for transfers between devices: 101 us -> 89 us  [to_chip(): return lax.ppermute(a, head_axis, chip_pairs)]
    unnamed x157 -> x171, local copies, waits for them, and re-layouts: 15.5 us -> 11.1 us
    ppermute x19 -> x20, starting transfers between devices: 24 us -> 27.2 us  [swap_section(): return lax.ppermute(a, section_axis, [(0, 1), (1, 0)])]
    ppermute x19 -> x20, waiting for transfers between devices: 78.2 us -> 79.7 us  [swap_section(): return lax.ppermute(a, section_axis, [(0, 1), (1, 0)])]
    ppermute x27 -> x30, waiting for transfers between devices: 57 us -> 56 us  [turn(): lax.ppermute(a, dp_axis, pairs)]
    convert_element_type x36 -> x39, other arithmetic: 11.5 us -> 11.3 us  [plus(): (one.astype(f32) + two.astype(f32)).astype(one.dtype)]
    ppermute x27 -> x30, starting transfers between devices: 53.5 us -> 53.6 us  [turn(): lax.ppermute(a, dp_axis, pairs)]
  transfers between devices with their start and end apart: 142 -> 146, of which waited for: 52 -> 53; matrix products, arithmetic and copies ran while one was open for 11% -> 11% of each run, Pallas kernels for 11% -> 14%
where the time goes in v6:
time: 558 us; the launch traced here: 551 us
  waiting for transfers between devices  241 us (43%)
  starting transfers between devices  138 us (25%)
  Pallas kernels  92.5 us (17%)
  other arithmetic  41.7 us (7%)
  local copies, waits for them, and re-layouts  19.1 us (3%)
  matrix products  14.9 us (3%)
    ppermute x34, waiting for transfers between devices, to_chip(): return lax.ppermute(a, head_axis, chip_pairs)  89 us
    ppermute x20, waiting for transfers between devices, swap_section(): return lax.ppermute(a, section_axis, [(0, 1), (1, 0)])  79.7 us
    ppermute x30, waiting for transfers between devices, turn(): lax.ppermute(a, dp_axis, pairs)  56 us
    ppermute x30, starting transfers between devices, turn(): lax.ppermute(a, dp_axis, pairs)  53.6 us
    ppermute x34, starting transfers between devices, to_chip(): return lax.ppermute(a, head_axis, chip_pairs)  39.8 us
    ppermute x20, starting transfers between devices, swap_section(): return lax.ppermute(a, section_axis, [(0, 1), (1, 0)])  27.2 us
    pallas_call x2, Pallas kernels, attn_bwd(): pl.pallas_call(functools.partial(attn_bwd_kernel, experts, head_width, le...  21.7 us
    pallas_call x2, Pallas kernels, attn_fwd(): pl.pallas_call(functools.partial(attn_fwd_kernel, experts, head_width, le...  20.2 us
  transfers between devices with their start and end apart: 146, of which 53 were waited for; matrix products, arithmetic and copies ran while one was open for 11% of the time, Pallas kernels for 14%

profile of v6, /device:TPU:0, one launch (start us, length us, event | category | flops | bytes accessed | tf_op | source)
XLA Modules:
  0.0 551.5 jit_solution(10397319373630795783)
XLA Ops:
  21.2 8.7 %collective-permute-done.9 = bf16[280,1024]{1,0:T(8,128)(2,1)} collective-permute-done((bf16[280,1024]{1,0:T(8,128)(2,1)}, bf16[280,1024]{1,0:T(8,128)(2,1)}, u32[]{:S(2)}, u32[]{:S(2)}) %collective-permute-start.9) | collective-permute-done | bytes 573472 | tf_op jit(solution)/shard_map/ppermute | solution.py:83
  48.5 9.4 %collective-permute-done.14 = bf16[280,1024]{1,0:T(8,128)(2,1)S(1)} collective-permute-done((bf16[280,1024]{1,0:T(8,128)(2,1)S(1)}, bf16[280,1024]{1,0:T(8,128)(2,1)S(1)}, u32[]{:S(2)}, u32[]{:S(2)}) %collective-permute-start.14) | collective-permute-done | bytes 573472 | tf_op jit(solution)/shard_map/ppermute | solution.py:727
  61.1 8.5 %collective-permute-done.23 = bf16[512,1024]{1,0:T(8,128)(2,1)S(1)} collective-permute-done((bf16[512,1024]{1,0:T(8,128)(2,1)S(1)}, bf16[512,1024]{1,0:T(8,128)(2,1)S(1)}, u32[]{:S(2)}, u32[]{:S(2)}) %collective-permute-start.23) | collective-permute-done | bytes 1048608 | tf_op jit(solution)/shard_map/ppermute | solution.py:83
  71.0 10.2 %attn_fwd.2 = (bf16[256,1024]{1,0:T(8,128)(2,1)S(1)}, bf16[256,1024]{1,0:T(8,128)(2,1)S(1)}, bf16[256,1024]{1,0:T(8,128)(2,1)S(1)}, bf16[256,1024]{1,0:T(8,128)(...) custom-call(s32[1]{0:T(128)} %bitcast.1.me_ref, ...), custom_call_target="tpu_custom_call" | custom-call | flops 3355443200 | bytes 16777216 | tf_op jit(solution)/shard_map/attn_fwd/pallas_call | solution.py:342
  92.6 7.2 %collective-permute-done.30.c_ref = bf16[128,1024]{1,0:T(8,128)(2,1)S(1)} collective-permute-done((bf16[128,1024]{1,0:T(8,128)(2,1)S(1)}, bf16[128,1024]{1,0:T(8,128)(2,1)S(1)}, u32[]{:S(2)}, u32[]{:S(2)}) %collective-permute-start.30) | collective-permute-done | bytes 262176 | tf_op jit(solution)/shard_map/ppermute | solution.py:79
  126.6 6.8 %collective-permute-done.29.c_ref = bf16[128,1024]{1,0:T(8,128)(2,1)S(1)} collective-permute-done((bf16[128,1024]{1,0:T(8,128)(2,1)S(1)}, bf16[128,1024]{1,0:T(8,128)(2,1)S(1)}, u32[]{:S(2)}, u32[]{:S(2)}) %collective-permute-start.29) | collective-permute-done | bytes 262176 | tf_op jit(solution)/shard_map/ppermute | solution.py:79
  144.6 5.0 collective-permute-done.42.refs_9_
  151.4 10.0 %attn_fwd.3 = (bf16[256,1024]{1,0:T(8,128)(2,1)S(1)}, bf16[256,1024]{1,0:T(8,128)(2,1)S(1)}, bf16[256,1024]{1,0:T(8,128)(2,1)S(1)}, bf16[256,1024]{1,0:T(8,128)(...) custom-call(s32[1]{0:T(128)} %bitcast.1.me_ref, ...), custom_call_target="tpu_custom_call" | custom-call | flops 3355443200 | bytes 16777216 | tf_op jit(solution)/shard_map/attn_fwd/pallas_call | solution.py:342
  168.2 6.6 %collective-permute-done.47.c_ref = bf16[128,1024]{1,0:T(8,128)(2,1)S(1)} collective-permute-done((bf16[128,1024]{1,0:T(8,128)(2,1)S(1)}, bf16[128,1024]{1,0:T(8,128)(2,1)S(1)}, u32[]{:S(2)}, u32[]{:S(2)}) %collective-permute-start.47) | collective-permute-done | bytes 262176 | tf_op jit(solution)/shard_map/ppermute | solution.py:79
  190.9 5.2 ffn_bwd.4
  196.2 5.6 %ffn_bwd.5 = (bf16[128,1024]{1,0:T(8,128)(2,1)S(1)}, bf16[128,1024]{1,0:T(8,128)(2,1)S(1)}, bf16[128,1024]{1,0:T(8,128)(2,1)S(1)}, bf16[128,1024]{1,0:T(8,128)(2...) custom-call(bf16[256,1024]{1,0:T(8,128)(2,1)S(1)} %dynamic-slice_bit, ...), custom_call_target="tpu_custom_call", output_to_operand_aliasing={{5}: (11, {}), {6}: (12, {}), {7}: (13, {}), {8}: (14, {})} | custom-call | flops 2147483648 | bytes 9437184 | tf_op jit(solution)/shard_map/ffn_bwd/pallas_call | solution.py:597
  216.4 7.0 %collective-permute-done.60.refs_5_ = bf16[128,1024]{1,0:T(8,128)(2,1)S(1)} collective-permute-done((bf16[128,1024]{1,0:T(8,128)(2,1)S(1)}, bf16[128,1024]{1,0:T(8,128)(2,1)S(1)}, u32[]{:S(2)}, u32[]{:S(2)}) %collective-permute-start.60) | collective-permute-done | bytes 262176 | tf_op jit(solution)/shard_map/ppermute | solution.py:79
  229.9 6.4 %collective-permute-done.71.refs_4_ = bf16[128,1024]{1,0:T(8,128)(2,1)S(1)} collective-permute-done((bf16[128,1024]{1,0:T(8,128)(2,1)S(1)}, bf16[128,1024]{1,0:T(8,128)(2,1)S(1)}, u32[]{:S(2)}, u32[]{:S(2)}) %collective-permute-start.71) | collective-permute-done | bytes 262176 | tf_op jit(solution)/shard_map/ppermute | solution.py:79
  238.6 11.1 %attn_bwd.2 = (bf16[256,1024]{1,0:T(8,128)(2,1)S(1)}, bf16[256,1024]{1,0:T(8,128)(2,1)}, bf16[256,1024]{1,0:T(8,128)(2,1)S(1)}, bf16[256,1024]{1,0:T(8,128)(2,1)...) custom-call(s32[1]{0:T(128)} %bitcast.1.me_ref, ...), custom_call_target="tpu_custom_call" | custom-call | flops 3355443200 | bytes 16777216 | tf_op jit(solution)/shard_map/attn_bwd/pallas_call | solution.py:450
  317.9 10.6 %attn_bwd.3 = (bf16[256,1024]{1,0:T(8,128)(2,1)S(1)}, bf16[256,1024]{1,0:T(8,128)(2,1)S(1)}, bf16[256,1024]{1,0:T(8,128)(2,1)S(1)}, bf16[256,1024]{1,0:T(8,128)(...) custom-call(s32[1]{0:T(128)} %bitcast.1.me_ref, ...), custom_call_target="tpu_custom_call" | custom-call | flops 3355443200 | bytes 16777216 | tf_op jit(solution)/shard_map/attn_bwd/pallas_call | solution.py:450
  336.4 5.7 %attn_grads.2 = bf16[1360,1024]{1,0:T(8,128)(2,1)S(1)} custom-call(bf16[1280,1024]{1,0:T(8,128)(2,1)S(1)} %copy-done.13, bf16[1280,1024]{1,0:T(8,128)(2,1)S(1)} %copy-done.11, bf16[1024,640]{1,0:T(8,128)(2,1)S(1)} %copy-done.23, bf16[1024,1024]{1,0:T(8,128)(2,1)S(1)} %copy-done.15), custom_call_target="tpu_custom_call" | custom-call | tf_op jit(solution)/shard_map/attn_grads/pallas_call | solution.py:649
  342.2 5.5 %attn_grads.3 = bf16[1360,1024]{1,0:T(8,128)(2,1)S(1)} custom-call(bf16[1280,1024]{1,0:T(8,128)(2,1)S(1)} %get-tuple-element.342.refs_0_, bf16[1280,1024]{1,0:T(8,128)(2,1)S(1)} %copy-done.9, bf16[1024,640]{1,0:T(8,128)(2,1)S(1)} %copy-done.21, bf16[1024,1024]{1,0:T(8,128)(2,1)S(1)} %get-tuple-element.345.refs_3_), custom_call_target="tpu_custom_call" | custom-call | tf_op jit(solution)/shard_map/attn_grads/pallas_call | solution.py:649
  372.1 17.3 %collective-permute-done.104 = bf16[512,1024]{1,0:T(8,128)(2,1)S(1)} collective-permute-done((bf16[512,1024]{1,0:T(8,128)(2,1)S(1)}, bf16[512,1024]{1,0:T(8,128)(2,1)S(1)}, u32[]{:S(2)}, u32[]{:S(2)}) %collective-permute-start.104) | collective-permute-done | bytes 1048608 | tf_op jit(solution)/shard_map/ppermute | solution.py:83
  396.3 16.0 %collective-permute-done.105 = bf16[512,1024]{1,0:T(8,128)(2,1)S(1)} collective-permute-done((bf16[512,1024]{1,0:T(8,128)(2,1)S(1)}, bf16[512,1024]{1,0:T(8,128)(2,1)S(1)}, u32[]{:S(2)}, u32[]{:S(2)}) %collective-permute-start.105) | collective-permute-done | bytes 1048608 | tf_op jit(solution)/shard_map/ppermute | solution.py:83
  421.6 10.2 %collective-permute-done.106 = bf16[400,1024]{1,0:T(8,128)(2,1)S(1)} collective-permute-done((bf16[400,1024]{1,0:T(8,128)(2,1)S(1)}, bf16[400,1024]{1,0:T(8,128)(2,1)S(1)}, u32[]{:S(2)}, u32[]{:S(2)}) %collective-permute-start.106) | collective-permute-done | bytes 819232 | tf_op jit(solution)/shard_map/ppermute | solution.py:83
  448.3 9.2 %collective-permute-done.107 = bf16[400,1024]{1,0:T(8,128)(2,1)S(1)} collective-permute-done((bf16[400,1024]{1,0:T(8,128)(2,1)S(1)}, bf16[400,1024]{1,0:T(8,128)(2,1)S(1)}, u32[]{:S(2)}, u32[]{:S(2)}) %collective-permute-start.107) | collective-permute-done | bytes 819232 | tf_op jit(solution)/shard_map/ppermute | solution.py:83
  475.7 5.5 collective-permute-done.126
  502.1 8.4 %collective-permute-done.137 = bf16[400,1024]{1,0:T(8,128)(2,1)S(1)} collective-permute-done((bf16[400,1024]{1,0:T(8,128)(2,1)S(1)}, bf16[400,1024]{1,0:T(8,128)(2,1)S(1)}, u32[]{:S(2)}, u32[]{:S(2)}) %collective-permute-start.137) | collective-permute-done | bytes 819232 | tf_op jit(solution)/shard_map/ppermute | solution.py:691
  517.2 26.4 %collective-permute-done.138 = bf16[288,1024]{1,0:T(8,128)(2,1)S(1)} collective-permute-done((bf16[288,1024]{1,0:T(8,128)(2,1)S(1)}, bf16[288,1024]{1,0:T(8,128)(2,1)S(1)}, u32[]{:S(2)}, u32[]{:S(2)}) %collective-permute-start.138) | collective-permute-done | bytes 589856 | tf_op jit(solution)/shard_map/ppermute | solution.py:691
  (607 shorter events, 325.5 us)
Async XLA Ops:
  6.5 24.8 %collective-permute-start = (bf16[64,1024]{1,0:T(8,128)(2,1)S(1)}, bf16[64,1024]{1,0:T(8,128)(2,1)}, u32[]{:S(2)}, u32[]{:S(2)}) collective-permute-start(bf16[64,1024]{1,0:T(8,128)(2,1)S(1)} %dynamic-slice_bitcast_fusion.2), channel_id=1, source_target_pairs={{0,16},{16,0},{1,17},{17,1},{2,18},{18,2},{3,19},{19,3},{4,20},{20... | collective-permute-start | bytes 393224 | tf_op jit(solution)/shard_map/ppermute | solution.py:83
  16.8 54.1 %collective-permute-start.5 = (bf16[256,1024]{1,0:T(8,128)(2,1)S(1)}, bf16[256,1024]{1,0:T(8,128)(2,1)S(1)}, u32[]{:S(2)}, u32[]{:S(2)}) collective-permute-start(bf16[256,1024]{1,0:T(8,128)(2,1)S(1)} %norm_only.3.refs_4_), channel_id=1, source_target_pairs={{0,4},{4,0},{8,12},{12,8},{1,5},{5,1},{9,13},{13,9},{2,6},{6,2},{1... | collective-permute-start | bytes 1572872 | tf_op jit(solution)/shard_map/ppermute | solution.py:75
  43.5 26.1 %collective-permute-start.23 = (bf16[512,1024]{1,0:T(8,128)(2,1)S(1)}, bf16[512,1024]{1,0:T(8,128)(2,1)S(1)}, u32[]{:S(2)}, u32[]{:S(2)}) collective-permute-start(bf16[512,1024]{1,0:T(8,128)(2,1)S(1)} %constant_dynamic-slice_fusion.1), channel_id=1, source_target_pairs={{0,16},{16,0},{1,17},{17,1},{2,18},{18,2},{3,19},{19,3},{4,20},{20... | collective-permute-start | bytes 3145736 | tf_op jit(solution)/shard_map/ppermute | solution.py:83
  57.9 26.7 %collective-permute-start.16 = (bf16[256,1024]{1,0:T(8,128)(2,1)S(1)}, bf16[256,1024]{1,0:T(8,128)(2,1)S(1)}, u32[]{:S(2)}, u32[]{:S(2)}) collective-permute-start(bf16[256,1024]{1,0:T(8,128)(2,1)S(1)} %dynamic-slice_bitcast_fusion.refs_0_.more_ref), channel_id=1, source_target_pairs={{0,8},{8,0},{4,12},{12,4},{1,9},{9,1},{5,13},{13,5},{2,10},{10,2},... | collective-permute-start | bytes 1572872 | tf_op jit(solution)/shard_map/ppermute | solution.py:79
  59.2 29.9 %collective-permute-start.25 = (bf16[512,1024]{1,0:T(8,128)(2,1)S(1)}, bf16[512,1024]{1,0:T(8,128)(2,1)S(1)}, u32[]{:S(2)}, u32[]{:S(2)}) collective-permute-start(bf16[512,1024]{1,0:T(8,128)(2,1)S(1)} %constant_dynamic-slice_fusion), channel_id=1, source_target_pairs={{0,16},{16,0},{1,17},{17,1},{2,18},{18,2},{3,19},{19,3},{4,20},{20... | collective-permute-start | bytes 3145736 | tf_op jit(solution)/shard_map/ppermute | solution.py:83
  69.6 36.4 %collective-permute-start.24 = (bf16[512,1024]{1,0:T(8,128)(2,1)S(1)}, bf16[512,1024]{1,0:T(8,128)(2,1)S(1)}, u32[]{:S(2)}, u32[]{:S(2)}) collective-permute-start(bf16[512,1024]{1,0:T(8,128)(2,1)S(1)} %collective-permute-done.23), channel_id=1, source_target_pairs={{0,1},{1,0},{2,3},{3,2},{4,5},{5,4},{6,7},{7,6},{8,9},{9,8},{10,11... | collective-permute-start | bytes 3145736 | tf_op jit(solution)/shard_map/ppermute | solution.py:727
  332.0 24.5 %collective-permute-start.97 = (bf16[256,1024]{1,0:T(8,128)(2,1)S(1)}, bf16[256,1024]{1,0:T(8,128)(2,1)S(1)}, u32[]{:S(2)}, u32[]{:S(2)}) collective-permute-start(bf16[256,1024]{1,0:T(8,128)(2,1)S(1)} %get-tuple-element.329), channel_id=1, source_target_pairs={{0,4},{4,0},{8,12},{12,8},{1,5},{5,1},{9,13},{13,9},{2,6},{6,2},{1... | collective-permute-start | bytes 1572872 | tf_op jit(solution)/shard_map/ppermute | solution.py:75
  333.3 31.7 %collective-permute-start.103 = (bf16[512,1024]{1,0:T(8,128)(2,1)}, bf16[512,1024]{1,0:T(8,128)(2,1)S(1)}, u32[]{:S(2)}, u32[]{:S(2)}) collective-permute-start(bf16[512,1024]{1,0:T(8,128)(2,1)} %broadcast_select_fusion.8), channel_id=1, source_target_pairs={{0,16},{16,0},{1,17},{17,1},{2,18},{18,2},{3,19},{19,3},{4,20},{20... | collective-permute-start | bytes 3145736 | tf_op jit(solution)/shard_map/ppermute | solution.py:83
  365.0 24.5 %collective-permute-start.104 = (bf16[512,1024]{1,0:T(8,128)(2,1)S(1)}, bf16[512,1024]{1,0:T(8,128)(2,1)S(1)}, u32[]{:S(2)}, u32[]{:S(2)}) collective-permute-start(bf16[512,1024]{1,0:T(8,128)(2,1)S(1)} %copy-done.75), channel_id=1, source_target_pairs={{0,16},{16,0},{1,17},{17,1},{2,18},{18,2},{3,19},{19,3},{4,20},{20... | collective-permute-start | bytes 3145736 | tf_op jit(solution)/shard_map/ppermute | solution.py:83
  367.7 91.1 %collective-permute-start.122 = (f32[8,1024]{1,0:T(8,128)S(1)}, f32[8,1024]{1,0:T(8,128)S(1)}, u32[]{:S(2)}, u32[]{:S(2)}) collective-permute-start(f32[8,1024]{1,0:T(8,128)S(1)} %fusion.21), channel_id=1, source_target_pairs={{0,16},{16,0},{1,17},{17,1},{2,18},{18,2},{3,19},{19,3},{4,20},{20... | collective-permute-start | bytes 98312 | tf_op jit(solution)/shard_map/ppermute | solution.py:83
  369.5 24.5 %collective-permute-start.115 = (bf16[256,1024]{1,0:T(8,128)(2,1)S(1)}, bf16[256,1024]{1,0:T(8,128)(2,1)S(1)}, u32[]{:S(2)}, u32[]{:S(2)}) collective-permute-start(bf16[256,1024]{1,0:T(8,128)(2,1)S(1)} %add_convert_fusion.23), channel_id=1, source_target_pairs={{1,2},{2,1},{5,6},{6,5},{9,10},{10,9},{13,14},{14,13},{17,18},{18,... | collective-permute-start | bytes 1572872 | tf_op jit(solution)/shard_map/ppermute | solution.py:691
  370.4 24.5 %collective-permute-start.143 = (bf16[256,1024]{1,0:T(8,128)(2,1)S(1)}, bf16[256,1024]{1,0:T(8,128)(2,1)S(1)}, u32[]{:S(2)}, u32[]{:S(2)}) collective-permute-start(bf16[256,1024]{1,0:T(8,128)(2,1)S(1)} %add_convert_fusion.22), channel_id=1, source_target_pairs={{1,0},{2,3},{5,4},{6,7},{9,8},{10,11},{13,12},{14,15},{17,16},{18,... | collective-permute-start | bytes 1572872 | tf_op jit(solution)/shard_map/ppermute | solution.py:691
  390.5 25.7 %collective-permute-start.114 = (bf16[512,1024]{1,0:T(8,128)(2,1)S(1)}, bf16[512,1024]{1,0:T(8,128)(2,1)S(1)}, u32[]{:S(2)}, u32[]{:S(2)}) collective-permute-start(bf16[512,1024]{1,0:T(8,128)(2,1)S(1)} %add_convert_fusion.7), channel_id=1, source_target_pairs={{0,1},{3,2},{4,5},{7,6},{8,9},{11,10},{12,13},{15,14},{16,17},{19,... | collective-permute-start | bytes 3145736 | tf_op jit(solution)/shard_map/ppermute | solution.py:691
  394.0 25.1 %collective-permute-start.113 = (bf16[512,1024]{1,0:T(8,128)(2,1)S(1)}, bf16[512,1024]{1,0:T(8,128)(2,1)S(1)}, u32[]{:S(2)}, u32[]{:S(2)}) collective-permute-start(bf16[512,1024]{1,0:T(8,128)(2,1)S(1)} %add_convert_fusion.6), channel_id=1, source_target_pairs={{1,2},{2,1},{5,6},{6,5},{9,10},{10,9},{13,14},{14,13},{17,18},{18,... | collective-permute-start | bytes 3145736 | tf_op jit(solution)/shard_map/ppermute | solution.py:691
  394.9 25.3 %collective-permute-start.144 = (bf16[256,1024]{1,0:T(8,128)(2,1)S(1)}, bf16[256,1024]{1,0:T(8,128)(2,1)S(1)}, u32[]{:S(2)}, u32[]{:S(2)}) collective-permute-start(bf16[256,1024]{1,0:T(8,128)(2,1)S(1)} %add_convert_fusion.21), channel_id=1, source_target_pairs={{1,0},{2,3},{5,4},{6,7},{9,8},{10,11},{13,12},{14,15},{17,16},{18,... | collective-permute-start | bytes 1572872 | tf_op jit(solution)/shard_map/ppermute | solution.py:691
  412.9 25.8 %collective-permute-start.124 = (bf16[512,1024]{1,0:T(8,128)(2,1)S(1)}, bf16[512,1024]{1,0:T(8,128)(2,1)S(1)}, u32[]{:S(2)}, u32[]{:S(2)}) collective-permute-start(bf16[512,1024]{1,0:T(8,128)(2,1)S(1)} %add_convert_fusion.5), channel_id=1, source_target_pairs={{0,1},{3,2},{4,5},{7,6},{8,9},{11,10},{12,13},{15,14},{16,17},{19,... | collective-permute-start | bytes 3145736 | tf_op jit(solution)/shard_map/ppermute | solution.py:691
  432.3 31.4 %collective-permute-start.116 = (bf16[400,1024]{1,0:T(8,128)(2,1)S(1)}, bf16[400,1024]{1,0:T(8,128)(2,1)S(1)}, u32[]{:S(2)}, u32[]{:S(2)}) collective-permute-start(bf16[400,1024]{1,0:T(8,128)(2,1)S(1)} %add_convert_fusion.14), channel_id=1, source_target_pairs={{0,1},{3,2},{4,5},{7,6},{8,9},{11,10},{12,13},{15,14},{16,17},{19,... | collective-permute-start | bytes 2457608 | tf_op jit(solution)/shard_map/ppermute | solution.py:691
  444.4 24.5 %collective-permute-start.141 = (bf16[512,1024]{1,0:T(8,128)(2,1)S(1)}, bf16[512,1024]{1,0:T(8,128)(2,1)S(1)}, u32[]{:S(2)}, u32[]{:S(2)}) collective-permute-start(bf16[512,1024]{1,0:T(8,128)(2,1)S(1)} %add_convert_fusion.1), channel_id=1, source_target_pairs={{1,0},{2,3},{5,4},{6,7},{9,8},{10,11},{13,12},{14,15},{17,16},{18,... | collective-permute-start | bytes 3145736 | tf_op jit(solution)/shard_map/ppermute | solution.py:691
  468.9 28.0 %collective-permute-start.142 = (bf16[512,1024]{1,0:T(8,128)(2,1)S(1)}, bf16[512,1024]{1,0:T(8,128)(2,1)S(1)}, u32[]{:S(2)}, u32[]{:S(2)}) collective-permute-start(bf16[512,1024]{1,0:T(8,128)(2,1)S(1)} %add_convert_fusion), channel_id=1, source_target_pairs={{1,0},{2,3},{5,4},{6,7},{9,8},{10,11},{13,12},{14,15},{17,16},{18,... | collective-permute-start | bytes 3145736 | tf_op jit(solution)/shard_map/ppermute | solution.py:691
  483.2 27.3 %collective-permute-start.137 = (bf16[400,1024]{1,0:T(8,128)(2,1)S(1)}, bf16[400,1024]{1,0:T(8,128)(2,1)S(1)}, u32[]{:S(2)}, u32[]{:S(2)}) collective-permute-start(bf16[400,1024]{1,0:T(8,128)(2,1)S(1)} %add_convert_fusion.10), channel_id=1, source_target_pairs={{1,0},{2,3},{5,4},{6,7},{9,8},{10,11},{13,12},{14,15},{17,16},{18,... | collective-permute-start | bytes 2457608 | tf_op jit(solution)/shard_map/ppermute | solution.py:691
  500.8 42.9 %collective-permute-start.134 = (f32[8,1024]{1,0:T(8,128)S(1)}, f32[8,1024]{1,0:T(8,128)S(1)}, u32[]{:S(2)}, u32[]{:S(2)}) collective-permute-start(f32[8,1024]{1,0:T(8,128)S(1)} %add.345), channel_id=1, source_target_pairs={{1,0},{2,3},{5,4},{6,7},{9,8},{10,11},{13,12},{14,15},{17,16},{18,... | collective-permute-start | bytes 98312 | tf_op jit(solution)/shard_map/ppermute | solution.py:691
  510.5 33.2 %collective-permute-start.133 = (bf16[400,1024]{1,0:T(8,128)(2,1)S(1)}, bf16[400,1024]{1,0:T(8,128)(2,1)S(1)}, u32[]{:S(2)}, u32[]{:S(2)}) collective-permute-start(bf16[400,1024]{1,0:T(8,128)(2,1)S(1)} %add_convert_fusion.9), channel_id=1, source_target_pairs={{1,0},{2,3},{5,4},{6,7},{9,8},{10,11},{13,12},{14,15},{17,16},{18,... | collective-permute-start | bytes 2457608 | tf_op jit(solution)/shard_map/ppermute | solution.py:691
  513.2 30.4 %collective-permute-start.138 = (bf16[288,1024]{1,0:T(8,128)(2,1)S(1)}, bf16[288,1024]{1,0:T(8,128)(2,1)S(1)}, u32[]{:S(2)}, u32[]{:S(2)}) collective-permute-start(bf16[288,1024]{1,0:T(8,128)(2,1)S(1)} %add_convert_fusion.15), channel_id=1, source_target_pairs={{1,0},{2,3},{5,4},{6,7},{9,8},{10,11},{13,12},{14,15},{17,16},{18,... | collective-permute-start | bytes 1769480 | tf_op jit(solution)/shard_map/ppermute | solution.py:691
  515.9 33.6 %collective-permute-start.140 = (bf16[272,1024]{1,0:T(8,128)(2,1)S(1)}, bf16[272,1024]{1,0:T(8,128)(2,1)S(1)}, u32[]{:S(2)}, u32[]{:S(2)}) collective-permute-start(bf16[272,1024]{1,0:T(8,128)(2,1)S(1)} %add_convert_fusion.18), channel_id=1, source_target_pairs={{1,0},{2,3},{5,4},{6,7},{9,8},{10,11},{13,12},{14,15},{17,16},{18,... | collective-permute-start | bytes 1671176 | tf_op jit(solution)/shard_map/ppermute | solution.py:691
  (206 other events, 2320.0 us)
